TPU v7x, 32 devices: a whole 2x2x4 slice. The times are simulated.
32 devices in a mesh: sy: 8 (over y, x, core), sx: 4 (over z).
Axes of the slice: x: 2, y: 2, z: 4, core: 2. Of those that a mesh axis runs over, the one named last changes fastest.
Arguments:
- object_tile: float32 [2, 1024, 512], P(None, 'sy', 'sx'), may hold values from -5 to 5
- probe_modes: float32 [2, 2, 128, 128], replicated, may hold values from -4 to 4
- scan_offsets: int32 [8, 4, 4, 2], P('sy', 'sx'), may hold values from 0 to 128
- intensities: float32 [8, 4, 4, 128, 128], P('sy', 'sx'), may hold values from 0 to 2
Outputs:
- object_out: float32 [2, 1024, 512], P(None, 'sy', 'sx')
- probe_out: float32 [2, 2, 128, 128], replicated
Inputs may be any that keep to these rules, and one draw needn't show every extreme that they name: `scan_offsets`: offsets are counted from 64 pixels above and to the left of the device's tile, so a patch stays within 64 pixels of its tile.
All inputs are finite; a program needn't handle non-finite values.
Results may differ from a plain program's by a relative error of at most 0.0003.
Values sent between devices are 32-bit elements; how exact they have to be, the bound alone decides.
No kernel may reach another device: no remote copies, remote signals or barrier semaphores. Data moves between devices by JAX's collectives and lax.ppermute only.
A program may use at most 64 MiB of HBM per device.

v0:
```python
import functools

import jax
import jax.numpy as jnp
import numpy as np
from jax import lax
from jax.experimental import pallas as pl
from jax.experimental.pallas import tpu as pltpu
from jax.sharding import PartitionSpec as P

ITERS = 2
OBJECT_STEP = 0.5
PROBE_STEP = 2.0
REGULAR = 1.0


def dft_tables(extent):
    line = np.arange(extent)
    angle = (line[:, None] * line[None, :] % extent) * (2.0 * np.pi / extent)
    cosine, sine = np.cos(angle) / np.sqrt(extent), np.sin(angle) / np.sqrt(extent)
    table = np.block([[cosine, -sine], [sine, cosine]])
    high = table.astype(jnp.bfloat16)
    low = (table - high.astype(np.float64)).astype(jnp.bfloat16)
    return np.stack([high, low, high.T, low.T])


def split(values):
    high = values.astype(jnp.bfloat16)
    return high, (values - high.astype(jnp.float32)).astype(jnp.bfloat16)


def product(left, right):
    dot = functools.partial(jnp.dot, preferred_element_type=jnp.float32)
    return dot(left[0], right[0]) + (dot(left[0], right[1]) + dot(left[1], right[0]))


def swapped(values, axis, odd):
    count = lax.axis_size(axis)
    pairs = []
    for first in range(1 if odd else 0, count - 1, 2):
        pairs += [(first, first + 1), (first + 1, first)]
    return lax.ppermute(values, axis, pairs)


def flipped(values, axis, bits):
    return lax.ppermute(values, axis, [(i, i ^ bits) for i in range(lax.axis_size(axis))])


def tree_sum(parts):
    while len(parts) > 1:
        parts = [parts[i] + parts[i + 1] for i in range(0, len(parts), 2)]
    return parts[0]


def scalars_of(offsets, canvas_size, halo):
    row, col = lax.axis_index("sy"), lax.axis_index("sx")
    rows, cols = lax.axis_size("sy"), lax.axis_size("sx")
    head = [
        row % 2,
        col % 2,
        row // 2,
        jnp.where(row == 0, halo, 0),
        jnp.where(row == rows - 1, canvas_size - halo, canvas_size),
        jnp.where(col == 0, halo, 0),
        jnp.where(col == cols - 1, canvas_size - halo, canvas_size),
    ]
    return jnp.concatenate([jnp.stack(head).astype(jnp.int32), offsets.reshape(-1)])


HEAD = 7


def updated_canvas(scal, canvas_ref, sums, store):
    half = canvas_ref.shape[-1]
    for a in range(2):
        row = pl.multiple_of(jnp.where(scal[0] == a, half, 0), half)
        for b in range(2):
            side = jnp.where(scal[1] == b, 1, 0)
            at_row = lax.broadcasted_iota(jnp.int32, (half, half), 0) + row
            at_col = lax.broadcasted_iota(jnp.int32, (half, half), 1) + side * half
            inside = (at_row >= scal[3]) & (at_row < scal[4]) & (at_col >= scal[5]) & (at_col < scal[6])
            scale = jnp.where(inside, OBJECT_STEP / (sums[b][a, 2] + REGULAR), 0.0)
            for part in range(2):
                here = (part, side, pl.ds(row, half))
                store(here, canvas_ref[here] - scale * sums[b][a, part])


def place_probe(scal, own_ref, other_ref, probe_ref):
    chips, planes, rows, _ = own_ref.shape
    for slot in range(chips):
        chunk = scal[2] ^ slot
        for which, ref in ((scal[0], own_ref), (1 - scal[0], other_ref)):
            start = pl.multiple_of((which * chips + chunk) * rows, rows)
            for plane in range(planes):
                probe_ref[plane // 2, plane % 2, pl.ds(start, rows), :] = ref[slot, plane]


def terms_body(scal, canvas_ref, probe_ref, measured_ref, table_ref, grad_out, keep_out, send_out, grad, sums):
    positions, extent, _ = measured_ref.shape
    modes = probe_ref.shape[0]
    w1 = (table_ref[0], table_ref[1])
    w2 = (table_ref[2], table_ref[3])
    grad[...] = jnp.zeros_like(grad)
    lighting = None
    for k in range(modes):
        for part in range(2):
            term = probe_ref[k, part] * probe_ref[k, part]
            lighting = term if lighting is None else lighting + term
    lane = lax.broadcasted_iota(jnp.int32, (extent, extent), 1)
    for j in range(positions):
        row, col = scal[HEAD + 2 * j], scal[HEAD + 2 * j + 1]
        turn = col & (extent - 1)
        back = (extent - col) & (extent - 1)
        o_r, o_i = [
            jnp.where(
                lane < extent - col,
                pltpu.roll(canvas_ref[part, 0, pl.ds(row, extent), :], back, 1),
                pltpu.roll(canvas_ref[part, 1, pl.ds(row, extent), :], back, 1),
            )
            for part in range(2)
        ]
        waves = []
        for k in range(modes):
            p_r, p_i = probe_ref[k, 0], probe_ref[k, 1]
            waves.append(jnp.concatenate([p_r * o_r - p_i * o_i, p_r * o_i + p_i * o_r], axis=1))
        half = product(split(jnp.concatenate(waves, axis=0)), w1)
        rows = [half[k * extent : (k + 1) * extent] for k in range(modes)]
        half = jnp.concatenate(
            [jnp.concatenate([r[:, part * extent : (part + 1) * extent] for r in rows], axis=1) for part in range(2)],
            axis=0,
        )
        spectrum = product(w2, split(half))
        squares = spectrum * spectrum
        power = squares[:extent] + squares[extent:]
        misfit = sum(power[:, k * extent : (k + 1) * extent] for k in range(modes)) - measured_ref[j]
        wide = jnp.concatenate([misfit] * modes, axis=1)
        weighted = spectrum * jnp.concatenate([wide, wide], axis=0)
        half = product(w1, split(weighted))
        half = jnp.concatenate(
            [
                jnp.concatenate([half[:extent, k * extent : (k + 1) * extent], half[extent:, k * extent : (k + 1) * extent]], axis=1)
                for k in range(modes)
            ],
            axis=0,
        )
        chi = product(split(half), w2)
        g_r = g_i = 0.0
        for k in range(modes):
            p_r, p_i = probe_ref[k, 0], probe_ref[k, 1]
            c_r = chi[k * extent : (k + 1) * extent, :extent]
            c_i = chi[k * extent : (k + 1) * extent, extent:]
            g_r = g_r + (p_r * c_r + p_i * c_i)
            g_i = g_i + (p_r * c_i - p_i * c_r)
            for part, term in ((0, o_r * c_r + o_i * c_i), (1, o_r * c_i - o_i * c_r)):
                plane = 2 * k + part
                sums[plane] = term if j == 0 else sums[plane] + term
        term = o_r * o_r + o_i * o_i
        sums[2 * modes] = term if j == 0 else sums[2 * modes] + term
        for plane, term in enumerate((g_r, g_i, lighting)):
            moved = pltpu.roll(term, turn, 1)
            grad[plane, 0, pl.ds(row, extent), :] += jnp.where(lane >= col, moved, 0.0)
            grad[plane, 1, pl.ds(row, extent), :] += jnp.where(lane < col, moved, 0.0)
    for a in range(2):
        row = pl.multiple_of(jnp.where(scal[0] == a, extent, 0), extent)
        for b in range(2):
            side = jnp.where(scal[1] == b, 1, 0)
            for plane in range(3):
                grad_out[a, b, plane] = grad[plane, side, pl.ds(row, extent), :]
    chips, planes, rows, _ = keep_out.shape
    for slot in range(chips):
        chunk = scal[2] ^ slot
        for which, ref in ((scal[0], keep_out), (1 - scal[0], send_out)):
            start = pl.multiple_of((which * chips + chunk) * rows, rows)
            for plane in range(planes):
                ref[slot, plane] = sums[plane, pl.ds(start, rows), :]


def first_kernel(scal, canvas_ref, probe_ref, measured_ref, table_ref, grad_out, keep_out, send_out, grad, sums):
    terms_body(scal, canvas_ref, probe_ref, measured_ref, table_ref, grad_out, keep_out, send_out, grad, sums)


def next_kernel(
    scal, old_ref, sums_a, sums_b, own_ref, other_ref, measured_ref, table_ref,
    grad_out, keep_out, send_out, canvas_ref, grad, sums, probe_ref,
):
    def store(here, values):
        canvas_ref[here] = values

    updated_canvas(scal, old_ref, (sums_a, sums_b), store)
    place_probe(scal, own_ref, other_ref, probe_ref)
    terms_body(scal, canvas_ref, probe_ref, measured_ref, table_ref, grad_out, keep_out, send_out, grad, sums)


def last_kernel(scal, old_ref, sums_a, sums_b, own_ref, other_ref, object_ref, probe_ref, canvas):
    half = old_ref.shape[-1]
    halo = half // 2

    def store(here, values):
        canvas[here] = values

    updated_canvas(scal, old_ref, (sums_a, sums_b), store)
    place_probe(scal, own_ref, other_ref, probe_ref)
    for part in range(2):
        middle = pl.ds(halo, half)
        lane = lax.broadcasted_iota(jnp.int32, (half, half), 1)
        object_ref[part] = jnp.where(
            lane < halo, pltpu.roll(canvas[part, 0, middle, :], halo, 1), pltpu.roll(canvas[part, 1, middle, :], halo, 1)
        )


SMEM = pl.BlockSpec(memory_space=pltpu.SMEM)
VMEM = pl.BlockSpec(memory_space=pltpu.VMEM)
PARAMS = pltpu.CompilerParams(vmem_limit_bytes=32 * 1024 * 1024)


def f32(*shape):
    return jax.ShapeDtypeStruct(shape, jnp.float32)


def fetch(tile, halo):
    def rims(values, axis, dim):
        odd = lax.axis_index(axis) % 2 == 1
        low = lax.slice_in_dim(values, 0, halo, axis=dim)
        high = lax.slice_in_dim(values, values.shape[dim] - halo, None, axis=dim)
        near = swapped(jnp.where(odd, low, high), axis, False)
        far = swapped(jnp.where(odd, high, low), axis, True)
        return jnp.where(odd, near, far), jnp.where(odd, far, near)

    above, below = rims(tile, "sy", 1)
    column = jnp.concatenate([above, tile, below], axis=1)
    left, right = rims(column, "sx", 2)
    return jnp.stack(
        [jnp.concatenate([left, column[..., :-halo]], axis=2), jnp.concatenate([column[..., halo:], right], axis=2)],
        axis=1,
    )


def neighbour_sums(grad):
    near = grad[0] + swapped(grad[0], "sy", False)
    far = grad[1] + swapped(grad[1], "sy", True)
    side_a = jnp.stack([near[0], far[0]])
    side_b = jnp.stack([near[1], far[1]])
    return side_a + swapped(side_a, "sx", False), side_b + swapped(side_b, "sx", True)


def probe_step(probe_chunk, keep, send):
    chips = keep.shape[0]
    planes = probe_chunk.shape[0]
    both = keep + swapped(send, "sy", False)
    total = tree_sum([both[0]] + [flipped(both[t], "sy", 2 * t) for t in range(1, chips)])
    total = tree_sum([total] + [flipped(total, "sx", t) for t in range(1, lax.axis_size("sx"))])
    fresh = probe_chunk - PROBE_STEP * total[:planes] / (total[planes:] + REGULAR)
    own = jnp.stack([fresh] + [flipped(fresh, "sy", 2 * t) for t in range(1, chips)])
    return fresh, own, swapped(own, "sy", False)


def per_device(object_tile, probe_modes, scan_offsets, intensities):
    tile = object_tile.shape[1]
    modes, _, extent, _ = probe_modes.shape
    halo = extent // 2
    size = tile + 2 * halo
    chips = lax.axis_size("sy") // 2
    rows = extent // 2 // chips
    planes = 2 * modes
    measured = intensities[0, 0]
    table = jnp.asarray(dft_tables(extent))
    scal = scalars_of(scan_offsets[0, 0], size, halo)
    outs = (f32(2, 2, 3, tile, tile), f32(chips, planes + 1, rows, extent), f32(chips, planes + 1, rows, extent))
    scratch = [pltpu.VMEM((3, 2, size, tile), jnp.float32), pltpu.VMEM((planes + 1, extent, extent), jnp.float32)]
    canvas = fetch(object_tile, halo)
    start = (lax.axis_index("sy") % 2 * chips + lax.axis_index("sy") // 2) * rows
    chunk = lax.dynamic_slice_in_dim(probe_modes.reshape(planes, extent, extent), start, rows, axis=1)
    grad, keep, send = pl.pallas_call(
        first_kernel,
        out_shape=outs,
        in_specs=[SMEM] + [VMEM] * 4,
        out_specs=[VMEM] * 3,
        scratch_shapes=scratch,
        compiler_params=PARAMS,
    )(scal, canvas, probe_modes, measured, table)
    for iteration in range(1, ITERS):
        sums_a, sums_b = neighbour_sums(grad)
        chunk, own, other = probe_step(chunk, keep, send)
        grad, keep, send, canvas = pl.pallas_call(
            next_kernel,
            out_shape=outs + (f32(2, 2, size, tile),),
            in_specs=[SMEM] + [VMEM] * 7,
            out_specs=[VMEM] * 4,
            scratch_shapes=scratch + [pltpu.VMEM(probe_modes.shape, jnp.float32)],
            compiler_params=PARAMS,
        )(scal, canvas, sums_a, sums_b, own, other, measured, table)
    sums_a, sums_b = neighbour_sums(grad)
    chunk, own, other = probe_step(chunk, keep, send)
    return pl.pallas_call(
        last_kernel,
        out_shape=(f32(2, tile, tile), f32(*probe_modes.shape)),
        in_specs=[SMEM] + [VMEM] * 5,
        out_specs=[VMEM] * 2,
        scratch_shapes=[pltpu.VMEM((2, 2, size, tile), jnp.float32)],
        compiler_params=PARAMS,
    )(scal, canvas, sums_a, sums_b, own, other)


def solution(mesh):
    placed = (P(None, "sy", "sx"), P(), P("sy", "sx", None, None), P("sy", "sx", None, None, None))
    return jax.shard_map(
        per_device,
        mesh=mesh,
        in_specs=placed,
        out_specs=(P(None, "sy", "sx"), P()),
        check_vma=False,
    )
```

profile of v0, /device:TPU:0, one launch (start us, length us, event | category | flops | bytes accessed | tf_op | source)
XLA Modules:
  0.0 105.4 jit_solution(954389988141884042)
XLA Ops:
  3.8 2.7 %collective-permute-start.2 = (f32[2,256,64]{2,1,0:T(8,128)S(1)}, f32[2,256,64]{2,1,0:T(8,128)S(1)}, u32[]{:S(2)}, u32[]{:S(2)}) collective-permute-start(f32[2,256,64]{2,1,0:T(8,128)S(1)} %get-tuple-element.35), channel_id=1, source_target_pairs={{0,1},{1,0},{2,3},{3,2},{4,5},{5,4},{6,7},{7,6},{8,9},{9,8},{10,11... | collective-permute-start | bytes 393224 | tf_op jit(solution)/shard_map/ppermute | solution.py:42
  8.1 2.7 %collective-permute-done.2 = f32[2,256,64]{2,1,0:T(8,128)S(1)} collective-permute-done((f32[2,256,64]{2,1,0:T(8,128)S(1)}, f32[2,256,64]{2,1,0:T(8,128)S(1)}, u32[]{:S(2)}, u32[]{:S(2)}) %collective-permute-start.2) | collective-permute-done | bytes 131104 | tf_op jit(solution)/shard_map/ppermute | solution.py:42
  12.3 4.8 %shard_map.68 = (f32[2,2,3,128,128]{4,3,2,1,0:T(8,128)S(1)}, f32[4,5,16,128]{3,2,1,0:T(8,128)S(1)}, f32[4,5,16,128]{3,2,1,0:T(8,128)S(1)}) custom-call(s32[15]{0:T(128)S(1)} %concatenate.12.scal, f32[2,2,256,128]{3,2,1,0:T(8,128)S(1)} %pad_maximum_fusion.canvas_ref.old_ref, f32[2,2,128,128]{3,2,1,0:T(8,128)S(1)} %copy-done.2, f32[4,128,128]{2,1,0:T(8,128)S(1)} %bitcast.67, ...), custom_call_target="tpu_custom_call" | custom-call | tf_op jit(solution)/shard_map/pallas_call | solution.py:273
  17.1 4.4 %collective-permute-start.8 = (f32[4,5,16,128]{3,2,1,0:T(8,128)S(1)}, f32[4,5,16,128]{3,2,1,0:T(8,128)S(1)}, u32[]{:S(2)}, u32[]{:S(2)}) collective-permute-start(f32[4,5,16,128]{3,2,1,0:T(8,128)S(1)} %get-tuple-element.11), channel_id=1, source_target_pairs={{0,4},{4,0},{8,12},{12,8},{16,20},{20,16},{24,28},{28,24},{1,5},{5... | collective-permute-start | bytes 491528 | tf_op jit(solution)/shard_map/ppermute | solution.py:42
  22.6 3.2 %collective-permute-start.11 = (f32[5,16,128]{2,1,0:T(8,128)S(1)}, f32[5,16,128]{2,1,0:T(8,128)S(1)}, u32[]{:S(2)}, u32[]{:S(2)}) collective-permute-start(f32[5,16,128]{2,1,0:T(8,128)S(1)} %get-tuple-element.41), channel_id=1, source_target_pairs={{0,24},{4,28},{8,16},{12,20},{16,8},{20,12},{24,0},{28,4},{1,25},{... | collective-permute-start | bytes 122888 | tf_op jit(solution)/shard_map/ppermute | solution.py:46
  25.7 2.7 %collective-permute-start.10 = (f32[5,16,128]{2,1,0:T(8,128)S(1)}, f32[5,16,128]{2,1,0:T(8,128)S(1)}, u32[]{:S(2)}, u32[]{:S(2)}) collective-permute-start(f32[5,16,128]{2,1,0:T(8,128)S(1)} %get-tuple-element.42), channel_id=1, source_target_pairs={{0,16},{4,20},{8,24},{12,28},{16,0},{20,4},{24,8},{28,12},{1,17},{... | collective-permute-start | bytes 122888 | tf_op jit(solution)/shard_map/ppermute | solution.py:46
  28.7 1.7 %collective-permute-done.10 = f32[5,16,128]{2,1,0:T(8,128)S(1)} collective-permute-done((f32[5,16,128]{2,1,0:T(8,128)S(1)}, f32[5,16,128]{2,1,0:T(8,128)S(1)}, u32[]{:S(2)}, u32[]{:S(2)}) %collective-permute-start.10) | collective-permute-done | bytes 40992 | tf_op jit(solution)/shard_map/ppermute | solution.py:46
  30.4 2.0 %collective-permute-done.9 = f32[5,16,128]{2,1,0:T(8,128)S(1)} collective-permute-done((f32[5,16,128]{2,1,0:T(8,128)S(1)}, f32[5,16,128]{2,1,0:T(8,128)S(1)}, u32[]{:S(2)}, u32[]{:S(2)}) %collective-permute-start.9) | collective-permute-done | bytes 40992 | tf_op jit(solution)/shard_map/ppermute | solution.py:46
  32.5 3.7 %collective-permute-start.14 = (f32[5,16,128]{2,1,0:T(8,128)S(1)}, f32[5,16,128]{2,1,0:T(8,128)S(1)}, u32[]{:S(2)}, u32[]{:S(2)}) collective-permute-start(f32[5,16,128]{2,1,0:T(8,128)S(1)} %fusion.3), channel_id=1, source_target_pairs={{0,3},{1,2},{2,1},{3,0},{4,7},{5,6},{6,5},{7,4},{8,11},{9,10},{10,... | collective-permute-start | bytes 122888 | tf_op jit(solution)/shard_map/ppermute | solution.py:46
  36.1 2.7 %collective-permute-start.13 = (f32[5,16,128]{2,1,0:T(8,128)S(1)}, f32[5,16,128]{2,1,0:T(8,128)S(1)}, u32[]{:S(2)}, u32[]{:S(2)}) collective-permute-start(f32[5,16,128]{2,1,0:T(8,128)S(1)} %fusion.3), channel_id=1, source_target_pairs={{0,2},{1,3},{2,0},{3,1},{4,6},{5,7},{6,4},{7,5},{8,10},{9,11},{10,... | collective-permute-start | bytes 122888 | tf_op jit(solution)/shard_map/ppermute | solution.py:46
  45.3 11.5 %collective-permute-start.17 = (f32[4,16,128]{2,1,0:T(8,128)S(1)}, f32[4,16,128]{2,1,0:T(8,128)S(1)}, u32[]{:S(2)}, u32[]{:S(2)}) collective-permute-start(f32[4,16,128]{2,1,0:T(8,128)S(1)} %fusion.7), channel_id=1, source_target_pairs={{0,24},{4,28},{8,16},{12,20},{16,8},{20,12},{24,0},{28,4},{1,25},{... | collective-permute-start | bytes 98312 | tf_op jit(solution)/shard_map/ppermute | solution.py:46
  57.4 1.5 %collective-permute-done.17 = f32[4,16,128]{2,1,0:T(8,128)S(1)} collective-permute-done((f32[4,16,128]{2,1,0:T(8,128)S(1)}, f32[4,16,128]{2,1,0:T(8,128)S(1)}, u32[]{:S(2)}, u32[]{:S(2)}) %collective-permute-start.17) | collective-permute-done | bytes 32800 | tf_op jit(solution)/shard_map/ppermute | solution.py:46
  58.9 1.8 %collective-permute-done.16 = f32[4,16,128]{2,1,0:T(8,128)S(1)} collective-permute-done((f32[4,16,128]{2,1,0:T(8,128)S(1)}, f32[4,16,128]{2,1,0:T(8,128)S(1)}, u32[]{:S(2)}, u32[]{:S(2)}) %collective-permute-start.16) | collective-permute-done | bytes 32800 | tf_op jit(solution)/shard_map/ppermute | solution.py:46
  62.1 5.0 %shard_map.69 = (f32[2,2,3,128,128]{4,3,2,1,0:T(8,128)S(1)}, f32[4,5,16,128]{3,2,1,0:T(8,128)S(1)}, f32[4,5,16,128]{3,2,1,0:T(8,128)S(1)}, f32[2,2,256,128]{3,2,1,0:T(8,128)S(1)}) custom-call(s32[15]{0:T(128)S(1)} %concatenate.12.scal, f32[2,2,256,128]{3,2,1,0:T(8,128)S(1)} %pad_maximum_fusion.canvas_ref.old_ref, f32[2,3,128,128]{3,2,1,0:T(8,128)S(1)} %fusion.17.sums_a, ...), custom_call_target="tpu_custom_call" | custom-call | tf_op jit(solution)/shard_map/pallas_call | solution.py:284
  68.6 1.5 %collective-permute-start.26 = (f32[5,16,128]{2,1,0:T(8,128)S(1)}, f32[5,16,128]{2,1,0:T(8,128)S(1)}, u32[]{:S(2)}, u32[]{:S(2)}) collective-permute-start(f32[5,16,128]{2,1,0:T(8,128)S(1)} %get-tuple-element.38), channel_id=1, source_target_pairs={{0,24},{4,28},{8,16},{12,20},{16,8},{20,12},{24,0},{28,4},{1,25},{... | collective-permute-start | bytes 122888 | tf_op jit(solution)/shard_map/ppermute | solution.py:46
  70.1 1.5 %collective-permute-start.25 = (f32[5,16,128]{2,1,0:T(8,128)S(1)}, f32[5,16,128]{2,1,0:T(8,128)S(1)}, u32[]{:S(2)}, u32[]{:S(2)}) collective-permute-start(f32[5,16,128]{2,1,0:T(8,128)S(1)} %get-tuple-element.39), channel_id=1, source_target_pairs={{0,16},{4,20},{8,24},{12,28},{16,0},{20,4},{24,8},{28,12},{1,17},{... | collective-permute-start | bytes 122888 | tf_op jit(solution)/shard_map/ppermute | solution.py:46
  72.1 1.5 %collective-permute-done.26 = f32[5,16,128]{2,1,0:T(8,128)S(1)} collective-permute-done((f32[5,16,128]{2,1,0:T(8,128)S(1)}, f32[5,16,128]{2,1,0:T(8,128)S(1)}, u32[]{:S(2)}, u32[]{:S(2)}) %collective-permute-start.26) | collective-permute-done | bytes 40992 | tf_op jit(solution)/shard_map/ppermute | solution.py:46
  74.1 1.5 %collective-permute-done.24 = f32[5,16,128]{2,1,0:T(8,128)S(1)} collective-permute-done((f32[5,16,128]{2,1,0:T(8,128)S(1)}, f32[5,16,128]{2,1,0:T(8,128)S(1)}, u32[]{:S(2)}, u32[]{:S(2)}) %collective-permute-start.24) | collective-permute-done | bytes 40992 | tf_op jit(solution)/shard_map/ppermute | solution.py:46
  75.7 2.4 %collective-permute-start.29 = (f32[5,16,128]{2,1,0:T(8,128)S(1)}, f32[5,16,128]{2,1,0:T(8,128)S(1)}, u32[]{:S(2)}, u32[]{:S(2)}) collective-permute-start(f32[5,16,128]{2,1,0:T(8,128)S(1)} %fusion.1), channel_id=1, source_target_pairs={{0,3},{1,2},{2,1},{3,0},{4,7},{5,6},{6,5},{7,4},{8,11},{9,10},{10,... | collective-permute-start | bytes 122888 | tf_op jit(solution)/shard_map/ppermute | solution.py:46
  78.1 3.0 %collective-permute-start.28 = (f32[5,16,128]{2,1,0:T(8,128)S(1)}, f32[5,16,128]{2,1,0:T(8,128)S(1)}, u32[]{:S(2)}, u32[]{:S(2)}) collective-permute-start(f32[5,16,128]{2,1,0:T(8,128)S(1)} %fusion.1), channel_id=1, source_target_pairs={{0,2},{1,3},{2,0},{3,1},{4,6},{5,7},{6,4},{7,5},{8,10},{9,11},{10,... | collective-permute-start | bytes 122888 | tf_op jit(solution)/shard_map/ppermute | solution.py:46
  81.9 1.8 %collective-permute-done.28 = f32[5,16,128]{2,1,0:T(8,128)S(1)} collective-permute-done((f32[5,16,128]{2,1,0:T(8,128)S(1)}, f32[5,16,128]{2,1,0:T(8,128)S(1)}, u32[]{:S(2)}, u32[]{:S(2)}) %collective-permute-start.28) | collective-permute-done | bytes 40992 | tf_op jit(solution)/shard_map/ppermute | solution.py:46
  87.0 11.3 %collective-permute-start.32 = (f32[4,16,128]{2,1,0:T(8,128)S(1)}, f32[4,16,128]{2,1,0:T(8,128)S(1)}, u32[]{:S(2)}, u32[]{:S(2)}) collective-permute-start(f32[4,16,128]{2,1,0:T(8,128)S(1)} %fusion.5), channel_id=1, source_target_pairs={{0,24},{4,28},{8,16},{12,20},{16,8},{20,12},{24,0},{28,4},{1,25},{... | collective-permute-start | bytes 98312 | tf_op jit(solution)/shard_map/ppermute | solution.py:46
  100.3 2.0 %collective-permute-done.31 = f32[4,16,128]{2,1,0:T(8,128)S(1)} collective-permute-done((f32[4,16,128]{2,1,0:T(8,128)S(1)}, f32[4,16,128]{2,1,0:T(8,128)S(1)}, u32[]{:S(2)}, u32[]{:S(2)}) %collective-permute-start.31) | collective-permute-done | bytes 32800 | tf_op jit(solution)/shard_map/ppermute | solution.py:46
  103.9 1.5 %shard_map.70 = (f32[2,128,128]{2,1,0:T(8,128)}, f32[2,2,128,128]{3,2,1,0:T(8,128)}) custom-call(s32[15]{0:T(128)S(1)} %concatenate.12.scal, f32[2,2,256,128]{3,2,1,0:T(8,128)S(1)} %get-tuple-element.12.old_ref, f32[2,3,128,128]{3,2,1,0:T(8,128)S(1)} %fusion.15.sums_a, f32[2,3,128,128]{3,2,1,0:T(8,128)S(1)} %fusion.14.sums_b, ...), custom_call_target="tpu_custom_call" | custom-call | tf_op jit(solution)/shard_map/pallas_call | solution.py:294
  (97 shorter events, 26.0 us)
Async XLA Ops:
  3.8 7.0 %collective-permute-start.2 = (f32[2,256,64]{2,1,0:T(8,128)S(1)}, f32[2,256,64]{2,1,0:T(8,128)S(1)}, u32[]{:S(2)}, u32[]{:S(2)}) collective-permute-start(f32[2,256,64]{2,1,0:T(8,128)S(1)} %get-tuple-element.35), channel_id=1, source_target_pairs={{0,1},{1,0},{2,3},{3,2},{4,5},{5,4},{6,7},{7,6},{8,9},{9,8},{10,11... | collective-permute-start | bytes 393224 | tf_op jit(solution)/shard_map/ppermute | solution.py:42
  6.5 4.4 %collective-permute-start.3 = (f32[2,256,64]{2,1,0:T(8,128)S(1)}, f32[2,256,64]{2,1,0:T(8,128)S(1)}, u32[]{:S(2)}, u32[]{:S(2)}) collective-permute-start(f32[2,256,64]{2,1,0:T(8,128)S(1)} %get-tuple-element.36), channel_id=1, source_target_pairs={{1,2},{2,1},{5,6},{6,5},{9,10},{10,9},{13,14},{14,13},{17,18},{18,... | collective-permute-start | bytes 393224 | tf_op jit(solution)/shard_map/ppermute | solution.py:42
  17.1 5.4 %collective-permute-start.8 = (f32[4,5,16,128]{3,2,1,0:T(8,128)S(1)}, f32[4,5,16,128]{3,2,1,0:T(8,128)S(1)}, u32[]{:S(2)}, u32[]{:S(2)}) collective-permute-start(f32[4,5,16,128]{3,2,1,0:T(8,128)S(1)} %get-tuple-element.11), channel_id=1, source_target_pairs={{0,4},{4,0},{8,12},{12,8},{16,20},{20,16},{24,28},{28,24},{1,5},{5... | collective-permute-start | bytes 491528 | tf_op jit(solution)/shard_map/ppermute | solution.py:42
  22.6 6.2 %collective-permute-start.11 = (f32[5,16,128]{2,1,0:T(8,128)S(1)}, f32[5,16,128]{2,1,0:T(8,128)S(1)}, u32[]{:S(2)}, u32[]{:S(2)}) collective-permute-start(f32[5,16,128]{2,1,0:T(8,128)S(1)} %get-tuple-element.41), channel_id=1, source_target_pairs={{0,24},{4,28},{8,16},{12,20},{16,8},{20,12},{24,0},{28,4},{1,25},{... | collective-permute-start | bytes 122888 | tf_op jit(solution)/shard_map/ppermute | solution.py:46
  25.7 4.7 %collective-permute-start.10 = (f32[5,16,128]{2,1,0:T(8,128)S(1)}, f32[5,16,128]{2,1,0:T(8,128)S(1)}, u32[]{:S(2)}, u32[]{:S(2)}) collective-permute-start(f32[5,16,128]{2,1,0:T(8,128)S(1)} %get-tuple-element.42), channel_id=1, source_target_pairs={{0,16},{4,20},{8,24},{12,28},{16,0},{20,4},{24,8},{28,12},{1,17},{... | collective-permute-start | bytes 122888 | tf_op jit(solution)/shard_map/ppermute | solution.py:46
  28.4 4.0 %collective-permute-start.9 = (f32[5,16,128]{2,1,0:T(8,128)S(1)}, f32[5,16,128]{2,1,0:T(8,128)S(1)}, u32[]{:S(2)}, u32[]{:S(2)}) collective-permute-start(f32[5,16,128]{2,1,0:T(8,128)S(1)} %get-tuple-element.43), channel_id=1, source_target_pairs={{0,8},{4,12},{8,0},{12,4},{16,24},{20,28},{24,16},{28,20},{1,9},{5... | collective-permute-start | bytes 122888 | tf_op jit(solution)/shard_map/ppermute | solution.py:46
  32.5 7.7 %collective-permute-start.14 = (f32[5,16,128]{2,1,0:T(8,128)S(1)}, f32[5,16,128]{2,1,0:T(8,128)S(1)}, u32[]{:S(2)}, u32[]{:S(2)}) collective-permute-start(f32[5,16,128]{2,1,0:T(8,128)S(1)} %fusion.3), channel_id=1, source_target_pairs={{0,3},{1,2},{2,1},{3,0},{4,7},{5,6},{6,5},{7,4},{8,11},{9,10},{10,... | collective-permute-start | bytes 122888 | tf_op jit(solution)/shard_map/ppermute | solution.py:46
  36.1 5.5 %collective-permute-start.13 = (f32[5,16,128]{2,1,0:T(8,128)S(1)}, f32[5,16,128]{2,1,0:T(8,128)S(1)}, u32[]{:S(2)}, u32[]{:S(2)}) collective-permute-start(f32[5,16,128]{2,1,0:T(8,128)S(1)} %fusion.3), channel_id=1, source_target_pairs={{0,2},{1,3},{2,0},{3,1},{4,6},{5,7},{6,4},{7,5},{8,10},{9,11},{10,... | collective-permute-start | bytes 122888 | tf_op jit(solution)/shard_map/ppermute | solution.py:46
  38.9 4.0 %collective-permute-start.12 = (f32[5,16,128]{2,1,0:T(8,128)S(1)}, f32[5,16,128]{2,1,0:T(8,128)S(1)}, u32[]{:S(2)}, u32[]{:S(2)}) collective-permute-start(f32[5,16,128]{2,1,0:T(8,128)S(1)} %fusion.3), channel_id=1, source_target_pairs={{0,1},{1,0},{2,3},{3,2},{4,5},{5,4},{6,7},{7,6},{8,9},{9,8},{10,11... | collective-permute-start | bytes 122888 | tf_op jit(solution)/shard_map/ppermute | solution.py:46
  43.1 17.7 %collective-permute-start.6 = (f32[2,3,128,128]{3,2,1,0:T(8,128)S(1)}, f32[2,3,128,128]{3,2,1,0:T(8,128)S(1)}, u32[]{:S(2)}, u32[]{:S(2)}) collective-permute-start(f32[2,3,128,128]{3,2,1,0:T(8,128)S(1)} %pad_maximum_fusion.1), channel_id=1, source_target_pairs={{0,1},{1,0},{2,3},{3,2},{4,5},{5,4},{6,7},{7,6},{8,9},{9,8},{10,11... | collective-permute-start | bytes 1179656 | tf_op jit(solution)/shard_map/ppermute | solution.py:42
  44.6 16.3 %collective-permute-start.7 = (f32[2,3,128,128]{3,2,1,0:T(8,128)S(1)}, f32[2,3,128,128]{3,2,1,0:T(8,128)S(1)}, u32[]{:S(2)}, u32[]{:S(2)}) collective-permute-start(f32[2,3,128,128]{3,2,1,0:T(8,128)S(1)} %pad_maximum_fusion.2), channel_id=1, source_target_pairs={{1,2},{2,1},{5,6},{6,5},{9,10},{10,9},{13,14},{14,13},{17,18},{18,... | collective-permute-start | bytes 1179656 | tf_op jit(solution)/shard_map/ppermute | solution.py:42
  45.3 13.6 %collective-permute-start.17 = (f32[4,16,128]{2,1,0:T(8,128)S(1)}, f32[4,16,128]{2,1,0:T(8,128)S(1)}, u32[]{:S(2)}, u32[]{:S(2)}) collective-permute-start(f32[4,16,128]{2,1,0:T(8,128)S(1)} %fusion.7), channel_id=1, source_target_pairs={{0,24},{4,28},{8,16},{12,20},{16,8},{20,12},{24,0},{28,4},{1,25},{... | collective-permute-start | bytes 98312 | tf_op jit(solution)/shard_map/ppermute | solution.py:46
  56.8 3.9 %collective-permute-start.16 = (f32[4,16,128]{2,1,0:T(8,128)S(1)}, f32[4,16,128]{2,1,0:T(8,128)S(1)}, u32[]{:S(2)}, u32[]{:S(2)}) collective-permute-start(f32[4,16,128]{2,1,0:T(8,128)S(1)} %fusion.7), channel_id=1, source_target_pairs={{0,16},{4,20},{8,24},{12,28},{16,0},{20,4},{24,8},{28,12},{1,17},{... | collective-permute-start | bytes 98312 | tf_op jit(solution)/shard_map/ppermute | solution.py:46
  68.6 5.0 %collective-permute-start.26 = (f32[5,16,128]{2,1,0:T(8,128)S(1)}, f32[5,16,128]{2,1,0:T(8,128)S(1)}, u32[]{:S(2)}, u32[]{:S(2)}) collective-permute-start(f32[5,16,128]{2,1,0:T(8,128)S(1)} %get-tuple-element.38), channel_id=1, source_target_pairs={{0,24},{4,28},{8,16},{12,20},{16,8},{20,12},{24,0},{28,4},{1,25},{... | collective-permute-start | bytes 122888 | tf_op jit(solution)/shard_map/ppermute | solution.py:46
  70.1 4.0 %collective-permute-start.25 = (f32[5,16,128]{2,1,0:T(8,128)S(1)}, f32[5,16,128]{2,1,0:T(8,128)S(1)}, u32[]{:S(2)}, u32[]{:S(2)}) collective-permute-start(f32[5,16,128]{2,1,0:T(8,128)S(1)} %get-tuple-element.39), channel_id=1, source_target_pairs={{0,16},{4,20},{8,24},{12,28},{16,0},{20,4},{24,8},{28,12},{1,17},{... | collective-permute-start | bytes 122888 | tf_op jit(solution)/shard_map/ppermute | solution.py:46
  71.6 4.0 %collective-permute-start.24 = (f32[5,16,128]{2,1,0:T(8,128)S(1)}, f32[5,16,128]{2,1,0:T(8,128)S(1)}, u32[]{:S(2)}, u32[]{:S(2)}) collective-permute-start(f32[5,16,128]{2,1,0:T(8,128)S(1)} %get-tuple-element.40), channel_id=1, source_target_pairs={{0,8},{4,12},{8,0},{12,4},{16,24},{20,28},{24,16},{28,20},{1,9},{5... | collective-permute-start | bytes 122888 | tf_op jit(solution)/shard_map/ppermute | solution.py:46
  75.7 6.2 %collective-permute-start.29 = (f32[5,16,128]{2,1,0:T(8,128)S(1)}, f32[5,16,128]{2,1,0:T(8,128)S(1)}, u32[]{:S(2)}, u32[]{:S(2)}) collective-permute-start(f32[5,16,128]{2,1,0:T(8,128)S(1)} %fusion.1), channel_id=1, source_target_pairs={{0,3},{1,2},{2,1},{3,0},{4,7},{5,6},{6,5},{7,4},{8,11},{9,10},{10,... | collective-permute-start | bytes 122888 | tf_op jit(solution)/shard_map/ppermute | solution.py:46
  78.1 5.6 %collective-permute-start.28 = (f32[5,16,128]{2,1,0:T(8,128)S(1)}, f32[5,16,128]{2,1,0:T(8,128)S(1)}, u32[]{:S(2)}, u32[]{:S(2)}) collective-permute-start(f32[5,16,128]{2,1,0:T(8,128)S(1)} %fusion.1), channel_id=1, source_target_pairs={{0,2},{1,3},{2,0},{3,1},{4,6},{5,7},{6,4},{7,5},{8,10},{9,11},{10,... | collective-permute-start | bytes 122888 | tf_op jit(solution)/shard_map/ppermute | solution.py:46
  81.1 4.0 %collective-permute-start.27 = (f32[5,16,128]{2,1,0:T(8,128)S(1)}, f32[5,16,128]{2,1,0:T(8,128)S(1)}, u32[]{:S(2)}, u32[]{:S(2)}) collective-permute-start(f32[5,16,128]{2,1,0:T(8,128)S(1)} %fusion.1), channel_id=1, source_target_pairs={{0,1},{1,0},{2,3},{3,2},{4,5},{5,4},{6,7},{7,6},{8,9},{9,8},{10,11... | collective-permute-start | bytes 122888 | tf_op jit(solution)/shard_map/ppermute | solution.py:46
  81.1 4.0 %collective-permute-start.19 = (f32[2,3,128,128]{3,2,1,0:T(8,128)S(1)}, f32[2,3,128,128]{3,2,1,0:T(8,128)S(1)}, u32[]{:S(2)}, u32[]{:S(2)}) collective-permute-start(f32[2,3,128,128]{3,2,1,0:T(8,128)S(1)} %get-tuple-element.18), channel_id=1, source_target_pairs={{0,4},{4,0},{8,12},{12,8},{16,20},{20,16},{24,28},{28,24},{1,5},{5... | collective-permute-start | bytes 1179656 | tf_op jit(solution)/shard_map/ppermute | solution.py:42
  85.3 17.3 %collective-permute-start.21 = (f32[2,3,128,128]{3,2,1,0:T(8,128)S(1)}, f32[2,3,128,128]{3,2,1,0:T(8,128)S(1)}, u32[]{:S(2)}, u32[]{:S(2)}) collective-permute-start(f32[2,3,128,128]{3,2,1,0:T(8,128)S(1)} %pad_maximum_fusion.3), channel_id=1, source_target_pairs={{0,1},{1,0},{2,3},{3,2},{4,5},{5,4},{6,7},{7,6},{8,9},{9,8},{10,11... | collective-permute-start | bytes 1179656 | tf_op jit(solution)/shard_map/ppermute | solution.py:42
  86.3 16.3 %collective-permute-start.22 = (f32[2,3,128,128]{3,2,1,0:T(8,128)S(1)}, f32[2,3,128,128]{3,2,1,0:T(8,128)S(1)}, u32[]{:S(2)}, u32[]{:S(2)}) collective-permute-start(f32[2,3,128,128]{3,2,1,0:T(8,128)S(1)} %pad_maximum_fusion.4), channel_id=1, source_target_pairs={{1,2},{2,1},{5,6},{6,5},{9,10},{10,9},{13,14},{14,13},{17,18},{18,... | collective-permute-start | bytes 1179656 | tf_op jit(solution)/shard_map/ppermute | solution.py:42
  87.0 13.2 %collective-permute-start.32 = (f32[4,16,128]{2,1,0:T(8,128)S(1)}, f32[4,16,128]{2,1,0:T(8,128)S(1)}, u32[]{:S(2)}, u32[]{:S(2)}) collective-permute-start(f32[4,16,128]{2,1,0:T(8,128)S(1)} %fusion.5), channel_id=1, source_target_pairs={{0,24},{4,28},{8,16},{12,20},{16,8},{20,12},{24,0},{28,4},{1,25},{... | collective-permute-start | bytes 98312 | tf_op jit(solution)/shard_map/ppermute | solution.py:46
  98.4 4.1 %collective-permute-start.30 = (f32[4,16,128]{2,1,0:T(8,128)S(1)}, f32[4,16,128]{2,1,0:T(8,128)S(1)}, u32[]{:S(2)}, u32[]{:S(2)}) collective-permute-start(f32[4,16,128]{2,1,0:T(8,128)S(1)} %fusion.5), channel_id=1, source_target_pairs={{0,8},{4,12},{8,0},{12,4},{16,24},{20,28},{24,16},{28,20},{1,9},{5... | collective-permute-start | bytes 98312 | tf_op jit(solution)/shard_map/ppermute | solution.py:46
  (15 other events, 30.1 us)
where the time goes:
time: 107 us; the launch traced here: 105 us
  starting transfers between devices  60.7 us (57%)
  waiting for transfers between devices  27.4 us (26%)
  Pallas kernels  11.3 us (11%)
  local copies, waits for them, and re-layouts  2.94 us (3%)
  other arithmetic  2 us (2%)
  between operations  1.12 us (1%)
    ppermute x18, starting transfers between devices, flipped(): lax.ppermute(values, axis, [(i, i ^ bits) for i in range(lax.axis_size(ax...  46.1 us
    ppermute x18, waiting for transfers between devices, flipped(): lax.ppermute(values, axis, [(i, i ^ bits) for i in range(lax.axis_size(ax...  19.8 us
    ppermute x16, starting transfers between devices, swapped(): return lax.ppermute(values, axis, pairs)  14.6 us
    ppermute x16, waiting for transfers between devices, swapped(): return lax.ppermute(values, axis, pairs)  7.63 us
    pallas_call x1, Pallas kernels, per_device(): pl.pallas_call(next_kernel, out_shape=outs + (f32(2, 2, size, tile),), in...  4.96 us
    pallas_call x1, Pallas kernels, per_device(): pl.pallas_call(first_kernel, out_shape=outs, in_specs=[SMEM] + [VMEM] * 4...  4.82 us
    unnamed x11, local copies, waits for them, and re-layouts  2.53 us
  transfers between devices with their start and end apart: 34, of which 20 were waited for; matrix products, arithmetic and copies ran while one was open for 1% of the time, Pallas kernels for 0%

commit v1 on v0

v1 whole, which is shorter than its diff:
```python
import functools

import jax
import jax.numpy as jnp
import numpy as np
from jax import lax
from jax.experimental import pallas as pl
from jax.experimental.pallas import tpu as pltpu
from jax.sharding import PartitionSpec as P

ITERS = 2
OBJECT_STEP = 0.5
PROBE_STEP = 2.0
REGULAR = 1.0


def dft_tables(extent):
    line = np.arange(extent)
    angle = (line[:, None] * line[None, :] % extent) * (2.0 * np.pi / extent)
    cosine, sine = np.cos(angle) / np.sqrt(extent), np.sin(angle) / np.sqrt(extent)
    table = np.block([[cosine, -sine], [sine, cosine]])
    high = table.astype(jnp.bfloat16)
    low = (table - high.astype(np.float64)).astype(jnp.bfloat16)
    return np.stack([high, low, high.T, low.T])


def split(values):
    high = values.astype(jnp.bfloat16)
    return high, (values - high.astype(jnp.float32)).astype(jnp.bfloat16)


def product(left, right):
    dot = functools.partial(jnp.dot, preferred_element_type=jnp.float32)
    return dot(left[0], right[0]) + (dot(left[0], right[1]) + dot(left[1], right[0]))


def swapped(values, axis, odd):
    count = lax.axis_size(axis)
    pairs = []
    for first in range(1 if odd else 0, count - 1, 2):
        pairs += [(first, first + 1), (first + 1, first)]
    return lax.ppermute(values, axis, pairs)


def flipped(values, axis, bits):
    return lax.ppermute(values, axis, [(i, i ^ bits) for i in range(lax.axis_size(axis))])


def tree_sum(parts):
    while len(parts) > 1:
        parts = [parts[i] + parts[i + 1] for i in range(0, len(parts), 2)]
    return parts[0]


def head_scalars(canvas_size, halo):
    row, col = lax.axis_index("sy"), lax.axis_index("sx")
    rows, cols = lax.axis_size("sy"), lax.axis_size("sx")
    head = [
        row % 2,
        col % 2,
        row // 2,
        jnp.where(row == 0, halo, 0),
        jnp.where(row == rows - 1, canvas_size - halo, canvas_size),
        jnp.where(col == 0, halo, 0),
        jnp.where(col == cols - 1, canvas_size - halo, canvas_size),
    ]
    return jnp.stack(head).astype(jnp.int32)


HEAD = 7


def light_kernel(scal, corners, probe_ref, scale_ref, lit):
    _, size, extent = scale_ref.shape
    lit[...] = jnp.zeros_like(lit)
    weight = sum(probe_ref[k, part] * probe_ref[k, part] for k in range(probe_ref.shape[0]) for part in range(2))
    lane = lax.broadcasted_iota(jnp.int32, (extent, extent), 1)

    count = corners.shape[0] // 18
    for device in range(9):
        for j in range(device * count, (device + 1) * count):
            row, col = corners[2 * j] + extent, corners[2 * j + 1]
            moved = pltpu.roll(weight, col & (extent - 1), 1)
            for side in range(2):
                if device % 3 == 2 * (1 - side):
                    continue
                covered = (lane + side * extent >= col) & (lane + side * extent < col + extent)
                lit[side, pl.ds(row, extent), :] += jnp.where(covered, moved, 0.0)
    at_row = lax.broadcasted_iota(jnp.int32, (size, extent), 0)
    at_col = lax.broadcasted_iota(jnp.int32, (size, extent), 1)
    for side in range(2):
        inside = (at_row >= scal[3]) & (at_row < scal[4]) & (at_col + side * extent >= scal[5])
        inside = inside & (at_col + side * extent < scal[6])
        lighting = lit[side, extent : extent + size, :]
        scale_ref[side] = jnp.where(inside, OBJECT_STEP / (lighting + REGULAR), 0.0)


def updated_canvas(scal, old_ref, scale_ref, sums, canvas_ref):
    half = old_ref.shape[-1]
    for a in range(2):
        row = pl.multiple_of(jnp.where(scal[0] == a, half, 0), half)
        for b in range(2):
            side = jnp.where(scal[1] == b, 1, 0)
            scale = scale_ref[side, pl.ds(row, half)]
            for part in range(2):
                here = (part, side, pl.ds(row, half))
                canvas_ref[here] = old_ref[here] - scale * sums[a][b, part]


def place_probe(scal, own_ref, other_ref, probe_ref):
    chips, planes, rows, _ = own_ref.shape
    for slot in range(chips):
        chunk = scal[2] ^ slot
        for which, ref in ((scal[0], own_ref), (1 - scal[0], other_ref)):
            start = pl.multiple_of((which * chips + chunk) * rows, rows)
            for plane in range(planes):
                probe_ref[plane // 2, plane % 2, pl.ds(start, rows), :] = ref[slot, plane]


def terms_body(scal, offs, canvas_ref, probe_ref, measured_ref, table_ref, outs, keep_out, send_out, grad, sums):
    positions, extent, _ = measured_ref.shape
    modes = probe_ref.shape[0]
    w1 = (table_ref[0], table_ref[1])
    w2 = (table_ref[2], table_ref[3])
    grad[...] = jnp.zeros_like(grad)
    lane = lax.broadcasted_iota(jnp.int32, (extent, extent), 1)
    group = positions // 2
    for first in range(0, positions, group):
        span = range(first, min(first + group, positions))
        patches = []
        for j in span:
            row, col = offs[2 * j], offs[2 * j + 1]
            back = (extent - col) & (extent - 1)
            patches.append([
                jnp.where(
                    lane < extent - col,
                    pltpu.roll(canvas_ref[part, 0, pl.ds(row, extent), :], back, 1),
                    pltpu.roll(canvas_ref[part, 1, pl.ds(row, extent), :], back, 1),
                )
                for part in range(2)
            ])
        waves = []
        for o_r, o_i in patches:
            for k in range(modes):
                p_r, p_i = probe_ref[k, 0], probe_ref[k, 1]
                waves.append(jnp.concatenate([p_r * o_r - p_i * o_i, p_r * o_i + p_i * o_r], axis=1))
        count = len(waves)
        half = product(split(jnp.concatenate(waves, axis=0)), w1)
        rows = [half[k * extent : (k + 1) * extent] for k in range(count)]
        half = jnp.concatenate(
            [jnp.concatenate([r[:, part * extent : (part + 1) * extent] for r in rows], axis=1) for part in range(2)],
            axis=0,
        )
        spectrum = product(w2, split(half))
        squares = spectrum * spectrum
        power = squares[:extent] + squares[extent:]
        wide = []
        for at, j in enumerate(span):
            misfit = sum(power[:, k * extent : (k + 1) * extent] for k in range(at * modes, (at + 1) * modes)) - measured_ref[j]
            wide += [misfit] * modes
        wide = jnp.concatenate(wide, axis=1)
        weighted = spectrum * jnp.concatenate([wide, wide], axis=0)
        half = product(w1, split(weighted))
        half = jnp.concatenate(
            [
                jnp.concatenate([half[:extent, k * extent : (k + 1) * extent], half[extent:, k * extent : (k + 1) * extent]], axis=1)
                for k in range(count)
            ],
            axis=0,
        )
        chi = product(split(half), w2)
        for at, j in enumerate(span):
            o_r, o_i = patches[at]
            row, col = offs[2 * j], offs[2 * j + 1]
            turn = col & (extent - 1)
            g_r = g_i = 0.0
            for k in range(modes):
                p_r, p_i = probe_ref[k, 0], probe_ref[k, 1]
                wave = at * modes + k
                c_r = chi[wave * extent : (wave + 1) * extent, :extent]
                c_i = chi[wave * extent : (wave + 1) * extent, extent:]
                g_r = g_r + (p_r * c_r + p_i * c_i)
                g_i = g_i + (p_r * c_i - p_i * c_r)
                for part, term in ((0, o_r * c_r + o_i * c_i), (1, o_r * c_i - o_i * c_r)):
                    plane = 2 * k + part
                    sums[plane] = term if j == 0 else sums[plane] + term
            term = o_r * o_r + o_i * o_i
            sums[2 * modes] = term if j == 0 else sums[2 * modes] + term
            for plane, term in enumerate((g_r, g_i)):
                moved = pltpu.roll(term, turn, 1)
                grad[plane, 0, pl.ds(row, extent), :] += jnp.where(lane >= col, moved, 0.0)
                grad[plane, 1, pl.ds(row, extent), :] += jnp.where(lane < col, moved, 0.0)
    if len(outs) == 1:
        give_quadrants(scal, grad, outs)
    else:
        give_rims(scal, grad, outs)
    chips, planes, rows, _ = keep_out.shape
    for slot in range(chips):
        chunk = scal[2] ^ slot
        for which, ref in ((scal[0], keep_out), (1 - scal[0], send_out)):
            start = pl.multiple_of((which * chips + chunk) * rows, rows)
            for plane in range(planes):
                ref[slot, plane] = sums[plane, pl.ds(start, rows), :]


def give_quadrants(scal, grad, outs):
    extent = grad.shape[-1]
    for a in range(2):
        row = pl.multiple_of(jnp.where(scal[0] == a, extent, 0), extent)
        for b in range(2):
            side = jnp.where(scal[1] == b, 1, 0)
            for plane in range(grad.shape[0]):
                outs[0][b, a, plane] = grad[plane, side, pl.ds(row, extent), :]


def give_rims(scal, grad, outs):
    extent = grad.shape[-1]
    halo = extent // 2
    lane = lax.broadcasted_iota(jnp.int32, (extent, extent), 1)
    for plane in range(grad.shape[0]):
        upper = [grad[plane, side, 0:extent, :] for side in range(2)]
        lower = [grad[plane, side, extent : 2 * extent, :] for side in range(2)]
        for start, rows in ((0, upper), (extent, lower)):
            outs[0][plane, start : start + extent, :] = jnp.where(
                lane < halo, pltpu.roll(rows[0], halo, 1), pltpu.roll(rows[1], halo, 1)
            )
        left = jnp.where(lane < halo, upper[0], pltpu.roll(lower[0], halo, 1))
        right = jnp.where(lane < halo, pltpu.roll(upper[1], halo, 1), lower[1])
        outs[1][1 - scal[1], plane] = left
        outs[1][scal[1], plane] = right


def rim_kernel(scal, own_ref, near_ref, far_ref, middle_ref, near_out, far_out):
    _, size, extent = own_ref.shape
    halo = extent // 2
    lane = lax.broadcasted_iota(jnp.int32, (extent, extent), 1)
    odd = scal[1] == 1
    for plane in range(own_ref.shape[0]):
        near, far = near_ref[plane], far_ref[plane]
        from_left, from_right = jnp.where(odd, near, far), jnp.where(odd, far, near)
        upper = own_ref[plane, 0:extent] + jnp.where(lane < halo, from_left, pltpu.roll(from_right, halo, 1))
        lower = own_ref[plane, extent:size] + jnp.where(lane < halo, pltpu.roll(from_left, halo, 1), from_right)
        middle_ref[plane, 0:halo] = upper[halo:]
        middle_ref[plane, halo:extent] = lower[:halo]
        near_out[plane] = jnp.where(scal[0] == 1, upper[:halo], lower[halo:])
        far_out[plane] = jnp.where(scal[0] == 1, lower[halo:], upper[:halo])


def first_kernel(
    scal, offs, tile_ref, rows_near, rows_far, cols_near, cols_far, probe_ref, measured_ref, table_ref, *rest
):
    outs, (keep_out, send_out, canvas_ref, grad, sums) = rest[:-5], rest[-5:]
    extent = tile_ref.shape[-1]
    halo = extent // 2
    size = 2 * extent
    odd_row, odd_col = scal[0] == 1, scal[1] == 1
    lane = lax.broadcasted_iota(jnp.int32, (extent, extent), 1)
    for part in range(2):
        near, far = (ref[part * halo : (part + 1) * halo] for ref in (rows_near, rows_far))
        above, below = jnp.where(odd_row, near, far), jnp.where(odd_row, far, near)
        for start in range(0, size, extent):
            half = pl.ds(start, extent)
            if start == 0:
                middle = jnp.concatenate([above, tile_ref[part, :halo]], axis=0)
            else:
                middle = jnp.concatenate([tile_ref[part, halo:], below], axis=0)
            middle = pltpu.roll(middle, halo, 1)
            near, far = cols_near[half], cols_far[half]
            if part == 1:
                near, far = pltpu.roll(near, halo, 1), pltpu.roll(far, halo, 1)
            left, right = jnp.where(odd_col, near, far), jnp.where(odd_col, far, near)
            canvas_ref[part, 0, half] = jnp.where(lane < halo, left, middle)
            canvas_ref[part, 1, half] = jnp.where(lane < halo, middle, pltpu.roll(right, halo, 1))
    terms_body(scal, offs, canvas_ref, probe_ref, measured_ref, table_ref, outs, keep_out, send_out, grad, sums)


def next_kernel(scal, offs, old_ref, scale_ref, near_ref, far_ref, own_ref, other_ref, measured_ref, table_ref, *rest):
    outs, (keep_out, send_out, canvas_ref, probe_ref, grad, sums) = rest[:-6], rest[-6:]
    updated_canvas(scal, old_ref, scale_ref, (near_ref, far_ref), canvas_ref)
    place_probe(scal, own_ref, other_ref, probe_ref)
    terms_body(scal, offs, canvas_ref, probe_ref, measured_ref, table_ref, outs, keep_out, send_out, grad, sums)


def last_kernel(scal, old_ref, scale_ref, middle_ref, near_ref, far_ref, own_ref, other_ref, object_ref, probe_ref):
    half = old_ref.shape[-1]
    halo = half // 2
    place_probe(scal, own_ref, other_ref, probe_ref)
    lane = lax.broadcasted_iota(jnp.int32, (half, half), 1)
    middle = pl.ds(halo, half)

    def tile_of(sides):
        return jnp.where(lane < halo, pltpu.roll(sides[0], halo, 1), pltpu.roll(sides[1], halo, 1))

    scale = tile_of([scale_ref[side, middle] for side in range(2)])
    odd = scal[0] == 1
    for part in range(2):
        near, far = near_ref[part], far_ref[part]
        from_rows = jnp.concatenate([jnp.where(odd, near, far), jnp.where(odd, far, near)], axis=0)
        old = tile_of([old_ref[part, side, middle] for side in range(2)])
        object_ref[part] = old - scale * (middle_ref[part] + from_rows)


SMEM = pl.BlockSpec(memory_space=pltpu.SMEM)
VMEM = pl.BlockSpec(memory_space=pltpu.VMEM)
PARAMS = pltpu.CompilerParams(vmem_limit_bytes=32 * 1024 * 1024)


def f32(*shape):
    return jax.ShapeDtypeStruct(shape, jnp.float32)


def kernel_call(body, outs, operands, scratch=(), scalars=2, flops=0):
    return pl.pallas_call(
        body,
        out_shape=outs,
        in_specs=[SMEM] * scalars + [VMEM] * (len(operands) - scalars),
        out_specs=jax.tree.map(lambda _: VMEM, outs),
        scratch_shapes=[pltpu.VMEM(shape, jnp.float32) for shape in scratch],
        compiler_params=PARAMS,
        cost_estimate=pl.CostEstimate(flops=flops, bytes_accessed=1 << 20, transcendentals=0),
    )(*operands)


def fetch(tile, offsets, halo):
    lanes = tile.shape[-1]
    odd_row, odd_col = (lax.axis_index(axis) % 2 == 1 for axis in ("sy", "sx"))
    corners = jnp.pad((offsets.reshape(1, -1) + 1).astype(jnp.float32), ((0, 7), (0, lanes - offsets.size)))

    def rows_of(rim):
        return jnp.concatenate([rim.reshape(-1, lanes), corners])

    upper, lower = tile[:, :halo], tile[:, -halo:]
    rows_near = swapped(rows_of(jnp.where(odd_row, upper, lower)), "sy", False)
    rows_far = swapped(rows_of(jnp.where(odd_row, lower, upper)), "sy", True)
    last = 2 * halo
    above, below = jnp.where(odd_row, rows_near, rows_far), jnp.where(odd_row, rows_far, rows_near)
    column = jnp.concatenate([above[:last].reshape(2, halo, lanes), tile, below[:last].reshape(2, halo, lanes)], axis=1)
    reach = jnp.concatenate([above[last : last + 1], corners[:1], below[last : last + 1], corners[3:]])

    def columns_of(rim):
        return jnp.concatenate([jnp.concatenate([rim[0], rim[1]], axis=1), reach])

    left, right = column[..., :halo], column[..., -halo:]
    cols_near = swapped(columns_of(jnp.where(odd_col, left, right)), "sx", False)
    cols_far = swapped(columns_of(jnp.where(odd_col, right, left)), "sx", True)
    sides = [jnp.where(odd_col, cols_near, cols_far), reach, jnp.where(odd_col, cols_far, cols_near)]
    found = jnp.stack([side[-8:-5, : offsets.size] for side in sides], axis=1).astype(jnp.int32) - 1
    found = found.reshape(3, 3, -1, 2)
    step = (jnp.arange(3, dtype=jnp.int32) - 1) * lanes
    shift = jnp.stack(jnp.broadcast_arrays(step[:, None], step[None, :]), axis=-1)[:, :, None]
    return rows_near, rows_far, cols_near, cols_far, jnp.where(found < 0, -lanes, found + shift).reshape(-1)


def after(value, *others):
    return lax.optimization_barrier((value, *others))[0]


def chip_sum(both):
    return tree_sum([both[0]] + [flipped(both[t], "sy", 2 * t) for t in range(1, both.shape[0])])


def probe_fresh(total, chunk):
    planes = chunk.shape[0]
    total = tree_sum([total] + [flipped(total, "sx", t) for t in range(1, lax.axis_size("sx"))])
    return chunk - PROBE_STEP * total[:planes] / (total[planes:] + REGULAR)


def probe_spread(fresh, chips):
    own = jnp.stack([fresh] + [flipped(fresh, "sy", 2 * t) for t in range(1, chips)])
    return own, swapped(own, "sy", False)


def per_device(object_tile, probe_modes, scan_offsets, intensities):
    tile = object_tile.shape[1]
    modes, _, extent, _ = probe_modes.shape
    halo = extent // 2
    size = tile + 2 * halo
    chips = lax.axis_size("sy") // 2
    rows = extent // 2 // chips
    planes = 2 * modes
    measured = intensities[0, 0]
    table = jnp.asarray(dft_tables(extent))
    scal = head_scalars(size, halo)
    offsets = scan_offsets[0, 0]
    offs = offsets.reshape(-1)
    probe_outs = (f32(chips, planes + 1, rows, extent),) * 2 + (f32(2, 2, size, tile),)
    quadrants = (f32(2, 2, 2, tile, tile),)
    rims = (f32(2, size, tile), f32(2, 2, tile, tile))
    scratch = ((2, 2, size, tile), (planes + 1, extent, extent))
    work = 2 * 3 * offsets.shape[0] * 4 * (2 * extent) ** 3

    start = (lax.axis_index("sy") % 2 * chips + lax.axis_index("sy") // 2) * rows
    chunk = lax.dynamic_slice_in_dim(probe_modes.reshape(planes, extent, extent), start, rows, axis=1)
    *halos, corners = fetch(object_tile, offsets, halo)

    def light(probe, corners):
        lit = (2, 2 * size, extent)
        return kernel_call(light_kernel, f32(2, size, tile), (scal, corners, probe), [lit], flops=work // 2)

    probe = probe_modes
    for iteration in range(ITERS):
        final = iteration == ITERS - 1
        outs = (rims if final else quadrants) + probe_outs
        if iteration == 0:
            operands = (scal, offs, object_tile, *halos, probe, measured, table)
            *given, keep, send, canvas = kernel_call(first_kernel, outs, operands, scratch, flops=work)
        else:
            operands = (scal, offs, canvas, scale, near, far, own, other, measured, table)
            outs = outs + (f32(*probe.shape),)
            *given, keep, send, canvas, probe = kernel_call(next_kernel, outs, operands, scratch, flops=work)
        both = keep + swapped(send, "sy", False)
        scale = light(probe, after(corners, both))
        if not final:
            (grad,) = given
            side_a = grad[0] + swapped(grad[0], "sx", False)
            side_b = grad[1] + swapped(grad[1], "sx", True)
            near, far = jnp.stack([side_a[0], side_b[0]]), jnp.stack([side_a[1], side_b[1]])
            total = after(chip_sum(both), near, far, scale)
            near = near + swapped(near, "sy", False)
            far = far + swapped(far, "sy", True)
            chunk = after(probe_fresh(total, chunk), near, far)
        else:
            own_columns, side = given
            near, far = swapped(side[0], "sx", False), swapped(side[1], "sx", True)
            total = after(chip_sum(both), near, far, scale)
            middle, near, far = kernel_call(
                rim_kernel, (f32(2, tile, tile),) + (f32(2, halo, tile),) * 2, (scal, own_columns, near, far), scalars=1
            )
            near, far = swapped(near, "sy", False), swapped(far, "sy", True)
            chunk = after(probe_fresh(total, chunk), near, far)
        own, other = probe_spread(chunk, chips)
    outs = (f32(2, tile, tile), f32(*probe.shape))
    return kernel_call(last_kernel, outs, (scal, canvas, scale, middle, near, far, own, other), scalars=1)


def solution(mesh):
    placed = (P(None, "sy", "sx"), P(), P("sy", "sx", None, None), P("sy", "sx", None, None, None))
    return jax.shard_map(
        per_device,
        mesh=mesh,
        in_specs=placed,
        out_specs=(P(None, "sy", "sx"), P()),
        check_vma=False,
    )
```

time: 107 us -> 94.6 us (0.88); the launches traced: 105 us -> 94.2 us
  waiting for transfers between devices: 27.4 us -> 21.1 us
  starting transfers between devices: 60.7 us -> 54.8 us
  Pallas kernels: 11.3 us -> 12.7 us
    ppermute x18, starting transfers between devices: 46.1 us -> 34.9 us  [flipped(): lax.ppermute(values, axis, [(i, i ^ bits) for i in range(lax.axis_size(ax...]
    ppermute x18, waiting for transfers between devices: 19.8 us -> 13.8 us  [flipped(): lax.ppermute(values, axis, [(i, i ^ bits) for i in range(lax.axis_size(ax...]
    ppermute x16, starting transfers between devices: 14.6 us -> 19.9 us  [swapped(): return lax.ppermute(values, axis, pairs)]
    pallas_call x3 -> x6, Pallas kernels: 11.3 us -> 12.7 us  [kernel_call(): pl.pallas_call(body, out_shape=outs, in_specs=[SMEM] * scalars + [VMEM] *...]
  transfers between devices with their start and end apart: 34 -> 34, of which waited for: 20 -> 16; matrix products, arithmetic and copies ran while one was open for 1% -> 1% of each run, Pallas kernels for 0% -> 4%
where the time goes in v1:
time: 94.6 us; the launch traced here: 94.2 us
  starting transfers between devices  54.8 us (58%)
  waiting for transfers between devices  21.1 us (22%)
  Pallas kernels  12.7 us (13%)
  local copies, waits for them, and re-layouts  2.83 us (3%)
  other arithmetic  1.64 us (2%)
  between operations  1.17 us (1%)
    ppermute x18, starting transfers between devices, flipped(): lax.ppermute(values, axis, [(i, i ^ bits) for i in range(lax.axis_size(ax...  34.9 us
    ppermute x16, starting transfers between devices, swapped(): return lax.ppermute(values, axis, pairs)  19.9 us
    ppermute x18, waiting for transfers between devices, flipped(): lax.ppermute(values, axis, [(i, i ^ bits) for i in range(lax.axis_size(ax...  13.8 us
    pallas_call x6, Pallas kernels, kernel_call(): pl.pallas_call(body, out_shape=outs, in_specs=[SMEM] * scalars + [VMEM] *...  12.7 us
    ppermute x16, waiting for transfers between devices, swapped(): return lax.ppermute(values, axis, pairs)  7.31 us
  transfers between devices with their start and end apart: 34, of which 16 were waited for; matrix products, arithmetic and copies ran while one was open for 1% of the time, Pallas kernels for 4%

profile of v1, /device:TPU:0, one launch (start us, length us, event | category | flops | bytes accessed | tf_op | source)
XLA Modules:
  0.0 94.2 jit_solution(4485763738224682169)
XLA Ops:
  3.1 4.4 %collective-permute-start = (f32[136,128]{1,0:T(8,128)S(1)}, f32[136,128]{1,0:T(8,128)S(1)}, u32[]{:S(2)}, u32[]{:S(2)}) collective-permute-start(f32[136,128]{1,0:T(8,128)S(1)} %get-tuple-element.69), channel_id=1, source_target_pairs={{0,4},{4,0},{8,12},{12,8},{16,20},{20,16},{24,28},{28,24},{1,5},{5... | collective-permute-start | bytes 208904 | tf_op jit(solution)/shard_map/ppermute | solution.py:42
  9.8 1.6 %collective-permute-start.2 = (f32[264,128]{1,0:T(8,128)S(1)}, f32[264,128]{1,0:T(8,128)S(1)}, u32[]{:S(2)}, u32[]{:S(2)}) collective-permute-start(f32[264,128]{1,0:T(8,128)S(1)} %concatenate.32), channel_id=1, source_target_pairs={{0,1},{1,0},{2,3},{3,2},{4,5},{5,4},{6,7},{7,6},{8,9},{9,8},{10,11... | collective-permute-start | bytes 405512 | tf_op jit(solution)/shard_map/ppermute | solution.py:42
  12.6 3.7 %collective-permute-done.2.cols_near = f32[264,128]{1,0:T(8,128)S(1)} collective-permute-done((f32[264,128]{1,0:T(8,128)S(1)}, f32[264,128]{1,0:T(8,128)S(1)}, u32[]{:S(2)}, u32[]{:S(2)}) %collective-permute-start.2) | collective-permute-done | bytes 135200 | tf_op jit(solution)/shard_map/ppermute | solution.py:42
  16.8 4.0 %shard_map.68 = (f32[2,2,2,128,128]{4,3,2,1,0:T(8,128)S(1)}, f32[4,5,16,128]{3,2,1,0:T(8,128)S(1)}, f32[4,5,16,128]{3,2,1,0:T(8,128)S(1)}, f32[2,2,256,128]{3,2,1,0:T(8,128)S(1)}) custom-call(s32[7]{0:T(128)S(1)} %stack.82.scal, s32[8]{0:T(128)S(1)} %reshape_squeeze.4.offs, f32[2,128,128]{2,1,0:T(8,128)S(1)} %copy-done, ...), custom_call_target="tpu_custom_call" | custom-call | flops 1610612736 | bytes 1048576 | tf_op jit(solution)/shard_map/pallas_call | solution.py:313
  21.0 4.7 %collective-permute-start.5 = (f32[2,2,128,128]{3,2,1,0:T(8,128)S(1)}, f32[2,2,128,128]{3,2,1,0:T(8,128)S(1)}, u32[]{:S(2)}, u32[]{:S(2)}) collective-permute-start(f32[2,2,128,128]{3,2,1,0:T(8,128)S(1)} %get-tuple-element.42), channel_id=1, source_target_pairs={{0,1},{1,0},{2,3},{3,2},{4,5},{5,4},{6,7},{7,6},{8,9},{9,8},{10,11... | collective-permute-start | bytes 786440 | tf_op jit(solution)/shard_map/ppermute | solution.py:42
  26.4 2.8 %collective-permute-start.11 = (f32[5,16,128]{2,1,0:T(8,128)S(1)}, f32[5,16,128]{2,1,0:T(8,128)S(1)}, u32[]{:S(2)}, u32[]{:S(2)}) collective-permute-start(f32[5,16,128]{2,1,0:T(8,128)S(1)} %get-tuple-element.61), channel_id=1, source_target_pairs={{0,24},{4,28},{8,16},{12,20},{16,8},{20,12},{24,0},{28,4},{1,25},{... | collective-permute-start | bytes 122888 | tf_op jit(solution)/shard_map/ppermute | solution.py:46
  31.7 1.6 %collective-permute-done.10 = f32[5,16,128]{2,1,0:T(8,128)S(1)} collective-permute-done((f32[5,16,128]{2,1,0:T(8,128)S(1)}, f32[5,16,128]{2,1,0:T(8,128)S(1)}, u32[]{:S(2)}, u32[]{:S(2)}) %collective-permute-start.10) | collective-permute-done | bytes 40992 | tf_op jit(solution)/shard_map/ppermute | solution.py:46
  34.6 3.1 %collective-permute-start.14 = (f32[5,16,128]{2,1,0:T(8,128)S(1)}, f32[5,16,128]{2,1,0:T(8,128)S(1)}, u32[]{:S(2)}, u32[]{:S(2)}) collective-permute-start(f32[5,16,128]{2,1,0:T(8,128)S(1)} %fusion.3), channel_id=1, source_target_pairs={{0,3},{1,2},{2,1},{3,0},{4,7},{5,6},{6,5},{7,4},{8,11},{9,10},{10,... | collective-permute-start | bytes 122888 | tf_op jit(solution)/shard_map/ppermute | solution.py:46
  37.7 1.8 %collective-permute-start.13 = (f32[5,16,128]{2,1,0:T(8,128)S(1)}, f32[5,16,128]{2,1,0:T(8,128)S(1)}, u32[]{:S(2)}, u32[]{:S(2)}) collective-permute-start(f32[5,16,128]{2,1,0:T(8,128)S(1)} %fusion.3), channel_id=1, source_target_pairs={{0,2},{1,3},{2,0},{3,1},{4,6},{5,7},{6,4},{7,5},{8,10},{9,11},{10,... | collective-permute-start | bytes 122888 | tf_op jit(solution)/shard_map/ppermute | solution.py:46
  40.4 2.6 %collective-permute-done.13 = f32[5,16,128]{2,1,0:T(8,128)S(1)} collective-permute-done((f32[5,16,128]{2,1,0:T(8,128)S(1)}, f32[5,16,128]{2,1,0:T(8,128)S(1)}, u32[]{:S(2)}, u32[]{:S(2)}) %collective-permute-start.13) | collective-permute-done | bytes 40992 | tf_op jit(solution)/shard_map/ppermute | solution.py:46
  43.6 7.1 %collective-permute-start.17 = (f32[4,16,128]{2,1,0:T(8,128)S(1)}, f32[4,16,128]{2,1,0:T(8,128)S(1)}, u32[]{:S(2)}, u32[]{:S(2)}) collective-permute-start(f32[4,16,128]{2,1,0:T(8,128)S(1)} %fusion.7), channel_id=1, source_target_pairs={{0,24},{4,28},{8,16},{12,20},{16,8},{20,12},{24,0},{28,4},{1,25},{... | collective-permute-start | bytes 98312 | tf_op jit(solution)/shard_map/ppermute | solution.py:46
  50.7 1.4 %collective-permute-start.16 = (f32[4,16,128]{2,1,0:T(8,128)S(1)}, f32[4,16,128]{2,1,0:T(8,128)S(1)}, u32[]{:S(2)}, u32[]{:S(2)}) collective-permute-start(f32[4,16,128]{2,1,0:T(8,128)S(1)} %fusion.7), channel_id=1, source_target_pairs={{0,16},{4,20},{8,24},{12,28},{16,0},{20,4},{24,8},{28,12},{1,17},{... | collective-permute-start | bytes 98312 | tf_op jit(solution)/shard_map/ppermute | solution.py:46
  52.1 1.4 %collective-permute-start.15 = (f32[4,16,128]{2,1,0:T(8,128)S(1)}, f32[4,16,128]{2,1,0:T(8,128)S(1)}, u32[]{:S(2)}, u32[]{:S(2)}) collective-permute-start(f32[4,16,128]{2,1,0:T(8,128)S(1)} %fusion.7), channel_id=1, source_target_pairs={{0,8},{4,12},{8,0},{12,4},{16,24},{20,28},{24,16},{28,20},{1,9},{5... | collective-permute-start | bytes 98312 | tf_op jit(solution)/shard_map/ppermute | solution.py:46
  53.5 1.4 %collective-permute-done.16 = f32[4,16,128]{2,1,0:T(8,128)S(1)} collective-permute-done((f32[4,16,128]{2,1,0:T(8,128)S(1)}, f32[4,16,128]{2,1,0:T(8,128)S(1)}, u32[]{:S(2)}, u32[]{:S(2)}) %collective-permute-start.16) | collective-permute-done | bytes 32800 | tf_op jit(solution)/shard_map/ppermute | solution.py:46
  57.5 4.0 %shard_map.70 = (f32[2,256,128]{2,1,0:T(8,128)S(1)}, f32[2,2,128,128]{3,2,1,0:T(8,128)S(1)}, f32[4,5,16,128]{3,2,1,0:T(8,128)S(1)}, f32[4,5,16,128]{3,2,1,0:T(8,...) custom-call(s32[7]{0:T(128)S(1)} %stack.82.scal, s32[8]{0:T(128)S(1)} %reshape_squeeze.4.offs, ...), custom_call_target="tpu_custom_call" | custom-call | flops 1610612736 | bytes 1048576 | tf_op jit(solution)/shard_map/pallas_call | solution.py:313
  62.4 4.6 %collective-permute-start.20 = (f32[2,128,128]{2,1,0:T(8,128)S(1)}, f32[2,128,128]{2,1,0:T(8,128)S(1)}, u32[]{:S(2)}, u32[]{:S(2)}) collective-permute-start(f32[2,128,128]{2,1,0:T(8,128)S(1)} %get-tuple-element.47), channel_id=1, source_target_pairs={{0,1},{1,0},{2,3},{3,2},{4,5},{5,4},{6,7},{7,6},{8,9},{9,8},{10,11... | collective-permute-start | bytes 393224 | tf_op jit(solution)/shard_map/ppermute | solution.py:42
  67.0 2.6 %collective-permute-start.26 = (f32[5,16,128]{2,1,0:T(8,128)S(1)}, f32[5,16,128]{2,1,0:T(8,128)S(1)}, u32[]{:S(2)}, u32[]{:S(2)}) collective-permute-start(f32[5,16,128]{2,1,0:T(8,128)S(1)} %get-tuple-element.58), channel_id=1, source_target_pairs={{0,24},{4,28},{8,16},{12,20},{16,8},{20,12},{24,0},{28,4},{1,25},{... | collective-permute-start | bytes 122888 | tf_op jit(solution)/shard_map/ppermute | solution.py:46
  72.0 1.6 %collective-permute-done.25 = f32[5,16,128]{2,1,0:T(8,128)S(1)} collective-permute-done((f32[5,16,128]{2,1,0:T(8,128)S(1)}, f32[5,16,128]{2,1,0:T(8,128)S(1)}, u32[]{:S(2)}, u32[]{:S(2)}) %collective-permute-start.25) | collective-permute-done | bytes 40992 | tf_op jit(solution)/shard_map/ppermute | solution.py:46
  73.7 1.5 %collective-permute-start.29 = (f32[5,16,128]{2,1,0:T(8,128)S(1)}, f32[5,16,128]{2,1,0:T(8,128)S(1)}, u32[]{:S(2)}, u32[]{:S(2)}) collective-permute-start(f32[5,16,128]{2,1,0:T(8,128)S(1)} %fusion.1), channel_id=1, source_target_pairs={{0,3},{1,2},{2,1},{3,0},{4,7},{5,6},{6,5},{7,4},{8,11},{9,10},{10,... | collective-permute-start | bytes 122888 | tf_op jit(solution)/shard_map/ppermute | solution.py:46
  75.2 2.9 %collective-permute-start.27 = (f32[5,16,128]{2,1,0:T(8,128)S(1)}, f32[5,16,128]{2,1,0:T(8,128)S(1)}, u32[]{:S(2)}, u32[]{:S(2)}) collective-permute-start(f32[5,16,128]{2,1,0:T(8,128)S(1)} %fusion.1), channel_id=1, source_target_pairs={{0,1},{1,0},{2,3},{3,2},{4,5},{5,4},{6,7},{7,6},{8,9},{9,8},{10,11... | collective-permute-start | bytes 122888 | tf_op jit(solution)/shard_map/ppermute | solution.py:46
  80.6 5.8 %collective-permute-start.32 = (f32[4,16,128]{2,1,0:T(8,128)S(1)}, f32[4,16,128]{2,1,0:T(8,128)S(1)}, u32[]{:S(2)}, u32[]{:S(2)}) collective-permute-start(f32[4,16,128]{2,1,0:T(8,128)S(1)} %fusion.5), channel_id=1, source_target_pairs={{0,24},{4,28},{8,16},{12,20},{16,8},{20,12},{24,0},{28,4},{1,25},{... | collective-permute-start | bytes 98312 | tf_op jit(solution)/shard_map/ppermute | solution.py:46
  87.4 1.5 %collective-permute-start.30 = (f32[4,16,128]{2,1,0:T(8,128)S(1)}, f32[4,16,128]{2,1,0:T(8,128)S(1)}, u32[]{:S(2)}, u32[]{:S(2)}) collective-permute-start(f32[4,16,128]{2,1,0:T(8,128)S(1)} %fusion.5), channel_id=1, source_target_pairs={{0,8},{4,12},{8,0},{12,4},{16,24},{20,28},{24,16},{28,20},{1,9},{5... | collective-permute-start | bytes 98312 | tf_op jit(solution)/shard_map/ppermute | solution.py:46
  88.9 1.5 %collective-permute-done.31 = f32[4,16,128]{2,1,0:T(8,128)S(1)} collective-permute-done((f32[4,16,128]{2,1,0:T(8,128)S(1)}, f32[4,16,128]{2,1,0:T(8,128)S(1)}, u32[]{:S(2)}, u32[]{:S(2)}) %collective-permute-start.31) | collective-permute-done | bytes 32800 | tf_op jit(solution)/shard_map/ppermute | solution.py:46
  92.8 1.4 %shard_map.73 = (f32[2,128,128]{2,1,0:T(8,128)}, f32[2,2,128,128]{3,2,1,0:T(8,128)}) custom-call(s32[7]{0:T(128)S(1)} %stack.82.scal, f32[2,2,256,128]{3,2,1,0:T(8,128)S(1)} %get-tuple-element.28.old_ref, f32[2,256,128]{2,1,0:T(8,128)S(1)} %shard_map.71.scale_ref, f32[2,128,128]{2,1,0:T(8,128)S(1)} %get-tuple-element.35.middle_ref, ...), custom_call_target="tpu_custom_call" | custom-call | bytes 1048576 | tf_op jit(solution)/shard_map/pallas_call | solution.py:313
  (118 shorter events, 24.2 us)
Async XLA Ops:
  2.4 5.0 %collective-permute-start.1 = (f32[136,128]{1,0:T(8,128)S(1)}, f32[136,128]{1,0:T(8,128)S(1)}, u32[]{:S(2)}, u32[]{:S(2)}) collective-permute-start(f32[136,128]{1,0:T(8,128)S(1)} %get-tuple-element.68), channel_id=1, source_target_pairs={{4,8},{8,4},{12,16},{16,12},{20,24},{24,20},{5,9},{9,5},{13,17},{1... | collective-permute-start | bytes 208904 | tf_op jit(solution)/shard_map/ppermute | solution.py:42
  3.1 5.3 %collective-permute-start = (f32[136,128]{1,0:T(8,128)S(1)}, f32[136,128]{1,0:T(8,128)S(1)}, u32[]{:S(2)}, u32[]{:S(2)}) collective-permute-start(f32[136,128]{1,0:T(8,128)S(1)} %get-tuple-element.69), channel_id=1, source_target_pairs={{0,4},{4,0},{8,12},{12,8},{16,20},{20,16},{24,28},{28,24},{1,5},{5... | collective-permute-start | bytes 208904 | tf_op jit(solution)/shard_map/ppermute | solution.py:42
  9.8 6.5 %collective-permute-start.2 = (f32[264,128]{1,0:T(8,128)S(1)}, f32[264,128]{1,0:T(8,128)S(1)}, u32[]{:S(2)}, u32[]{:S(2)}) collective-permute-start(f32[264,128]{1,0:T(8,128)S(1)} %concatenate.32), channel_id=1, source_target_pairs={{0,1},{1,0},{2,3},{3,2},{4,5},{5,4},{6,7},{7,6},{8,9},{9,8},{10,11... | collective-permute-start | bytes 405512 | tf_op jit(solution)/shard_map/ppermute | solution.py:42
  11.5 4.8 %collective-permute-start.3 = (f32[264,128]{1,0:T(8,128)S(1)}, f32[264,128]{1,0:T(8,128)S(1)}, u32[]{:S(2)}, u32[]{:S(2)}) collective-permute-start(f32[264,128]{1,0:T(8,128)S(1)} %concatenate.34), channel_id=1, source_target_pairs={{1,2},{2,1},{5,6},{6,5},{9,10},{10,9},{13,14},{14,13},{17,18},{18,... | collective-permute-start | bytes 405512 | tf_op jit(solution)/shard_map/ppermute | solution.py:42
  20.8 5.6 %collective-permute-start.4 = (f32[4,5,16,128]{3,2,1,0:T(8,128)S(1)}, f32[4,5,16,128]{3,2,1,0:T(8,128)S(1)}, u32[]{:S(2)}, u32[]{:S(2)}) collective-permute-start(f32[4,5,16,128]{3,2,1,0:T(8,128)S(1)} %get-tuple-element.23), channel_id=1, source_target_pairs={{0,4},{4,0},{8,12},{12,8},{16,20},{20,16},{24,28},{28,24},{1,5},{5... | collective-permute-start | bytes 491528 | tf_op jit(solution)/shard_map/ppermute | solution.py:42
  21.0 13.3 %collective-permute-start.5 = (f32[2,2,128,128]{3,2,1,0:T(8,128)S(1)}, f32[2,2,128,128]{3,2,1,0:T(8,128)S(1)}, u32[]{:S(2)}, u32[]{:S(2)}) collective-permute-start(f32[2,2,128,128]{3,2,1,0:T(8,128)S(1)} %get-tuple-element.42), channel_id=1, source_target_pairs={{0,1},{1,0},{2,3},{3,2},{4,5},{5,4},{6,7},{7,6},{8,9},{9,8},{10,11... | collective-permute-start | bytes 786440 | tf_op jit(solution)/shard_map/ppermute | solution.py:42
  25.7 8.6 %collective-permute-start.6 = (f32[2,2,128,128]{3,2,1,0:T(8,128)S(1)}, f32[2,2,128,128]{3,2,1,0:T(8,128)S(1)}, u32[]{:S(2)}, u32[]{:S(2)}) collective-permute-start(f32[2,2,128,128]{3,2,1,0:T(8,128)S(1)} %get-tuple-element.43), channel_id=1, source_target_pairs={{1,2},{2,1},{5,6},{6,5},{9,10},{10,9},{13,14},{14,13},{17,18},{18,... | collective-permute-start | bytes 786440 | tf_op jit(solution)/shard_map/ppermute | solution.py:42
  26.4 5.2 %collective-permute-start.11 = (f32[5,16,128]{2,1,0:T(8,128)S(1)}, f32[5,16,128]{2,1,0:T(8,128)S(1)}, u32[]{:S(2)}, u32[]{:S(2)}) collective-permute-start(f32[5,16,128]{2,1,0:T(8,128)S(1)} %get-tuple-element.61), channel_id=1, source_target_pairs={{0,24},{4,28},{8,16},{12,20},{16,8},{20,12},{24,0},{28,4},{1,25},{... | collective-permute-start | bytes 122888 | tf_op jit(solution)/shard_map/ppermute | solution.py:46
  29.3 4.0 %collective-permute-start.10 = (f32[5,16,128]{2,1,0:T(8,128)S(1)}, f32[5,16,128]{2,1,0:T(8,128)S(1)}, u32[]{:S(2)}, u32[]{:S(2)}) collective-permute-start(f32[5,16,128]{2,1,0:T(8,128)S(1)} %get-tuple-element.62), channel_id=1, source_target_pairs={{0,16},{4,20},{8,24},{12,28},{16,0},{20,4},{24,8},{28,12},{1,17},{... | collective-permute-start | bytes 122888 | tf_op jit(solution)/shard_map/ppermute | solution.py:46
  34.6 5.9 %collective-permute-start.14 = (f32[5,16,128]{2,1,0:T(8,128)S(1)}, f32[5,16,128]{2,1,0:T(8,128)S(1)}, u32[]{:S(2)}, u32[]{:S(2)}) collective-permute-start(f32[5,16,128]{2,1,0:T(8,128)S(1)} %fusion.3), channel_id=1, source_target_pairs={{0,3},{1,2},{2,1},{3,0},{4,7},{5,6},{6,5},{7,4},{8,11},{9,10},{10,... | collective-permute-start | bytes 122888 | tf_op jit(solution)/shard_map/ppermute | solution.py:46
  37.7 5.3 %collective-permute-start.13 = (f32[5,16,128]{2,1,0:T(8,128)S(1)}, f32[5,16,128]{2,1,0:T(8,128)S(1)}, u32[]{:S(2)}, u32[]{:S(2)}) collective-permute-start(f32[5,16,128]{2,1,0:T(8,128)S(1)} %fusion.3), channel_id=1, source_target_pairs={{0,2},{1,3},{2,0},{3,1},{4,6},{5,7},{6,4},{7,5},{8,10},{9,11},{10,... | collective-permute-start | bytes 122888 | tf_op jit(solution)/shard_map/ppermute | solution.py:46
  39.5 4.0 %collective-permute-start.12 = (f32[5,16,128]{2,1,0:T(8,128)S(1)}, f32[5,16,128]{2,1,0:T(8,128)S(1)}, u32[]{:S(2)}, u32[]{:S(2)}) collective-permute-start(f32[5,16,128]{2,1,0:T(8,128)S(1)} %fusion.3), channel_id=1, source_target_pairs={{0,1},{1,0},{2,3},{3,2},{4,5},{5,4},{6,7},{7,6},{8,9},{9,8},{10,11... | collective-permute-start | bytes 122888 | tf_op jit(solution)/shard_map/ppermute | solution.py:46
  39.5 4.1 %collective-permute-start.7 = (f32[2,2,128,128]{3,2,1,0:T(8,128)S(1)}, f32[2,2,128,128]{3,2,1,0:T(8,128)S(1)}, u32[]{:S(2)}, u32[]{:S(2)}) collective-permute-start(f32[2,2,128,128]{3,2,1,0:T(8,128)S(1)} %pad_maximum_fusion.1), channel_id=1, source_target_pairs={{0,4},{4,0},{8,12},{12,8},{16,20},{20,16},{24,28},{28,24},{1,5},{5... | collective-permute-start | bytes 786440 | tf_op jit(solution)/shard_map/ppermute | solution.py:42
  39.5 4.1 %collective-permute-start.8 = (f32[2,2,128,128]{3,2,1,0:T(8,128)S(1)}, f32[2,2,128,128]{3,2,1,0:T(8,128)S(1)}, u32[]{:S(2)}, u32[]{:S(2)}) collective-permute-start(f32[2,2,128,128]{3,2,1,0:T(8,128)S(1)} %pad_maximum_fusion.2), channel_id=1, source_target_pairs={{4,8},{8,4},{12,16},{16,12},{20,24},{24,20},{5,9},{9,5},{13,17},{1... | collective-permute-start | bytes 786440 | tf_op jit(solution)/shard_map/ppermute | solution.py:42
  43.6 9.8 %collective-permute-start.17 = (f32[4,16,128]{2,1,0:T(8,128)S(1)}, f32[4,16,128]{2,1,0:T(8,128)S(1)}, u32[]{:S(2)}, u32[]{:S(2)}) collective-permute-start(f32[4,16,128]{2,1,0:T(8,128)S(1)} %fusion.7), channel_id=1, source_target_pairs={{0,24},{4,28},{8,16},{12,20},{16,8},{20,12},{24,0},{28,4},{1,25},{... | collective-permute-start | bytes 98312 | tf_op jit(solution)/shard_map/ppermute | solution.py:46
  50.7 4.1 %collective-permute-start.16 = (f32[4,16,128]{2,1,0:T(8,128)S(1)}, f32[4,16,128]{2,1,0:T(8,128)S(1)}, u32[]{:S(2)}, u32[]{:S(2)}) collective-permute-start(f32[4,16,128]{2,1,0:T(8,128)S(1)} %fusion.7), channel_id=1, source_target_pairs={{0,16},{4,20},{8,24},{12,28},{16,0},{20,4},{24,8},{28,12},{1,17},{... | collective-permute-start | bytes 98312 | tf_op jit(solution)/shard_map/ppermute | solution.py:46
  61.4 5.5 %collective-permute-start.19 = (f32[4,5,16,128]{3,2,1,0:T(8,128)S(1)}, f32[4,5,16,128]{3,2,1,0:T(8,128)S(1)}, u32[]{:S(2)}, u32[]{:S(2)}) collective-permute-start(f32[4,5,16,128]{3,2,1,0:T(8,128)S(1)} %get-tuple-element.30), channel_id=1, source_target_pairs={{0,4},{4,0},{8,12},{12,8},{16,20},{20,16},{24,28},{28,24},{1,5},{5... | collective-permute-start | bytes 491528 | tf_op jit(solution)/shard_map/ppermute | solution.py:42
  61.7 12.0 %collective-permute-start.21 = (f32[2,128,128]{2,1,0:T(8,128)S(1)}, f32[2,128,128]{2,1,0:T(8,128)S(1)}, u32[]{:S(2)}, u32[]{:S(2)}) collective-permute-start(f32[2,128,128]{2,1,0:T(8,128)S(1)} %get-tuple-element.46), channel_id=1, source_target_pairs={{1,2},{2,1},{5,6},{6,5},{9,10},{10,9},{13,14},{14,13},{17,18},{18,... | collective-permute-start | bytes 393224 | tf_op jit(solution)/shard_map/ppermute | solution.py:42
  62.4 11.3 %collective-permute-start.20 = (f32[2,128,128]{2,1,0:T(8,128)S(1)}, f32[2,128,128]{2,1,0:T(8,128)S(1)}, u32[]{:S(2)}, u32[]{:S(2)}) collective-permute-start(f32[2,128,128]{2,1,0:T(8,128)S(1)} %get-tuple-element.47), channel_id=1, source_target_pairs={{0,1},{1,0},{2,3},{3,2},{4,5},{5,4},{6,7},{7,6},{8,9},{9,8},{10,11... | collective-permute-start | bytes 393224 | tf_op jit(solution)/shard_map/ppermute | solution.py:42
  67.0 5.0 %collective-permute-start.26 = (f32[5,16,128]{2,1,0:T(8,128)S(1)}, f32[5,16,128]{2,1,0:T(8,128)S(1)}, u32[]{:S(2)}, u32[]{:S(2)}) collective-permute-start(f32[5,16,128]{2,1,0:T(8,128)S(1)} %get-tuple-element.58), channel_id=1, source_target_pairs={{0,24},{4,28},{8,16},{12,20},{16,8},{20,12},{24,0},{28,4},{1,25},{... | collective-permute-start | bytes 122888 | tf_op jit(solution)/shard_map/ppermute | solution.py:46
  73.7 5.9 %collective-permute-start.29 = (f32[5,16,128]{2,1,0:T(8,128)S(1)}, f32[5,16,128]{2,1,0:T(8,128)S(1)}, u32[]{:S(2)}, u32[]{:S(2)}) collective-permute-start(f32[5,16,128]{2,1,0:T(8,128)S(1)} %fusion.1), channel_id=1, source_target_pairs={{0,3},{1,2},{2,1},{3,0},{4,7},{5,6},{6,5},{7,4},{8,11},{9,10},{10,... | collective-permute-start | bytes 122888 | tf_op jit(solution)/shard_map/ppermute | solution.py:46
  75.2 5.3 %collective-permute-start.28 = (f32[5,16,128]{2,1,0:T(8,128)S(1)}, f32[5,16,128]{2,1,0:T(8,128)S(1)}, u32[]{:S(2)}, u32[]{:S(2)}) collective-permute-start(f32[5,16,128]{2,1,0:T(8,128)S(1)} %fusion.1), channel_id=1, source_target_pairs={{0,2},{1,3},{2,0},{3,1},{4,6},{5,7},{6,4},{7,5},{8,10},{9,11},{10,... | collective-permute-start | bytes 122888 | tf_op jit(solution)/shard_map/ppermute | solution.py:46
  75.2 5.3 %collective-permute-start.27 = (f32[5,16,128]{2,1,0:T(8,128)S(1)}, f32[5,16,128]{2,1,0:T(8,128)S(1)}, u32[]{:S(2)}, u32[]{:S(2)}) collective-permute-start(f32[5,16,128]{2,1,0:T(8,128)S(1)} %fusion.1), channel_id=1, source_target_pairs={{0,1},{1,0},{2,3},{3,2},{4,5},{5,4},{6,7},{7,6},{8,9},{9,8},{10,11... | collective-permute-start | bytes 122888 | tf_op jit(solution)/shard_map/ppermute | solution.py:46
  80.6 8.3 %collective-permute-start.32 = (f32[4,16,128]{2,1,0:T(8,128)S(1)}, f32[4,16,128]{2,1,0:T(8,128)S(1)}, u32[]{:S(2)}, u32[]{:S(2)}) collective-permute-start(f32[4,16,128]{2,1,0:T(8,128)S(1)} %fusion.5), channel_id=1, source_target_pairs={{0,24},{4,28},{8,16},{12,20},{16,8},{20,12},{24,0},{28,4},{1,25},{... | collective-permute-start | bytes 98312 | tf_op jit(solution)/shard_map/ppermute | solution.py:46
  (15 other events, 53.0 us)

commit v2 on v1

--- a/solution.py
+++ b/solution.py
@@ -193,14 +193,19 @@
     if len(outs) == 1:
         give_quadrants(scal, grad, outs)
     else:
-        give_rims(scal, grad, outs)
+        give_rims(scal, grad, outs, send_out)
     chips, planes, rows, _ = keep_out.shape
     for slot in range(chips):
         chunk = scal[2] ^ slot
         for which, ref in ((scal[0], keep_out), (1 - scal[0], send_out)):
             start = pl.multiple_of((which * chips + chunk) * rows, rows)
             for plane in range(planes):
-                ref[slot, plane] = sums[plane, pl.ds(start, rows), :]
+                piece = sums[plane, pl.ds(start, rows), :]
+                if len(ref.shape) == 2:
+                    at = (slot * planes + plane) * rows
+                    ref[at : at + rows, :] = piece
+                else:
+                    ref[slot, plane] = piece
 
 
 def give_quadrants(scal, grad, outs):
@@ -213,37 +218,64 @@
                 outs[0][b, a, plane] = grad[plane, side, pl.ds(row, extent), :]
 
 
-def give_rims(scal, grad, outs):
-    extent = grad.shape[-1]
+def give_rims(scal, grad, outs, send_out):
+    planes, sides, size, extent = grad.shape
+    halo = extent // 2
+    base = send_out.shape[0] - planes * sides * halo
+    outer = (pl.multiple_of(jnp.where(scal[0] == 1, 0, size - halo), halo), pl.multiple_of(jnp.where(scal[0] == 1, size - halo, 0), halo))
+    for plane in range(planes):
+        for side in range(sides):
+            at = (plane * sides + side) * halo
+            outs[0][plane, side] = grad[plane, side, halo : size - halo, :]
+            send_out[base + at : base + at + halo, :] = grad[plane, side, pl.ds(outer[0], halo), :]
+            outs[1][at : at + halo, :] = grad[plane, side, pl.ds(outer[1], halo), :]
+
+
+def middle_kernel(scal, own_ref, near_ref, far_ref, total_ref, middle_ref, near_out, far_out):
+    planes, sides, extent, _ = own_ref.shape
+    halo = extent // 2
+    base = near_ref.shape[0] - planes * sides * halo
+    head = total_ref.shape[0]
+    odd_row, odd_col = scal[0] == 1, scal[1] == 1
+    lane = lax.broadcasted_iota(jnp.int32, (extent, extent), 1)
+    rims = []
+    for plane in range(planes):
+        rows = []
+        for side in range(sides):
+            at = (plane * sides + side) * halo
+            near, far = near_ref[base + at : base + at + halo, :], far_ref[at : at + halo, :]
+            other = jnp.concatenate([jnp.where(odd_row, near, far), jnp.where(odd_row, far, near)], axis=0)
+            rows.append(own_ref[plane, side] + other)
+        turned = [pltpu.roll(part, halo, 1) for part in rows]
+        middle_ref[plane] = jnp.where(lane < halo, turned[0], turned[1])
+        rims.append((rows[0], turned[1]) if plane == 0 else (turned[0], rows[1]))
+    left, right = (jnp.where(lane < halo, rims[0][side], rims[1][side]) for side in range(sides))
+    for ref, rim in ((near_out, jnp.where(odd_col, left, right)), (far_out, jnp.where(odd_col, right, left))):
+        ref[:head, :] = total_ref[...]
+        ref[head:, :] = rim
+
+
+def object_kernel(scal, old_ref, scale_ref, middle_ref, near_ref, far_ref, object_ref):
+    extent = old_ref.shape[-1]
     halo = extent // 2
     lane = lax.broadcasted_iota(jnp.int32, (extent, extent), 1)
-    for plane in range(grad.shape[0]):
-        upper = [grad[plane, side, 0:extent, :] for side in range(2)]
-        lower = [grad[plane, side, extent : 2 * extent, :] for side in range(2)]
-        for start, rows in ((0, upper), (extent, lower)):
-            outs[0][plane, start : start + extent, :] = jnp.where(
-                lane < halo, pltpu.roll(rows[0], halo, 1), pltpu.roll(rows[1], halo, 1)
-            )
-        left = jnp.where(lane < halo, upper[0], pltpu.roll(lower[0], halo, 1))
-        right = jnp.where(lane < halo, pltpu.roll(upper[1], halo, 1), lower[1])
-        outs[1][1 - scal[1], plane] = left
-        outs[1][scal[1], plane] = right
-
-
-def rim_kernel(scal, own_ref, near_ref, far_ref, middle_ref, near_out, far_out):
-    _, size, extent = own_ref.shape
-    halo = extent // 2
-    lane = lax.broadcasted_iota(jnp.int32, (extent, extent), 1)
+    middle = pl.ds(halo, extent)
+
+    def tile_of(sides):
+        return jnp.where(lane < halo, pltpu.roll(sides[0], halo, 1), pltpu.roll(sides[1], halo, 1))
+
+    scale = tile_of([scale_ref[side, middle] for side in range(2)])
     odd = scal[1] == 1
-    for plane in range(own_ref.shape[0]):
-        near, far = near_ref[plane], far_ref[plane]
-        from_left, from_right = jnp.where(odd, near, far), jnp.where(odd, far, near)
-        upper = own_ref[plane, 0:extent] + jnp.where(lane < halo, from_left, pltpu.roll(from_right, halo, 1))
-        lower = own_ref[plane, extent:size] + jnp.where(lane < halo, pltpu.roll(from_left, halo, 1), from_right)
-        middle_ref[plane, 0:halo] = upper[halo:]
-        middle_ref[plane, halo:extent] = lower[:halo]
-        near_out[plane] = jnp.where(scal[0] == 1, upper[:halo], lower[halo:])
-        far_out[plane] = jnp.where(scal[0] == 1, lower[halo:], upper[:halo])
+    near, far = (ref[ref.shape[0] - extent :, :] for ref in (near_ref, far_ref))
+    left = jnp.where(scal[5] > 0, 0.0, jnp.where(odd, near, far))
+    right = jnp.where(scal[6] < 2 * extent, 0.0, jnp.where(odd, far, near))
+    for part in range(2):
+        if part == 0:
+            beside = jnp.where(lane < halo, left, pltpu.roll(right, halo, 1))
+        else:
+            beside = jnp.where(lane < halo, pltpu.roll(left, halo, 1), right)
+        old = tile_of([old_ref[part, side, middle] for side in range(2)])
+        object_ref[part] = old - scale * (middle_ref[part] + beside)
 
 
 def first_kernel(
@@ -281,23 +313,8 @@
     terms_body(scal, offs, canvas_ref, probe_ref, measured_ref, table_ref, outs, keep_out, send_out, grad, sums)
 
 
-def last_kernel(scal, old_ref, scale_ref, middle_ref, near_ref, far_ref, own_ref, other_ref, object_ref, probe_ref):
-    half = old_ref.shape[-1]
-    halo = half // 2
+def last_kernel(scal, own_ref, other_ref, probe_ref):
     place_probe(scal, own_ref, other_ref, probe_ref)
-    lane = lax.broadcasted_iota(jnp.int32, (half, half), 1)
-    middle = pl.ds(halo, half)
-
-    def tile_of(sides):
-        return jnp.where(lane < halo, pltpu.roll(sides[0], halo, 1), pltpu.roll(sides[1], halo, 1))
-
-    scale = tile_of([scale_ref[side, middle] for side in range(2)])
-    odd = scal[0] == 1
-    for part in range(2):
-        near, far = near_ref[part], far_ref[part]
-        from_rows = jnp.concatenate([jnp.where(odd, near, far), jnp.where(odd, far, near)], axis=0)
-        old = tile_of([old_ref[part, side, middle] for side in range(2)])
-        object_ref[part] = old - scale * (middle_ref[part] + from_rows)
 
 
 SMEM = pl.BlockSpec(memory_space=pltpu.SMEM)
@@ -359,15 +376,18 @@
     return tree_sum([both[0]] + [flipped(both[t], "sy", 2 * t) for t in range(1, both.shape[0])])
 
 
-def probe_fresh(total, chunk):
-    planes = chunk.shape[0]
-    total = tree_sum([total] + [flipped(total, "sx", t) for t in range(1, lax.axis_size("sx"))])
+def probe_fresh(parts, chunk):
+    planes, rows, lanes = chunk.shape
+    total = tree_sum(parts).reshape(planes + 1, rows, lanes)
     return chunk - PROBE_STEP * total[:planes] / (total[planes:] + REGULAR)
 
 
+def across(total, start):
+    return [total] + [flipped(total, "sx", t) for t in range(start, lax.axis_size("sx"))]
+
+
 def probe_spread(fresh, chips):
-    own = jnp.stack([fresh] + [flipped(fresh, "sy", 2 * t) for t in range(1, chips)])
-    return own, swapped(own, "sy", False)
+    return jnp.stack([fresh] + [flipped(fresh, "sy", 2 * t) for t in range(1, chips)])
 
 
 def per_device(object_tile, probe_modes, scan_offsets, intensities):
@@ -383,9 +403,11 @@
     scal = head_scalars(size, halo)
     offsets = scan_offsets[0, 0]
     offs = offsets.reshape(-1)
-    probe_outs = (f32(chips, planes + 1, rows, extent),) * 2 + (f32(2, 2, size, tile),)
+    kept = (chips, planes + 1, rows, extent)
+    count = chips * (planes + 1) * rows
+    rim_rows = 2 * 2 * halo
     quadrants = (f32(2, 2, 2, tile, tile),)
-    rims = (f32(2, size, tile), f32(2, 2, tile, tile))
+    rims = (f32(2, 2, tile, tile), f32(rim_rows, tile))
     scratch = ((2, 2, size, tile), (planes + 1, extent, extent))
     work = 2 * 3 * offsets.shape[0] * 4 * (2 * extent) ** 3
 
@@ -400,7 +422,8 @@
     probe = probe_modes
     for iteration in range(ITERS):
         final = iteration == ITERS - 1
-        outs = (rims if final else quadrants) + probe_outs
+        sent = (count + rim_rows, extent) if final else kept
+        outs = (rims if final else quadrants) + (f32(*kept), f32(*sent), f32(2, 2, size, tile))
         if iteration == 0:
             operands = (scal, offs, object_tile, *halos, probe, measured, table)
             *given, keep, send, canvas = kernel_call(first_kernel, outs, operands, scratch, flops=work)
@@ -408,29 +431,40 @@
             operands = (scal, offs, canvas, scale, near, far, own, other, measured, table)
             outs = outs + (f32(*probe.shape),)
             *given, keep, send, canvas, probe = kernel_call(next_kernel, outs, operands, scratch, flops=work)
-        both = keep + swapped(send, "sy", False)
+        received = swapped(send, "sy", False)
+        both = keep + received.reshape(-1, extent)[:count].reshape(kept)
         scale = light(probe, after(corners, both))
         if not final:
             (grad,) = given
             side_a = grad[0] + swapped(grad[0], "sx", False)
             side_b = grad[1] + swapped(grad[1], "sx", True)
             near, far = jnp.stack([side_a[0], side_b[0]]), jnp.stack([side_a[1], side_b[1]])
-            total = after(chip_sum(both), near, far, scale)
             near = near + swapped(near, "sy", False)
             far = far + swapped(far, "sy", True)
-            chunk = after(probe_fresh(total, chunk), near, far)
+            total = after(chip_sum(both), near, scale)
+            chunk = after(probe_fresh(across(total, 1), chunk), near, far)
         else:
-            own_columns, side = given
-            near, far = swapped(side[0], "sx", False), swapped(side[1], "sx", True)
-            total = after(chip_sum(both), near, far, scale)
+            own_rows, far = given
+            far = swapped(far, "sy", True)
+            total = after(chip_sum(both), far, scale).reshape(-1, extent)
+            message = f32(total.shape[0] + tile, tile)
             middle, near, far = kernel_call(
-                rim_kernel, (f32(2, tile, tile),) + (f32(2, halo, tile),) * 2, (scal, own_columns, near, far), scalars=1
+                middle_kernel, (f32(2, tile, tile), message, message), (scal, own_rows, received, far, total), scalars=1
             )
-            near, far = swapped(near, "sy", False), swapped(far, "sy", True)
-            chunk = after(probe_fresh(total, chunk), near, far)
-        own, other = probe_spread(chunk, chips)
-    outs = (f32(2, tile, tile), f32(*probe.shape))
-    return kernel_call(last_kernel, outs, (scal, canvas, scale, middle, near, far, own, other), scalars=1)
+            near = flipped(near, "sx", 1)
+            head = total.shape[0]
+            if lax.axis_size("sx") == 4:
+                far = flipped(far, "sx", 3)
+                parts = [total, near[:head], flipped(total, "sx", 2), far[:head]]
+            else:
+                far = swapped(far, "sx", True)
+                parts = across(total, 2)
+                parts.insert(1, near[:head])
+            chunk = probe_fresh(parts, chunk)
+            outcome = kernel_call(object_kernel, f32(2, tile, tile), (scal, canvas, scale, middle, near, far), scalars=1)
+        own = probe_spread(chunk, chips)
+        other = swapped(after(own, outcome) if final else own, "sy", False)
+    return outcome, kernel_call(last_kernel, f32(*probe.shape), (scal, own, other), scalars=1)
 
 
 def solution(mesh):

time: 94.6 us -> 89.2 us (0.943)
  starting transfers between devices: 54.8 us -> 42.9 us
  waiting for transfers between devices: 21.1 us -> 26.6 us
  Pallas kernels: 12.7 us -> 13.8 us
    ppermute x18, starting transfers between devices: 34.9 us -> 28.4 us  [flipped(): lax.ppermute(values, axis, [(i, i ^ bits) for i in range(lax.axis_size(ax...]
    ppermute x16 -> x13, starting transfers between devices: 19.9 us -> 14.6 us  [swapped(): return lax.ppermute(values, axis, pairs)]
    ppermute x18, waiting for transfers between devices: 13.8 us -> 17.6 us  [flipped(): lax.ppermute(values, axis, [(i, i ^ bits) for i in range(lax.axis_size(ax...]
    ppermute x16 -> x13, waiting for transfers between devices: 7.31 us -> 8.97 us  [swapped(): return lax.ppermute(values, axis, pairs)]
    pallas_call x6 -> x7, Pallas kernels: 12.7 us -> 13.8 us  [kernel_call(): pl.pallas_call(body, out_shape=outs, in_specs=[SMEM] * scalars + [VMEM] *...]
  transfers between devices with their start and end apart: 34 -> 31, of which waited for: 16 -> 19; matrix products, arithmetic and copies ran while one was open for 1% -> 1% of each run, Pallas kernels for 4% -> 5%
where the time goes in v2:
time: 89.2 us; the launch traced here: 88.9 us
  starting transfers between devices  42.9 us (48%)
  waiting for transfers between devices  26.6 us (30%)
  Pallas kernels  13.8 us (15%)
  local copies, waits for them, and re-layouts  2.83 us (3%)
  other arithmetic  1.66 us (2%)
  between operations  1.12 us (1%)
    ppermute x18, starting transfers between devices, flipped(): lax.ppermute(values, axis, [(i, i ^ bits) for i in range(lax.axis_size(ax...  28.4 us
    ppermute x18, waiting for transfers between devices, flipped(): lax.ppermute(values, axis, [(i, i ^ bits) for i in range(lax.axis_size(ax...  17.6 us
    ppermute x13, starting transfers between devices, swapped(): return lax.ppermute(values, axis, pairs)  14.6 us
    pallas_call x7, Pallas kernels, kernel_call(): pl.pallas_call(body, out_shape=outs, in_specs=[SMEM] * scalars + [VMEM] *...  13.8 us
    ppermute x13, waiting for transfers between devices, swapped(): return lax.ppermute(values, axis, pairs)  8.97 us
  transfers between devices with their start and end apart: 31, of which 19 were waited for; matrix products, arithmetic and copies ran while one was open for 1% of the time, Pallas kernels for 5%

profile of v2, /device:TPU:0, one launch (start us, length us, event | category | flops | bytes accessed | tf_op | source)
XLA Modules:
  0.0 88.9 jit_solution(3554001160542756928)
XLA Ops:
  3.1 4.4 %collective-permute-start = (f32[136,128]{1,0:T(8,128)S(1)}, f32[136,128]{1,0:T(8,128)S(1)}, u32[]{:S(2)}, u32[]{:S(2)}) collective-permute-start(f32[136,128]{1,0:T(8,128)S(1)} %get-tuple-element.67), channel_id=1, source_target_pairs={{0,4},{4,0},{8,12},{12,8},{16,20},{20,16},{24,28},{28,24},{1,5},{5... | collective-permute-start | bytes 208904 | tf_op jit(solution)/shard_map/ppermute | solution.py:42
  9.8 1.6 %collective-permute-start.2 = (f32[264,128]{1,0:T(8,128)S(1)}, f32[264,128]{1,0:T(8,128)S(1)}, u32[]{:S(2)}, u32[]{:S(2)}) collective-permute-start(f32[264,128]{1,0:T(8,128)S(1)} %concatenate.32), channel_id=1, source_target_pairs={{0,1},{1,0},{2,3},{3,2},{4,5},{5,4},{6,7},{7,6},{8,9},{9,8},{10,11... | collective-permute-start | bytes 405512 | tf_op jit(solution)/shard_map/ppermute | solution.py:42
  12.6 3.7 %collective-permute-done.2.cols_near = f32[264,128]{1,0:T(8,128)S(1)} collective-permute-done((f32[264,128]{1,0:T(8,128)S(1)}, f32[264,128]{1,0:T(8,128)S(1)}, u32[]{:S(2)}, u32[]{:S(2)}) %collective-permute-start.2) | collective-permute-done | bytes 135200 | tf_op jit(solution)/shard_map/ppermute | solution.py:42
  16.8 4.0 %shard_map.68 = (f32[2,2,2,128,128]{4,3,2,1,0:T(8,128)S(1)}, f32[4,5,16,128]{3,2,1,0:T(8,128)S(1)}, f32[4,5,16,128]{3,2,1,0:T(8,128)S(1)}, f32[2,2,256,128]{3,2,1,0:T(8,128)S(1)}) custom-call(s32[7]{0:T(128)S(1)} %stack.82.scal, s32[8]{0:T(128)S(1)} %reshape_squeeze.4.offs, f32[2,128,128]{2,1,0:T(8,128)S(1)} %copy-done, ...), custom_call_target="tpu_custom_call" | custom-call | flops 1610612736 | bytes 1048576 | tf_op jit(solution)/shard_map/pallas_call | solution.py:330
  21.0 4.7 %collective-permute-start.5 = (f32[2,2,128,128]{3,2,1,0:T(8,128)S(1)}, f32[2,2,128,128]{3,2,1,0:T(8,128)S(1)}, u32[]{:S(2)}, u32[]{:S(2)}) collective-permute-start(f32[2,2,128,128]{3,2,1,0:T(8,128)S(1)} %get-tuple-element.42), channel_id=1, source_target_pairs={{0,1},{1,0},{2,3},{3,2},{4,5},{5,4},{6,7},{7,6},{8,9},{9,8},{10,11... | collective-permute-start | bytes 786440 | tf_op jit(solution)/shard_map/ppermute | solution.py:42
  26.4 2.9 %collective-permute-start.11 = (f32[5,16,128]{2,1,0:T(8,128)S(1)}, f32[5,16,128]{2,1,0:T(8,128)S(1)}, u32[]{:S(2)}, u32[]{:S(2)}) collective-permute-start(f32[5,16,128]{2,1,0:T(8,128)S(1)} %get-tuple-element.59), channel_id=1, source_target_pairs={{0,24},{4,28},{8,16},{12,20},{16,8},{20,12},{24,0},{28,4},{1,25},{... | collective-permute-start | bytes 122888 | tf_op jit(solution)/shard_map/ppermute | solution.py:46
  30.3 1.3 %shard_map.69.scale_ref = f32[2,256,128]{2,1,0:T(8,128)S(1)} custom-call(s32[7]{0:T(128)S(1)} %stack.82.scal, s32[72]{0:T(128)S(1)} %select_n.114.corners, f32[2,2,128,128]{3,2,1,0:T(8,128)S(1)} %copy-done.1), custom_call_target="tpu_custom_call" | custom-call | flops 805306368 | bytes 1048576 | tf_op jit(solution)/shard_map/pallas_call | solution.py:330
  34.4 3.1 %collective-permute-start.14 = (f32[5,16,128]{2,1,0:T(8,128)S(1)}, f32[5,16,128]{2,1,0:T(8,128)S(1)}, u32[]{:S(2)}, u32[]{:S(2)}) collective-permute-start(f32[5,16,128]{2,1,0:T(8,128)S(1)} %fusion.4), channel_id=1, source_target_pairs={{0,3},{1,2},{2,1},{3,0},{4,7},{5,6},{6,5},{7,4},{8,11},{9,10},{10,... | collective-permute-start | bytes 122888 | tf_op jit(solution)/shard_map/ppermute | solution.py:46
  37.5 2.1 %collective-permute-start.13 = (f32[5,16,128]{2,1,0:T(8,128)S(1)}, f32[5,16,128]{2,1,0:T(8,128)S(1)}, u32[]{:S(2)}, u32[]{:S(2)}) collective-permute-start(f32[5,16,128]{2,1,0:T(8,128)S(1)} %fusion.4), channel_id=1, source_target_pairs={{0,2},{1,3},{2,0},{3,1},{4,6},{5,7},{6,4},{7,5},{8,10},{9,11},{10,... | collective-permute-start | bytes 122888 | tf_op jit(solution)/shard_map/ppermute | solution.py:46
  40.2 2.3 %collective-permute-done.13 = f32[5,16,128]{2,1,0:T(8,128)S(1)} collective-permute-done((f32[5,16,128]{2,1,0:T(8,128)S(1)}, f32[5,16,128]{2,1,0:T(8,128)S(1)}, u32[]{:S(2)}, u32[]{:S(2)}) %collective-permute-start.13) | collective-permute-done | bytes 40992 | tf_op jit(solution)/shard_map/ppermute | solution.py:46
  43.6 4.5 %collective-permute-start.17 = (f32[4,16,128]{2,1,0:T(8,128)S(1)}, f32[4,16,128]{2,1,0:T(8,128)S(1)}, u32[]{:S(2)}, u32[]{:S(2)}) collective-permute-start(f32[4,16,128]{2,1,0:T(8,128)S(1)} %fusion.6), channel_id=1, source_target_pairs={{0,24},{4,28},{8,16},{12,20},{16,8},{20,12},{24,0},{28,4},{1,25},{... | collective-permute-start | bytes 98312 | tf_op jit(solution)/shard_map/ppermute | solution.py:46
  48.6 1.3 %collective-permute-start.15 = (f32[4,16,128]{2,1,0:T(8,128)S(1)}, f32[4,16,128]{2,1,0:T(8,128)S(1)}, u32[]{:S(2)}, u32[]{:S(2)}) collective-permute-start(f32[4,16,128]{2,1,0:T(8,128)S(1)} %fusion.6), channel_id=1, source_target_pairs={{0,8},{4,12},{8,0},{12,4},{16,24},{20,28},{24,16},{28,20},{1,9},{5... | collective-permute-start | bytes 98312 | tf_op jit(solution)/shard_map/ppermute | solution.py:46
  50.0 2.0 %collective-permute-done.16 = f32[4,16,128]{2,1,0:T(8,128)S(1)} collective-permute-done((f32[4,16,128]{2,1,0:T(8,128)S(1)}, f32[4,16,128]{2,1,0:T(8,128)S(1)}, u32[]{:S(2)}, u32[]{:S(2)}) %collective-permute-start.16) | collective-permute-done | bytes 32800 | tf_op jit(solution)/shard_map/ppermute | solution.py:46
  52.6 1.3 %collective-permute-done.18.other_ref = f32[4,4,16,128]{3,2,1,0:T(8,128)S(1)} collective-permute-done((f32[4,4,16,128]{3,2,1,0:T(8,128)S(1)}, f32[4,4,16,128]{3,2,1,0:T(8,128)S(1)}, u32[]{:S(2)}, u32[]{:S(2)}) %collective-permute-start.18) | collective-permute-done | bytes 131104 | tf_op jit(solution)/shard_map/ppermute | solution.py:42
  53.9 3.8 %shard_map.70 = (f32[2,2,128,128]{3,2,1,0:T(8,128)S(1)}, f32[256,128]{1,0:T(8,128)S(1)}, f32[4,5,16,128]{3,2,1,0:T(8,128)S(1)}, f32[576,128]{1,0:T(8,128)S(1)}, ...) custom-call(s32[7]{0:T(128)S(1)} %stack.82.scal, s32[8]{0:T(128)S(1)} %reshape_squeeze.4.offs, ...), custom_call_target="tpu_custom_call" | custom-call | flops 1610612736 | bytes 1048576 | tf_op jit(solution)/shard_map/pallas_call | solution.py:330
  59.4 3.5 %collective-permute-start.23 = (f32[5,16,128]{2,1,0:T(8,128)S(1)}, f32[5,16,128]{2,1,0:T(8,128)S(1)}, u32[]{:S(2)}, u32[]{:S(2)}) collective-permute-start(f32[5,16,128]{2,1,0:T(8,128)S(1)} %get-tuple-element.56), channel_id=1, source_target_pairs={{0,24},{4,28},{8,16},{12,20},{16,8},{20,12},{24,0},{28,4},{1,25},{... | collective-permute-start | bytes 122888 | tf_op jit(solution)/shard_map/ppermute | solution.py:46
  64.2 1.3 %shard_map.71.scale_ref = f32[2,256,128]{2,1,0:T(8,128)S(1)} custom-call(s32[7]{0:T(128)S(1)} %stack.82.scal, s32[72]{0:T(128)S(1)} %select_n.114.corners, f32[2,2,128,128]{3,2,1,0:T(8,128)S(1)} %get-tuple-element.32.probe_ref), custom_call_target="tpu_custom_call" | custom-call | flops 805306368 | bytes 1048576 | tf_op jit(solution)/shard_map/pallas_call | solution.py:330
  68.7 1.7 %collective-permute-start.24 = (f32[208,128]{1,0:T(8,128)S(1)}, f32[208,128]{1,0:T(8,128)S(1)}, u32[]{:S(2)}, u32[]{:S(2)}) collective-permute-start(f32[208,128]{1,0:T(8,128)S(1)} %get-tuple-element.37), channel_id=1, source_target_pairs={{0,1},{1,0},{2,3},{3,2},{4,5},{5,4},{6,7},{7,6},{8,9},{9,8},{10,11... | collective-permute-start | bytes 319496 | tf_op jit(solution)/shard_map/ppermute | solution.py:46
  70.4 2.6 %collective-permute-start.25 = (f32[208,128]{1,0:T(8,128)S(1)}, f32[208,128]{1,0:T(8,128)S(1)}, u32[]{:S(2)}, u32[]{:S(2)}) collective-permute-start(f32[208,128]{1,0:T(8,128)S(1)} %get-tuple-element.38), channel_id=1, source_target_pairs={{0,3},{1,2},{2,1},{3,0},{4,7},{5,6},{6,5},{7,4},{8,11},{9,10},{10,... | collective-permute-start | bytes 319496 | tf_op jit(solution)/shard_map/ppermute | solution.py:46
  73.0 6.5 %collective-permute-done.26 = f32[80,128]{1,0:T(8,128)S(1)} collective-permute-done((f32[80,128]{1,0:T(8,128)S(1)}, f32[80,128]{1,0:T(8,128)S(1)}, u32[]{:S(2)}, u32[]{:S(2)}) %collective-permute-start.26) | collective-permute-done | bytes 40992 | tf_op jit(solution)/shard_map/ppermute | solution.py:46
  79.6 2.2 %collective-permute-start.29 = (f32[4,16,128]{2,1,0:T(8,128)S(1)}, f32[4,16,128]{2,1,0:T(8,128)S(1)}, u32[]{:S(2)}, u32[]{:S(2)}) collective-permute-start(f32[4,16,128]{2,1,0:T(8,128)S(1)} %divide_subtract_fusion), channel_id=1, source_target_pairs={{0,24},{4,28},{8,16},{12,20},{16,8},{20,12},{24,0},{28,4},{1,25},{... | collective-permute-start | bytes 98312 | tf_op jit(solution)/shard_map/ppermute | solution.py:46
  83.1 1.4 %shard_map.73 = f32[2,128,128]{2,1,0:T(8,128)} custom-call(s32[7]{0:T(128)S(1)} %stack.82.scal, f32[2,2,256,128]{3,2,1,0:T(8,128)S(1)} %get-tuple-element.28.old_ref, f32[2,256,128]{2,1,0:T(8,128)S(1)} %shard_map.71.scale_ref, f32[2,128,128]{2,1,0:T(8,128)S(1)} %get-tuple-element.36.middle_ref, f32[208,128]{1,0:T(8,128)S(1)} %collective-permute-done.24.near_ref, ...), custom_call_target="tpu_custom_call" | custom-call | bytes 1048576 | tf_op jit(solution)/shard_map/pallas_call | solution.py:330
  86.3 1.3 %collective-permute-done.30.other_ref = f32[4,4,16,128]{3,2,1,0:T(8,128)S(1)} collective-permute-done((f32[4,4,16,128]{3,2,1,0:T(8,128)S(1)}, f32[4,4,16,128]{3,2,1,0:T(8,128)S(1)}, u32[]{:S(2)}, u32[]{:S(2)}) %collective-permute-start.30) | collective-permute-done | bytes 131104 | tf_op jit(solution)/shard_map/ppermute | solution.py:42
  87.6 1.3 %shard_map.74 = f32[2,2,128,128]{3,2,1,0:T(8,128)} custom-call(s32[7]{0:T(128)S(1)} %stack.82.scal, f32[4,4,16,128]{3,2,1,0:T(8,128)S(1)} %pad_maximum_fusion.6.own_ref, f32[4,4,16,128]{3,2,1,0:T(8,128)S(1)} %collective-permute-done.30.other_ref), custom_call_target="tpu_custom_call" | custom-call | bytes 1048576 | tf_op jit(solution)/shard_map/pallas_call | solution.py:330
  (114 shorter events, 22.8 us)
Async XLA Ops:
  2.4 5.0 %collective-permute-start.1 = (f32[136,128]{1,0:T(8,128)S(1)}, f32[136,128]{1,0:T(8,128)S(1)}, u32[]{:S(2)}, u32[]{:S(2)}) collective-permute-start(f32[136,128]{1,0:T(8,128)S(1)} %get-tuple-element.66), channel_id=1, source_target_pairs={{4,8},{8,4},{12,16},{16,12},{20,24},{24,20},{5,9},{9,5},{13,17},{1... | collective-permute-start | bytes 208904 | tf_op jit(solution)/shard_map/ppermute | solution.py:42
  3.1 5.3 %collective-permute-start = (f32[136,128]{1,0:T(8,128)S(1)}, f32[136,128]{1,0:T(8,128)S(1)}, u32[]{:S(2)}, u32[]{:S(2)}) collective-permute-start(f32[136,128]{1,0:T(8,128)S(1)} %get-tuple-element.67), channel_id=1, source_target_pairs={{0,4},{4,0},{8,12},{12,8},{16,20},{20,16},{24,28},{28,24},{1,5},{5... | collective-permute-start | bytes 208904 | tf_op jit(solution)/shard_map/ppermute | solution.py:42
  9.8 6.5 %collective-permute-start.2 = (f32[264,128]{1,0:T(8,128)S(1)}, f32[264,128]{1,0:T(8,128)S(1)}, u32[]{:S(2)}, u32[]{:S(2)}) collective-permute-start(f32[264,128]{1,0:T(8,128)S(1)} %concatenate.32), channel_id=1, source_target_pairs={{0,1},{1,0},{2,3},{3,2},{4,5},{5,4},{6,7},{7,6},{8,9},{9,8},{10,11... | collective-permute-start | bytes 405512 | tf_op jit(solution)/shard_map/ppermute | solution.py:42
  11.5 4.8 %collective-permute-start.3 = (f32[264,128]{1,0:T(8,128)S(1)}, f32[264,128]{1,0:T(8,128)S(1)}, u32[]{:S(2)}, u32[]{:S(2)}) collective-permute-start(f32[264,128]{1,0:T(8,128)S(1)} %concatenate.34), channel_id=1, source_target_pairs={{1,2},{2,1},{5,6},{6,5},{9,10},{10,9},{13,14},{14,13},{17,18},{18,... | collective-permute-start | bytes 405512 | tf_op jit(solution)/shard_map/ppermute | solution.py:42
  20.8 5.5 %collective-permute-start.4 = (f32[4,5,16,128]{3,2,1,0:T(8,128)S(1)}, f32[4,5,16,128]{3,2,1,0:T(8,128)S(1)}, u32[]{:S(2)}, u32[]{:S(2)}) collective-permute-start(f32[4,5,16,128]{3,2,1,0:T(8,128)S(1)} %get-tuple-element.23), channel_id=1, source_target_pairs={{0,4},{4,0},{8,12},{12,8},{16,20},{20,16},{24,28},{28,24},{1,5},{5... | collective-permute-start | bytes 491528 | tf_op jit(solution)/shard_map/ppermute | solution.py:42
  21.0 11.5 %collective-permute-start.5 = (f32[2,2,128,128]{3,2,1,0:T(8,128)S(1)}, f32[2,2,128,128]{3,2,1,0:T(8,128)S(1)}, u32[]{:S(2)}, u32[]{:S(2)}) collective-permute-start(f32[2,2,128,128]{3,2,1,0:T(8,128)S(1)} %get-tuple-element.42), channel_id=1, source_target_pairs={{0,1},{1,0},{2,3},{3,2},{4,5},{5,4},{6,7},{7,6},{8,9},{9,8},{10,11... | collective-permute-start | bytes 786440 | tf_op jit(solution)/shard_map/ppermute | solution.py:42
  25.7 6.9 %collective-permute-start.6 = (f32[2,2,128,128]{3,2,1,0:T(8,128)S(1)}, f32[2,2,128,128]{3,2,1,0:T(8,128)S(1)}, u32[]{:S(2)}, u32[]{:S(2)}) collective-permute-start(f32[2,2,128,128]{3,2,1,0:T(8,128)S(1)} %get-tuple-element.43), channel_id=1, source_target_pairs={{1,2},{2,1},{5,6},{6,5},{9,10},{10,9},{13,14},{14,13},{17,18},{18,... | collective-permute-start | bytes 786440 | tf_op jit(solution)/shard_map/ppermute | solution.py:42
  26.4 7.1 %collective-permute-start.11 = (f32[5,16,128]{2,1,0:T(8,128)S(1)}, f32[5,16,128]{2,1,0:T(8,128)S(1)}, u32[]{:S(2)}, u32[]{:S(2)}) collective-permute-start(f32[5,16,128]{2,1,0:T(8,128)S(1)} %get-tuple-element.59), channel_id=1, source_target_pairs={{0,24},{4,28},{8,16},{12,20},{16,8},{20,12},{24,0},{28,4},{1,25},{... | collective-permute-start | bytes 122888 | tf_op jit(solution)/shard_map/ppermute | solution.py:46
  29.3 4.3 %collective-permute-start.10 = (f32[5,16,128]{2,1,0:T(8,128)S(1)}, f32[5,16,128]{2,1,0:T(8,128)S(1)}, u32[]{:S(2)}, u32[]{:S(2)}) collective-permute-start(f32[5,16,128]{2,1,0:T(8,128)S(1)} %get-tuple-element.60), channel_id=1, source_target_pairs={{0,16},{4,20},{8,24},{12,28},{16,0},{20,4},{24,8},{28,12},{1,17},{... | collective-permute-start | bytes 122888 | tf_op jit(solution)/shard_map/ppermute | solution.py:46
  30.3 4.0 %collective-permute-start.9 = (f32[5,16,128]{2,1,0:T(8,128)S(1)}, f32[5,16,128]{2,1,0:T(8,128)S(1)}, u32[]{:S(2)}, u32[]{:S(2)}) collective-permute-start(f32[5,16,128]{2,1,0:T(8,128)S(1)} %get-tuple-element.61), channel_id=1, source_target_pairs={{0,8},{4,12},{8,0},{12,4},{16,24},{20,28},{24,16},{28,20},{1,9},{5... | collective-permute-start | bytes 122888 | tf_op jit(solution)/shard_map/ppermute | solution.py:46
  32.8 7.0 %collective-permute-start.8 = (f32[2,2,128,128]{3,2,1,0:T(8,128)S(1)}, f32[2,2,128,128]{3,2,1,0:T(8,128)S(1)}, u32[]{:S(2)}, u32[]{:S(2)}) collective-permute-start(f32[2,2,128,128]{3,2,1,0:T(8,128)S(1)} %pad_maximum_fusion.2), channel_id=1, source_target_pairs={{4,8},{8,4},{12,16},{16,12},{20,24},{24,20},{5,9},{9,5},{13,17},{1... | collective-permute-start | bytes 786440 | tf_op jit(solution)/shard_map/ppermute | solution.py:42
  34.4 5.9 %collective-permute-start.14 = (f32[5,16,128]{2,1,0:T(8,128)S(1)}, f32[5,16,128]{2,1,0:T(8,128)S(1)}, u32[]{:S(2)}, u32[]{:S(2)}) collective-permute-start(f32[5,16,128]{2,1,0:T(8,128)S(1)} %fusion.4), channel_id=1, source_target_pairs={{0,3},{1,2},{2,1},{3,0},{4,7},{5,6},{6,5},{7,4},{8,11},{9,10},{10,... | collective-permute-start | bytes 122888 | tf_op jit(solution)/shard_map/ppermute | solution.py:46
  37.5 5.1 %collective-permute-start.13 = (f32[5,16,128]{2,1,0:T(8,128)S(1)}, f32[5,16,128]{2,1,0:T(8,128)S(1)}, u32[]{:S(2)}, u32[]{:S(2)}) collective-permute-start(f32[5,16,128]{2,1,0:T(8,128)S(1)} %fusion.4), channel_id=1, source_target_pairs={{0,2},{1,3},{2,0},{3,1},{4,6},{5,7},{6,4},{7,5},{8,10},{9,11},{10,... | collective-permute-start | bytes 122888 | tf_op jit(solution)/shard_map/ppermute | solution.py:46
  39.6 4.0 %collective-permute-start.12 = (f32[5,16,128]{2,1,0:T(8,128)S(1)}, f32[5,16,128]{2,1,0:T(8,128)S(1)}, u32[]{:S(2)}, u32[]{:S(2)}) collective-permute-start(f32[5,16,128]{2,1,0:T(8,128)S(1)} %fusion.4), channel_id=1, source_target_pairs={{0,1},{1,0},{2,3},{3,2},{4,5},{5,4},{6,7},{7,6},{8,9},{9,8},{10,11... | collective-permute-start | bytes 122888 | tf_op jit(solution)/shard_map/ppermute | solution.py:46
  43.6 6.4 %collective-permute-start.17 = (f32[4,16,128]{2,1,0:T(8,128)S(1)}, f32[4,16,128]{2,1,0:T(8,128)S(1)}, u32[]{:S(2)}, u32[]{:S(2)}) collective-permute-start(f32[4,16,128]{2,1,0:T(8,128)S(1)} %fusion.6), channel_id=1, source_target_pairs={{0,24},{4,28},{8,16},{12,20},{16,8},{20,12},{24,0},{28,4},{1,25},{... | collective-permute-start | bytes 98312 | tf_op jit(solution)/shard_map/ppermute | solution.py:46
  48.1 3.9 %collective-permute-start.16 = (f32[4,16,128]{2,1,0:T(8,128)S(1)}, f32[4,16,128]{2,1,0:T(8,128)S(1)}, u32[]{:S(2)}, u32[]{:S(2)}) collective-permute-start(f32[4,16,128]{2,1,0:T(8,128)S(1)} %fusion.6), channel_id=1, source_target_pairs={{0,16},{4,20},{8,24},{12,28},{16,0},{20,4},{24,8},{28,12},{1,17},{... | collective-permute-start | bytes 98312 | tf_op jit(solution)/shard_map/ppermute | solution.py:46
  57.9 10.0 %collective-permute-start.20 = (f32[256,128]{1,0:T(8,128)S(1)}, f32[256,128]{1,0:T(8,128)S(1)}, u32[]{:S(2)}, u32[]{:S(2)}) collective-permute-start(f32[256,128]{1,0:T(8,128)S(1)} %get-tuple-element.34), channel_id=1, source_target_pairs={{4,8},{8,4},{12,16},{16,12},{20,24},{24,20},{5,9},{9,5},{13,17},{1... | collective-permute-start | bytes 393224 | tf_op jit(solution)/shard_map/ppermute | solution.py:42
  59.4 7.2 %collective-permute-start.23 = (f32[5,16,128]{2,1,0:T(8,128)S(1)}, f32[5,16,128]{2,1,0:T(8,128)S(1)}, u32[]{:S(2)}, u32[]{:S(2)}) collective-permute-start(f32[5,16,128]{2,1,0:T(8,128)S(1)} %get-tuple-element.56), channel_id=1, source_target_pairs={{0,24},{4,28},{8,16},{12,20},{16,8},{20,12},{24,0},{28,4},{1,25},{... | collective-permute-start | bytes 122888 | tf_op jit(solution)/shard_map/ppermute | solution.py:46
  63.0 4.1 %collective-permute-start.22 = (f32[5,16,128]{2,1,0:T(8,128)S(1)}, f32[5,16,128]{2,1,0:T(8,128)S(1)}, u32[]{:S(2)}, u32[]{:S(2)}) collective-permute-start(f32[5,16,128]{2,1,0:T(8,128)S(1)} %get-tuple-element.57), channel_id=1, source_target_pairs={{0,16},{4,20},{8,24},{12,28},{16,0},{20,4},{24,8},{28,12},{1,17},{... | collective-permute-start | bytes 122888 | tf_op jit(solution)/shard_map/ppermute | solution.py:46
  63.4 4.5 %collective-permute-start.21 = (f32[5,16,128]{2,1,0:T(8,128)S(1)}, f32[5,16,128]{2,1,0:T(8,128)S(1)}, u32[]{:S(2)}, u32[]{:S(2)}) collective-permute-start(f32[5,16,128]{2,1,0:T(8,128)S(1)} %get-tuple-element.58), channel_id=1, source_target_pairs={{0,8},{4,12},{8,0},{12,4},{16,24},{20,28},{24,16},{28,20},{1,9},{5... | collective-permute-start | bytes 122888 | tf_op jit(solution)/shard_map/ppermute | solution.py:46
  68.7 10.9 %collective-permute-start.24 = (f32[208,128]{1,0:T(8,128)S(1)}, f32[208,128]{1,0:T(8,128)S(1)}, u32[]{:S(2)}, u32[]{:S(2)}) collective-permute-start(f32[208,128]{1,0:T(8,128)S(1)} %get-tuple-element.37), channel_id=1, source_target_pairs={{0,1},{1,0},{2,3},{3,2},{4,5},{5,4},{6,7},{7,6},{8,9},{9,8},{10,11... | collective-permute-start | bytes 319496 | tf_op jit(solution)/shard_map/ppermute | solution.py:46
  70.4 9.1 %collective-permute-start.25 = (f32[208,128]{1,0:T(8,128)S(1)}, f32[208,128]{1,0:T(8,128)S(1)}, u32[]{:S(2)}, u32[]{:S(2)}) collective-permute-start(f32[208,128]{1,0:T(8,128)S(1)} %get-tuple-element.38), channel_id=1, source_target_pairs={{0,3},{1,2},{2,1},{3,0},{4,7},{5,6},{6,5},{7,4},{8,11},{9,10},{10,... | collective-permute-start | bytes 319496 | tf_op jit(solution)/shard_map/ppermute | solution.py:46
  73.0 6.5 %collective-permute-start.26 = (f32[80,128]{1,0:T(8,128)S(1)}, f32[80,128]{1,0:T(8,128)S(1)}, u32[]{:S(2)}, u32[]{:S(2)}) collective-permute-start(f32[80,128]{1,0:T(8,128)S(1)} %bitcast.72), channel_id=1, source_target_pairs={{0,2},{1,3},{2,0},{3,1},{4,6},{5,7},{6,4},{7,5},{8,10},{9,11},{10,... | collective-permute-start | bytes 122888 | tf_op jit(solution)/shard_map/ppermute | solution.py:46
  79.6 5.0 %collective-permute-start.29 = (f32[4,16,128]{2,1,0:T(8,128)S(1)}, f32[4,16,128]{2,1,0:T(8,128)S(1)}, u32[]{:S(2)}, u32[]{:S(2)}) collective-permute-start(f32[4,16,128]{2,1,0:T(8,128)S(1)} %divide_subtract_fusion), channel_id=1, source_target_pairs={{0,24},{4,28},{8,16},{12,20},{16,8},{20,12},{24,0},{28,4},{1,25},{... | collective-permute-start | bytes 98312 | tf_op jit(solution)/shard_map/ppermute | solution.py:46
  (12 other events, 40.7 us)

commit v3 on v2

--- a/solution.py
+++ b/solution.py
@@ -76,10 +76,9 @@
     weight = sum(probe_ref[k, part] * probe_ref[k, part] for k in range(probe_ref.shape[0]) for part in range(2))
     lane = lax.broadcasted_iota(jnp.int32, (extent, extent), 1)
 
-    count = corners.shape[0] // 18
-    for device in range(9):
-        for j in range(device * count, (device + 1) * count):
-            row, col = corners[2 * j] + extent, corners[2 * j + 1]
+    for device in range(corners.shape[0]):
+        for j in range(corners.shape[2]):
+            row, col = corners[device, 0, j] + extent, corners[device, 1, j]
             moved = pltpu.roll(weight, col & (extent - 1), 1)
             for side in range(2):
                 if device % 3 == 2 * (1 - side):
@@ -129,7 +128,7 @@
         span = range(first, min(first + group, positions))
         patches = []
         for j in span:
-            row, col = offs[2 * j], offs[2 * j + 1]
+            row, col = offs[0, j], offs[1, j]
             back = (extent - col) & (extent - 1)
             patches.append([
                 jnp.where(
@@ -171,7 +170,7 @@
         chi = product(split(half), w2)
         for at, j in enumerate(span):
             o_r, o_i = patches[at]
-            row, col = offs[2 * j], offs[2 * j + 1]
+            row, col = offs[0, j], offs[1, j]
             turn = col & (extent - 1)
             g_r = g_i = 0.0
             for k in range(modes):
@@ -190,7 +189,7 @@
                 moved = pltpu.roll(term, turn, 1)
                 grad[plane, 0, pl.ds(row, extent), :] += jnp.where(lane >= col, moved, 0.0)
                 grad[plane, 1, pl.ds(row, extent), :] += jnp.where(lane < col, moved, 0.0)
-    if len(outs) == 1:
+    if len(outs[0].shape) == len(outs[1].shape):
         give_quadrants(scal, grad, outs)
     else:
         give_rims(scal, grad, outs, send_out)
@@ -215,7 +214,7 @@
         for b in range(2):
             side = jnp.where(scal[1] == b, 1, 0)
             for plane in range(grad.shape[0]):
-                outs[0][b, a, plane] = grad[plane, side, pl.ds(row, extent), :]
+                outs[b][a, plane] = grad[plane, side, pl.ds(row, extent), :]
 
 
 def give_rims(scal, grad, outs, send_out):
@@ -279,8 +278,10 @@
 
 
 def first_kernel(
-    scal, offs, tile_ref, rows_near, rows_far, cols_near, cols_far, probe_ref, measured_ref, table_ref, *rest
+    scal, offs, tile_ref, rows_near, rows_far, cols_near, cols_far, reach, probe_ref, measured_ref, table_ref,
+    reaches_out, *rest,
 ):
+    reaches_out[0:8, :], reaches_out[8:16, :], reaches_out[16:24, :] = cols_near[-8:, :], cols_far[-8:, :], reach[...]
     outs, (keep_out, send_out, canvas_ref, grad, sums) = rest[:-5], rest[-5:]
     extent = tile_ref.shape[-1]
     halo = extent // 2
@@ -338,34 +339,44 @@
     )(*operands)
 
 
-def fetch(tile, offsets, halo):
+def fetch(tile, offs, halo):
     lanes = tile.shape[-1]
     odd_row, odd_col = (lax.axis_index(axis) % 2 == 1 for axis in ("sy", "sx"))
-    corners = jnp.pad((offsets.reshape(1, -1) + 1).astype(jnp.float32), ((0, 7), (0, lanes - offsets.size)))
-
-    def rows_of(rim):
-        return jnp.concatenate([rim.reshape(-1, lanes), corners])
-
-    upper, lower = tile[:, :halo], tile[:, -halo:]
-    rows_near = swapped(rows_of(jnp.where(odd_row, upper, lower)), "sy", False)
-    rows_far = swapped(rows_of(jnp.where(odd_row, lower, upper)), "sy", True)
+    upper, lower = tile[:, :halo].reshape(-1, lanes), tile[:, halo:].reshape(-1, lanes)
+    near, far = jnp.where(odd_row, upper, lower), jnp.where(odd_row, lower, upper)
+    own = jnp.pad((after(offs, near, far) + 1).astype(jnp.float32), ((0, 6), (0, lanes - offs.shape[1])))
+    near, far = jnp.concatenate([near, own]), jnp.concatenate([far, own])
+    rows_near, rows_far = swapped(near, "sy", False), swapped(far, "sy", True)
+    side = after(tile, near, far)
+    left = jnp.concatenate([side[0, :, :halo], side[1, :, :halo]], axis=1)
+    right = jnp.concatenate([side[0, :, halo:], side[1, :, halo:]], axis=1)
+    left, right = jnp.where(odd_col, left, right), jnp.where(odd_col, right, left)
+    above, below = jnp.where(odd_row, rows_near, rows_far), jnp.where(odd_row, rows_far, rows_near)
     last = 2 * halo
-    above, below = jnp.where(odd_row, rows_near, rows_far), jnp.where(odd_row, rows_far, rows_near)
-    column = jnp.concatenate([above[:last].reshape(2, halo, lanes), tile, below[:last].reshape(2, halo, lanes)], axis=1)
-    reach = jnp.concatenate([above[last : last + 1], corners[:1], below[last : last + 1], corners[3:]])
-
-    def columns_of(rim):
-        return jnp.concatenate([jnp.concatenate([rim[0], rim[1]], axis=1), reach])
-
-    left, right = column[..., :halo], column[..., -halo:]
-    cols_near = swapped(columns_of(jnp.where(odd_col, left, right)), "sx", False)
-    cols_far = swapped(columns_of(jnp.where(odd_col, right, left)), "sx", True)
-    sides = [jnp.where(odd_col, cols_near, cols_far), reach, jnp.where(odd_col, cols_far, cols_near)]
-    found = jnp.stack([side[-8:-5, : offsets.size] for side in sides], axis=1).astype(jnp.int32) - 1
-    found = found.reshape(3, 3, -1, 2)
-    step = (jnp.arange(3, dtype=jnp.int32) - 1) * lanes
-    shift = jnp.stack(jnp.broadcast_arrays(step[:, None], step[None, :]), axis=-1)[:, :, None]
-    return rows_near, rows_far, cols_near, cols_far, jnp.where(found < 0, -lanes, found + shift).reshape(-1)
+    reach = jnp.concatenate([above[last : last + 2], own[:2], below[last : last + 2], own[6:]])
+
+    def columns_of(middle, first):
+        ends = []
+        for rim in (above, below):
+            rim = rim[:last].reshape(2, halo, lanes)
+            half = [jnp.where(first, rim[part, :, :halo], rim[part, :, halo:]) for part in range(2)]
+            ends.append(jnp.concatenate(half, axis=1))
+        return jnp.concatenate([ends[0], middle, ends[1], reach])
+
+    cols_near = swapped(columns_of(left, odd_col), "sx", False)
+    cols_far = swapped(columns_of(right, ~odd_col), "sx", True)
+    return rows_near, rows_far, cols_near, cols_far, reach
+
+
+def corners_of(reaches, positions, extent):
+    near, far, own = reaches[:8], reaches[8:16], reaches[16:]
+    odd = lax.axis_index("sx") % 2 == 1
+    sides = [jnp.where(odd, near, far), own, jnp.where(odd, far, near)]
+    found = jnp.stack([side[:6, :positions].reshape(3, 2, positions) for side in sides], axis=1)
+    found = found.reshape(9, 2, positions).astype(jnp.int32) - 1
+    at = jnp.arange(9, dtype=jnp.int32)
+    step = (jnp.stack([at // 3, at % 3], axis=1) - 1) * extent
+    return jnp.where(found < 0, -extent, found + step[:, :, None])
 
 
 def after(value, *others):
@@ -402,18 +413,19 @@
     table = jnp.asarray(dft_tables(extent))
     scal = head_scalars(size, halo)
     offsets = scan_offsets[0, 0]
-    offs = offsets.reshape(-1)
+    positions = offsets.shape[0]
+    offs = offsets.T
     kept = (chips, planes + 1, rows, extent)
     count = chips * (planes + 1) * rows
     rim_rows = 2 * 2 * halo
-    quadrants = (f32(2, 2, 2, tile, tile),)
+    quadrants = (f32(2, 2, tile, tile),) * 2
     rims = (f32(2, 2, tile, tile), f32(rim_rows, tile))
     scratch = ((2, 2, size, tile), (planes + 1, extent, extent))
-    work = 2 * 3 * offsets.shape[0] * 4 * (2 * extent) ** 3
+    work = 2 * 3 * positions * 4 * (2 * extent) ** 3
 
     start = (lax.axis_index("sy") % 2 * chips + lax.axis_index("sy") // 2) * rows
     chunk = lax.dynamic_slice_in_dim(probe_modes.reshape(planes, extent, extent), start, rows, axis=1)
-    *halos, corners = fetch(object_tile, offsets, halo)
+    halos = fetch(object_tile, offs, halo)
 
     def light(probe, corners):
         lit = (2, 2 * size, extent)
@@ -426,18 +438,20 @@
         outs = (rims if final else quadrants) + (f32(*kept), f32(*sent), f32(2, 2, size, tile))
         if iteration == 0:
             operands = (scal, offs, object_tile, *halos, probe, measured, table)
-            *given, keep, send, canvas = kernel_call(first_kernel, outs, operands, scratch, flops=work)
+            outs = (f32(24, tile),) + outs
+            reaches, *given, keep, send, canvas = kernel_call(first_kernel, outs, operands, scratch, flops=work)
         else:
             operands = (scal, offs, canvas, scale, near, far, own, other, measured, table)
             outs = outs + (f32(*probe.shape),)
             *given, keep, send, canvas, probe = kernel_call(next_kernel, outs, operands, scratch, flops=work)
         received = swapped(send, "sy", False)
         both = keep + received.reshape(-1, extent)[:count].reshape(kept)
+        if iteration == 0:
+            corners = corners_of(after(reaches, both), positions, tile)
         scale = light(probe, after(corners, both))
         if not final:
-            (grad,) = given
-            side_a = grad[0] + swapped(grad[0], "sx", False)
-            side_b = grad[1] + swapped(grad[1], "sx", True)
+            side_a = given[0] + swapped(given[0], "sx", False)
+            side_b = given[1] + swapped(given[1], "sx", True)
             near, far = jnp.stack([side_a[0], side_b[0]]), jnp.stack([side_a[1], side_b[1]])
             near = near + swapped(near, "sy", False)
             far = far + swapped(far, "sy", True)
@@ -451,15 +465,11 @@
             middle, near, far = kernel_call(
                 middle_kernel, (f32(2, tile, tile), message, message), (scal, own_rows, received, far, total), scalars=1
             )
+            head = total.shape[0]
             near = flipped(near, "sx", 1)
-            head = total.shape[0]
-            if lax.axis_size("sx") == 4:
-                far = flipped(far, "sx", 3)
-                parts = [total, near[:head], flipped(total, "sx", 2), far[:head]]
-            else:
-                far = swapped(far, "sx", True)
-                parts = across(total, 2)
-                parts.insert(1, near[:head])
+            far = swapped(far[head:], "sx", True)
+            parts = across(total, 2)
+            parts.insert(1, near[:head])
             chunk = probe_fresh(parts, chunk)
             outcome = kernel_call(object_kernel, f32(2, tile, tile), (scal, canvas, scale, middle, near, far), scalars=1)
         own = probe_spread(chunk, chips)

time: 89.2 us -> 86.5 us (0.970)
  waiting for transfers between devices: 26.6 us -> 24.2 us
  local copies, waits for them, and re-layouts: 2.83 us -> 1.18 us
    ppermute x18, waiting for transfers between devices: 17.6 us -> 15.6 us  [flipped(): lax.ppermute(values, axis, [(i, i ^ bits) for i in range(lax.axis_size(ax...]
    unnamed x11 -> x10, local copies, waits for them, and re-layouts: 1.64 us -> 0.69 us
    ppermute x13 -> x14, starting transfers between devices: 14.6 us -> 15.5 us  [swapped(): return lax.ppermute(values, axis, pairs)]
    ppermute x13 -> x14, waiting for transfers between devices: 8.97 us -> 8.58 us  [swapped(): return lax.ppermute(values, axis, pairs)]
  transfers between devices with their start and end apart: 31 -> 32, of which waited for: 19 -> 21; matrix products, arithmetic and copies ran while one was open for 1% -> 1% of each run, Pallas kernels for 5% -> 5%
where the time goes in v3:
time: 86.5 us; the launch traced here: 86.2 us
  starting transfers between devices  43.6 us (50%)
  waiting for transfers between devices  24.2 us (28%)
  Pallas kernels  14.2 us (16%)
  other arithmetic  1.91 us (2%)
  local copies, waits for them, and re-layouts  1.18 us (1%)
  between operations  1.14 us (1%)
    ppermute x18, starting transfers between devices, flipped(): lax.ppermute(values, axis, [(i, i ^ bits) for i in range(lax.axis_size(ax...  28.1 us
    ppermute x18, waiting for transfers between devices, flipped(): lax.ppermute(values, axis, [(i, i ^ bits) for i in range(lax.axis_size(ax...  15.6 us
    ppermute x14, starting transfers between devices, swapped(): return lax.ppermute(values, axis, pairs)  15.5 us
    pallas_call x7, Pallas kernels, kernel_call(): pl.pallas_call(body, out_shape=outs, in_specs=[SMEM] * scalars + [VMEM] *...  14.2 us
    ppermute x14, waiting for transfers between devices, swapped(): return lax.ppermute(values, axis, pairs)  8.58 us
  transfers between devices with their start and end apart: 32, of which 21 were waited for; matrix products, arithmetic and copies ran while one was open for 1% of the time, Pallas kernels for 5%

profile of v3, /device:TPU:0, one launch (start us, length us, event | category | flops | bytes accessed | tf_op | source)
XLA Modules:
  0.0 86.2 jit_solution(17581472682189501128)
XLA Ops:
  3.1 4.4 %collective-permute-start = (f32[136,128]{1,0:T(8,128)S(1)}, f32[136,128]{1,0:T(8,128)S(1)}, u32[]{:S(2)}, u32[]{:S(2)}) collective-permute-start(f32[136,128]{1,0:T(8,128)S(1)} %get-tuple-element.81), channel_id=1, source_target_pairs={{0,4},{4,0},{8,12},{12,8},{16,20},{20,16},{24,28},{28,24},{1,5},{5... | collective-permute-start | bytes 208904 | tf_op jit(solution)/shard_map/ppermute | solution.py:42
  8.7 1.6 %collective-permute-start.2 = (f32[264,128]{1,0:T(8,128)S(1)}, f32[264,128]{1,0:T(8,128)S(1)}, u32[]{:S(2)}, u32[]{:S(2)}) collective-permute-start(f32[264,128]{1,0:T(8,128)S(1)} %concatenate.45), channel_id=1, source_target_pairs={{0,1},{1,0},{2,3},{3,2},{4,5},{5,4},{6,7},{7,6},{8,9},{9,8},{10,11... | collective-permute-start | bytes 405512 | tf_op jit(solution)/shard_map/ppermute | solution.py:42
  11.4 3.8 %collective-permute-done.2.cols_near = f32[264,128]{1,0:T(8,128)S(1)} collective-permute-done((f32[264,128]{1,0:T(8,128)S(1)}, f32[264,128]{1,0:T(8,128)S(1)}, u32[]{:S(2)}, u32[]{:S(2)}) %collective-permute-start.2) | collective-permute-done | bytes 135200 | tf_op jit(solution)/shard_map/ppermute | solution.py:42
  15.2 4.0 %shard_map.68 = (f32[24,128]{1,0:T(8,128)S(1)}, f32[2,2,128,128]{3,2,1,0:T(8,128)S(1)}, f32[2,2,128,128]{3,2,1,0:T(8,128)S(1)}, f32[4,5,16,128]{3,2,1,0:T(8,128)...) custom-call(s32[7]{0:T(128)S(1)} %stack.75.scal, s32[2,4]{1,0:T(2,128)S(1)} %bitcast.90, ...), custom_call_target="tpu_custom_call" | custom-call | flops 1610612736 | bytes 1048576 | tf_op jit(solution)/shard_map/pallas_call | solution.py:331
  19.5 4.9 %collective-permute-start.5 = (f32[2,2,128,128]{3,2,1,0:T(8,128)S(1)}, f32[2,2,128,128]{3,2,1,0:T(8,128)S(1)}, u32[]{:S(2)}, u32[]{:S(2)}) collective-permute-start(f32[2,2,128,128]{3,2,1,0:T(8,128)S(1)} %get-tuple-element.34), channel_id=1, source_target_pairs={{0,1},{1,0},{2,3},{3,2},{4,5},{5,4},{6,7},{7,6},{8,9},{9,8},{10,11... | collective-permute-start | bytes 786440 | tf_op jit(solution)/shard_map/ppermute | solution.py:42
  25.3 2.8 %collective-permute-start.11 = (f32[5,16,128]{2,1,0:T(8,128)S(1)}, f32[5,16,128]{2,1,0:T(8,128)S(1)}, u32[]{:S(2)}, u32[]{:S(2)}) collective-permute-start(f32[5,16,128]{2,1,0:T(8,128)S(1)} %get-tuple-element.59), channel_id=1, source_target_pairs={{0,24},{4,28},{8,16},{12,20},{16,8},{20,12},{24,0},{28,4},{1,25},{... | collective-permute-start | bytes 122888 | tf_op jit(solution)/shard_map/ppermute | solution.py:46
  29.1 1.5 %shard_map.69.scale_ref = f32[2,256,128]{2,1,0:T(8,128)S(1)} custom-call(s32[7]{0:T(128)S(1)} %stack.75.scal, s32[9,2,4]{2,1,0:T(2,128)S(1)} %compare_select_fusion.corners, f32[2,2,128,128]{3,2,1,0:T(8,128)S(1)} %copy-done.1), custom_call_target="tpu_custom_call" | custom-call | flops 805306368 | bytes 1048576 | tf_op jit(solution)/shard_map/pallas_call | solution.py:331
  33.2 3.1 %collective-permute-start.14 = (f32[5,16,128]{2,1,0:T(8,128)S(1)}, f32[5,16,128]{2,1,0:T(8,128)S(1)}, u32[]{:S(2)}, u32[]{:S(2)}) collective-permute-start(f32[5,16,128]{2,1,0:T(8,128)S(1)} %fusion.4), channel_id=1, source_target_pairs={{0,3},{1,2},{2,1},{3,0},{4,7},{5,6},{6,5},{7,4},{8,11},{9,10},{10,... | collective-permute-start | bytes 122888 | tf_op jit(solution)/shard_map/ppermute | solution.py:46
  36.3 1.9 %collective-permute-start.13 = (f32[5,16,128]{2,1,0:T(8,128)S(1)}, f32[5,16,128]{2,1,0:T(8,128)S(1)}, u32[]{:S(2)}, u32[]{:S(2)}) collective-permute-start(f32[5,16,128]{2,1,0:T(8,128)S(1)} %fusion.4), channel_id=1, source_target_pairs={{0,2},{1,3},{2,0},{3,1},{4,6},{5,7},{6,4},{7,5},{8,10},{9,11},{10,... | collective-permute-start | bytes 122888 | tf_op jit(solution)/shard_map/ppermute | solution.py:46
  39.1 2.1 %collective-permute-done.13 = f32[5,16,128]{2,1,0:T(8,128)S(1)} collective-permute-done((f32[5,16,128]{2,1,0:T(8,128)S(1)}, f32[5,16,128]{2,1,0:T(8,128)S(1)}, u32[]{:S(2)}, u32[]{:S(2)}) %collective-permute-start.13) | collective-permute-done | bytes 40992 | tf_op jit(solution)/shard_map/ppermute | solution.py:46
  42.2 4.5 %collective-permute-start.17 = (f32[4,16,128]{2,1,0:T(8,128)S(1)}, f32[4,16,128]{2,1,0:T(8,128)S(1)}, u32[]{:S(2)}, u32[]{:S(2)}) collective-permute-start(f32[4,16,128]{2,1,0:T(8,128)S(1)} %fusion.6), channel_id=1, source_target_pairs={{0,24},{4,28},{8,16},{12,20},{16,8},{20,12},{24,0},{28,4},{1,25},{... | collective-permute-start | bytes 98312 | tf_op jit(solution)/shard_map/ppermute | solution.py:46
  47.1 1.3 %collective-permute-start.15 = (f32[4,16,128]{2,1,0:T(8,128)S(1)}, f32[4,16,128]{2,1,0:T(8,128)S(1)}, u32[]{:S(2)}, u32[]{:S(2)}) collective-permute-start(f32[4,16,128]{2,1,0:T(8,128)S(1)} %fusion.6), channel_id=1, source_target_pairs={{0,8},{4,12},{8,0},{12,4},{16,24},{20,28},{24,16},{28,20},{1,9},{5... | collective-permute-start | bytes 98312 | tf_op jit(solution)/shard_map/ppermute | solution.py:46
  48.6 2.0 %collective-permute-done.16 = f32[4,16,128]{2,1,0:T(8,128)S(1)} collective-permute-done((f32[4,16,128]{2,1,0:T(8,128)S(1)}, f32[4,16,128]{2,1,0:T(8,128)S(1)}, u32[]{:S(2)}, u32[]{:S(2)}) %collective-permute-start.16) | collective-permute-done | bytes 32800 | tf_op jit(solution)/shard_map/ppermute | solution.py:46
  51.1 1.3 %collective-permute-done.18.other_ref = f32[4,4,16,128]{3,2,1,0:T(8,128)S(1)} collective-permute-done((f32[4,4,16,128]{3,2,1,0:T(8,128)S(1)}, f32[4,4,16,128]{3,2,1,0:T(8,128)S(1)}, u32[]{:S(2)}, u32[]{:S(2)}) %collective-permute-start.18) | collective-permute-done | bytes 131104 | tf_op jit(solution)/shard_map/ppermute | solution.py:42
  52.5 3.8 %shard_map.70 = (f32[2,2,128,128]{3,2,1,0:T(8,128)S(1)}, f32[256,128]{1,0:T(8,128)S(1)}, f32[4,5,16,128]{3,2,1,0:T(8,128)S(1)}, f32[576,128]{1,0:T(8,128)S(1)}, ...) custom-call(s32[7]{0:T(128)S(1)} %stack.75.scal, s32[2,4]{1,0:T(2,128)S(1)} %bitcast.91, ...), custom_call_target="tpu_custom_call" | custom-call | flops 1610612736 | bytes 1048576 | tf_op jit(solution)/shard_map/pallas_call | solution.py:331
  58.0 3.5 %collective-permute-start.23 = (f32[5,16,128]{2,1,0:T(8,128)S(1)}, f32[5,16,128]{2,1,0:T(8,128)S(1)}, u32[]{:S(2)}, u32[]{:S(2)}) collective-permute-start(f32[5,16,128]{2,1,0:T(8,128)S(1)} %get-tuple-element.56), channel_id=1, source_target_pairs={{0,24},{4,28},{8,16},{12,20},{16,8},{20,12},{24,0},{28,4},{1,25},{... | collective-permute-start | bytes 122888 | tf_op jit(solution)/shard_map/ppermute | solution.py:46
  62.8 1.5 %shard_map.71.scale_ref = f32[2,256,128]{2,1,0:T(8,128)S(1)} custom-call(s32[7]{0:T(128)S(1)} %stack.75.scal, s32[9,2,4]{2,1,0:T(2,128)S(1)} %compare_select_fusion.corners, f32[2,2,128,128]{3,2,1,0:T(8,128)S(1)} %get-tuple-element.42.probe_ref), custom_call_target="tpu_custom_call" | custom-call | flops 805306368 | bytes 1048576 | tf_op jit(solution)/shard_map/pallas_call | solution.py:331
  67.3 1.7 %collective-permute-start.24 = (f32[208,128]{1,0:T(8,128)S(1)}, f32[208,128]{1,0:T(8,128)S(1)}, u32[]{:S(2)}, u32[]{:S(2)}) collective-permute-start(f32[208,128]{1,0:T(8,128)S(1)} %get-tuple-element.47), channel_id=1, source_target_pairs={{0,1},{1,0},{2,3},{3,2},{4,5},{5,4},{6,7},{7,6},{8,9},{9,8},{10,11... | collective-permute-start | bytes 319496 | tf_op jit(solution)/shard_map/ppermute | solution.py:46
  69.0 1.9 %collective-permute-start.26 = (f32[80,128]{1,0:T(8,128)S(1)}, f32[80,128]{1,0:T(8,128)S(1)}, u32[]{:S(2)}, u32[]{:S(2)}) collective-permute-start(f32[80,128]{1,0:T(8,128)S(1)} %bitcast.86), channel_id=1, source_target_pairs={{0,2},{1,3},{2,0},{3,1},{4,6},{5,7},{6,4},{7,5},{8,10},{9,11},{10,... | collective-permute-start | bytes 122888 | tf_op jit(solution)/shard_map/ppermute | solution.py:46
  72.4 2.0 %collective-permute-done.26 = f32[80,128]{1,0:T(8,128)S(1)} collective-permute-done((f32[80,128]{1,0:T(8,128)S(1)}, f32[80,128]{1,0:T(8,128)S(1)}, u32[]{:S(2)}, u32[]{:S(2)}) %collective-permute-start.26) | collective-permute-done | bytes 40992 | tf_op jit(solution)/shard_map/ppermute | solution.py:46
  74.4 2.3 %collective-permute-done.27 = f32[80,128]{1,0:T(8,128)S(1)} collective-permute-done((f32[80,128]{1,0:T(8,128)S(1)}, f32[80,128]{1,0:T(8,128)S(1)}, u32[]{:S(2)}, u32[]{:S(2)}) %collective-permute-start.27) | collective-permute-done | bytes 40992 | tf_op jit(solution)/shard_map/ppermute | solution.py:46
  76.8 1.9 %collective-permute-start.30 = (f32[4,16,128]{2,1,0:T(8,128)S(1)}, f32[4,16,128]{2,1,0:T(8,128)S(1)}, u32[]{:S(2)}, u32[]{:S(2)}) collective-permute-start(f32[4,16,128]{2,1,0:T(8,128)S(1)} %divide_subtract_fusion), channel_id=1, source_target_pairs={{0,24},{4,28},{8,16},{12,20},{16,8},{20,12},{24,0},{28,4},{1,25},{... | collective-permute-start | bytes 98312 | tf_op jit(solution)/shard_map/ppermute | solution.py:46
  80.3 1.4 %shard_map.73 = f32[2,128,128]{2,1,0:T(8,128)} custom-call(s32[7]{0:T(128)S(1)} %stack.75.scal, f32[2,2,256,128]{3,2,1,0:T(8,128)S(1)} %get-tuple-element.38.old_ref, f32[2,256,128]{2,1,0:T(8,128)S(1)} %shard_map.71.scale_ref, f32[2,128,128]{2,1,0:T(8,128)S(1)} %get-tuple-element.46.middle_ref, f32[208,128]{1,0:T(8,128)S(1)} %collective-permute-done.24.near_ref, ...), custom_call_target="tpu_custom_call" | custom-call | bytes 1048576 | tf_op jit(solution)/shard_map/pallas_call | solution.py:331
  83.6 1.3 %collective-permute-done.31.other_ref = f32[4,4,16,128]{3,2,1,0:T(8,128)S(1)} collective-permute-done((f32[4,4,16,128]{3,2,1,0:T(8,128)S(1)}, f32[4,4,16,128]{3,2,1,0:T(8,128)S(1)}, u32[]{:S(2)}, u32[]{:S(2)}) %collective-permute-start.31) | collective-permute-done | bytes 131104 | tf_op jit(solution)/shard_map/ppermute | solution.py:42
  (115 shorter events, 24.3 us)
Async XLA Ops:
  2.3 5.4 %collective-permute-start.1 = (f32[136,128]{1,0:T(8,128)S(1)}, f32[136,128]{1,0:T(8,128)S(1)}, u32[]{:S(2)}, u32[]{:S(2)}) collective-permute-start(f32[136,128]{1,0:T(8,128)S(1)} %get-tuple-element.80), channel_id=1, source_target_pairs={{4,8},{8,4},{12,16},{16,12},{20,24},{24,20},{5,9},{9,5},{13,17},{1... | collective-permute-start | bytes 208904 | tf_op jit(solution)/shard_map/ppermute | solution.py:42
  3.1 5.3 %collective-permute-start = (f32[136,128]{1,0:T(8,128)S(1)}, f32[136,128]{1,0:T(8,128)S(1)}, u32[]{:S(2)}, u32[]{:S(2)}) collective-permute-start(f32[136,128]{1,0:T(8,128)S(1)} %get-tuple-element.81), channel_id=1, source_target_pairs={{0,4},{4,0},{8,12},{12,8},{16,20},{20,16},{24,28},{28,24},{1,5},{5... | collective-permute-start | bytes 208904 | tf_op jit(solution)/shard_map/ppermute | solution.py:42
  8.7 6.5 %collective-permute-start.2 = (f32[264,128]{1,0:T(8,128)S(1)}, f32[264,128]{1,0:T(8,128)S(1)}, u32[]{:S(2)}, u32[]{:S(2)}) collective-permute-start(f32[264,128]{1,0:T(8,128)S(1)} %concatenate.45), channel_id=1, source_target_pairs={{0,1},{1,0},{2,3},{3,2},{4,5},{5,4},{6,7},{7,6},{8,9},{9,8},{10,11... | collective-permute-start | bytes 405512 | tf_op jit(solution)/shard_map/ppermute | solution.py:42
  10.6 4.6 %collective-permute-start.3 = (f32[264,128]{1,0:T(8,128)S(1)}, f32[264,128]{1,0:T(8,128)S(1)}, u32[]{:S(2)}, u32[]{:S(2)}) collective-permute-start(f32[264,128]{1,0:T(8,128)S(1)} %concatenate.48), channel_id=1, source_target_pairs={{1,2},{2,1},{5,6},{6,5},{9,10},{10,9},{13,14},{14,13},{17,18},{18,... | collective-permute-start | bytes 405512 | tf_op jit(solution)/shard_map/ppermute | solution.py:42
  19.2 5.8 %collective-permute-start.4 = (f32[4,5,16,128]{3,2,1,0:T(8,128)S(1)}, f32[4,5,16,128]{3,2,1,0:T(8,128)S(1)}, u32[]{:S(2)}, u32[]{:S(2)}) collective-permute-start(f32[4,5,16,128]{3,2,1,0:T(8,128)S(1)} %get-tuple-element.31), channel_id=1, source_target_pairs={{0,4},{4,0},{8,12},{12,8},{16,20},{20,16},{24,28},{28,24},{1,5},{5... | collective-permute-start | bytes 491528 | tf_op jit(solution)/shard_map/ppermute | solution.py:42
  19.5 11.7 %collective-permute-start.5 = (f32[2,2,128,128]{3,2,1,0:T(8,128)S(1)}, f32[2,2,128,128]{3,2,1,0:T(8,128)S(1)}, u32[]{:S(2)}, u32[]{:S(2)}) collective-permute-start(f32[2,2,128,128]{3,2,1,0:T(8,128)S(1)} %get-tuple-element.34), channel_id=1, source_target_pairs={{0,1},{1,0},{2,3},{3,2},{4,5},{5,4},{6,7},{7,6},{8,9},{9,8},{10,11... | collective-permute-start | bytes 786440 | tf_op jit(solution)/shard_map/ppermute | solution.py:42
  24.4 6.9 %collective-permute-start.6 = (f32[2,2,128,128]{3,2,1,0:T(8,128)S(1)}, f32[2,2,128,128]{3,2,1,0:T(8,128)S(1)}, u32[]{:S(2)}, u32[]{:S(2)}) collective-permute-start(f32[2,2,128,128]{3,2,1,0:T(8,128)S(1)} %get-tuple-element.35), channel_id=1, source_target_pairs={{1,2},{2,1},{5,6},{6,5},{9,10},{10,9},{13,14},{14,13},{17,18},{18,... | collective-permute-start | bytes 786440 | tf_op jit(solution)/shard_map/ppermute | solution.py:42
  25.3 6.9 %collective-permute-start.11 = (f32[5,16,128]{2,1,0:T(8,128)S(1)}, f32[5,16,128]{2,1,0:T(8,128)S(1)}, u32[]{:S(2)}, u32[]{:S(2)}) collective-permute-start(f32[5,16,128]{2,1,0:T(8,128)S(1)} %get-tuple-element.59), channel_id=1, source_target_pairs={{0,24},{4,28},{8,16},{12,20},{16,8},{20,12},{24,0},{28,4},{1,25},{... | collective-permute-start | bytes 122888 | tf_op jit(solution)/shard_map/ppermute | solution.py:46
  28.1 4.1 %collective-permute-start.10 = (f32[5,16,128]{2,1,0:T(8,128)S(1)}, f32[5,16,128]{2,1,0:T(8,128)S(1)}, u32[]{:S(2)}, u32[]{:S(2)}) collective-permute-start(f32[5,16,128]{2,1,0:T(8,128)S(1)} %get-tuple-element.60), channel_id=1, source_target_pairs={{0,16},{4,20},{8,24},{12,28},{16,0},{20,4},{24,8},{28,12},{1,17},{... | collective-permute-start | bytes 122888 | tf_op jit(solution)/shard_map/ppermute | solution.py:46
  29.1 4.0 %collective-permute-start.9 = (f32[5,16,128]{2,1,0:T(8,128)S(1)}, f32[5,16,128]{2,1,0:T(8,128)S(1)}, u32[]{:S(2)}, u32[]{:S(2)}) collective-permute-start(f32[5,16,128]{2,1,0:T(8,128)S(1)} %get-tuple-element.61), channel_id=1, source_target_pairs={{0,8},{4,12},{8,0},{12,4},{16,24},{20,28},{24,16},{28,20},{1,9},{5... | collective-permute-start | bytes 122888 | tf_op jit(solution)/shard_map/ppermute | solution.py:46
  31.5 7.0 %collective-permute-start.8 = (f32[2,2,128,128]{3,2,1,0:T(8,128)S(1)}, f32[2,2,128,128]{3,2,1,0:T(8,128)S(1)}, u32[]{:S(2)}, u32[]{:S(2)}) collective-permute-start(f32[2,2,128,128]{3,2,1,0:T(8,128)S(1)} %pad_maximum_fusion.1), channel_id=1, source_target_pairs={{4,8},{8,4},{12,16},{16,12},{20,24},{24,20},{5,9},{9,5},{13,17},{1... | collective-permute-start | bytes 786440 | tf_op jit(solution)/shard_map/ppermute | solution.py:42
  33.2 5.9 %collective-permute-start.14 = (f32[5,16,128]{2,1,0:T(8,128)S(1)}, f32[5,16,128]{2,1,0:T(8,128)S(1)}, u32[]{:S(2)}, u32[]{:S(2)}) collective-permute-start(f32[5,16,128]{2,1,0:T(8,128)S(1)} %fusion.4), channel_id=1, source_target_pairs={{0,3},{1,2},{2,1},{3,0},{4,7},{5,6},{6,5},{7,4},{8,11},{9,10},{10,... | collective-permute-start | bytes 122888 | tf_op jit(solution)/shard_map/ppermute | solution.py:46
  36.3 4.9 %collective-permute-start.13 = (f32[5,16,128]{2,1,0:T(8,128)S(1)}, f32[5,16,128]{2,1,0:T(8,128)S(1)}, u32[]{:S(2)}, u32[]{:S(2)}) collective-permute-start(f32[5,16,128]{2,1,0:T(8,128)S(1)} %fusion.4), channel_id=1, source_target_pairs={{0,2},{1,3},{2,0},{3,1},{4,6},{5,7},{6,4},{7,5},{8,10},{9,11},{10,... | collective-permute-start | bytes 122888 | tf_op jit(solution)/shard_map/ppermute | solution.py:46
  38.2 4.0 %collective-permute-start.12 = (f32[5,16,128]{2,1,0:T(8,128)S(1)}, f32[5,16,128]{2,1,0:T(8,128)S(1)}, u32[]{:S(2)}, u32[]{:S(2)}) collective-permute-start(f32[5,16,128]{2,1,0:T(8,128)S(1)} %fusion.4), channel_id=1, source_target_pairs={{0,1},{1,0},{2,3},{3,2},{4,5},{5,4},{6,7},{7,6},{8,9},{9,8},{10,11... | collective-permute-start | bytes 122888 | tf_op jit(solution)/shard_map/ppermute | solution.py:46
  42.2 6.4 %collective-permute-start.17 = (f32[4,16,128]{2,1,0:T(8,128)S(1)}, f32[4,16,128]{2,1,0:T(8,128)S(1)}, u32[]{:S(2)}, u32[]{:S(2)}) collective-permute-start(f32[4,16,128]{2,1,0:T(8,128)S(1)} %fusion.6), channel_id=1, source_target_pairs={{0,24},{4,28},{8,16},{12,20},{16,8},{20,12},{24,0},{28,4},{1,25},{... | collective-permute-start | bytes 98312 | tf_op jit(solution)/shard_map/ppermute | solution.py:46
  56.5 10.1 %collective-permute-start.20 = (f32[256,128]{1,0:T(8,128)S(1)}, f32[256,128]{1,0:T(8,128)S(1)}, u32[]{:S(2)}, u32[]{:S(2)}) collective-permute-start(f32[256,128]{1,0:T(8,128)S(1)} %get-tuple-element.44), channel_id=1, source_target_pairs={{4,8},{8,4},{12,16},{16,12},{20,24},{24,20},{5,9},{9,5},{13,17},{1... | collective-permute-start | bytes 393224 | tf_op jit(solution)/shard_map/ppermute | solution.py:42
  58.0 7.2 %collective-permute-start.23 = (f32[5,16,128]{2,1,0:T(8,128)S(1)}, f32[5,16,128]{2,1,0:T(8,128)S(1)}, u32[]{:S(2)}, u32[]{:S(2)}) collective-permute-start(f32[5,16,128]{2,1,0:T(8,128)S(1)} %get-tuple-element.56), channel_id=1, source_target_pairs={{0,24},{4,28},{8,16},{12,20},{16,8},{20,12},{24,0},{28,4},{1,25},{... | collective-permute-start | bytes 122888 | tf_op jit(solution)/shard_map/ppermute | solution.py:46
  61.6 4.1 %collective-permute-start.22 = (f32[5,16,128]{2,1,0:T(8,128)S(1)}, f32[5,16,128]{2,1,0:T(8,128)S(1)}, u32[]{:S(2)}, u32[]{:S(2)}) collective-permute-start(f32[5,16,128]{2,1,0:T(8,128)S(1)} %get-tuple-element.57), channel_id=1, source_target_pairs={{0,16},{4,20},{8,24},{12,28},{16,0},{20,4},{24,8},{28,12},{1,17},{... | collective-permute-start | bytes 122888 | tf_op jit(solution)/shard_map/ppermute | solution.py:46
  62.0 4.5 %collective-permute-start.21 = (f32[5,16,128]{2,1,0:T(8,128)S(1)}, f32[5,16,128]{2,1,0:T(8,128)S(1)}, u32[]{:S(2)}, u32[]{:S(2)}) collective-permute-start(f32[5,16,128]{2,1,0:T(8,128)S(1)} %get-tuple-element.58), channel_id=1, source_target_pairs={{0,8},{4,12},{8,0},{12,4},{16,24},{20,28},{24,16},{28,20},{1,9},{5... | collective-permute-start | bytes 122888 | tf_op jit(solution)/shard_map/ppermute | solution.py:46
  67.3 9.4 %collective-permute-start.24 = (f32[208,128]{1,0:T(8,128)S(1)}, f32[208,128]{1,0:T(8,128)S(1)}, u32[]{:S(2)}, u32[]{:S(2)}) collective-permute-start(f32[208,128]{1,0:T(8,128)S(1)} %get-tuple-element.47), channel_id=1, source_target_pairs={{0,1},{1,0},{2,3},{3,2},{4,5},{5,4},{6,7},{7,6},{8,9},{9,8},{10,11... | collective-permute-start | bytes 319496 | tf_op jit(solution)/shard_map/ppermute | solution.py:46
  69.0 5.4 %collective-permute-start.26 = (f32[80,128]{1,0:T(8,128)S(1)}, f32[80,128]{1,0:T(8,128)S(1)}, u32[]{:S(2)}, u32[]{:S(2)}) collective-permute-start(f32[80,128]{1,0:T(8,128)S(1)} %bitcast.86), channel_id=1, source_target_pairs={{0,2},{1,3},{2,0},{3,1},{4,6},{5,7},{6,4},{7,5},{8,10},{9,11},{10,... | collective-permute-start | bytes 122888 | tf_op jit(solution)/shard_map/ppermute | solution.py:46
  70.9 5.8 %collective-permute-start.27 = (f32[80,128]{1,0:T(8,128)S(1)}, f32[80,128]{1,0:T(8,128)S(1)}, u32[]{:S(2)}, u32[]{:S(2)}) collective-permute-start(f32[80,128]{1,0:T(8,128)S(1)} %bitcast.87), channel_id=1, source_target_pairs={{0,3},{1,2},{2,1},{3,0},{4,7},{5,6},{6,5},{7,4},{8,11},{9,10},{10,... | collective-permute-start | bytes 122888 | tf_op jit(solution)/shard_map/ppermute | solution.py:46
  71.7 8.6 %collective-permute-start.25 = (f32[128,128]{1,0:T(8,128)S(1)}, f32[128,128]{1,0:T(8,128)S(1)}, u32[]{:S(2)}, u32[]{:S(2)}) collective-permute-start(f32[128,128]{1,0:T(8,128)S(1)} %slice.186), channel_id=1, source_target_pairs={{1,2},{2,1},{5,6},{6,5},{9,10},{10,9},{13,14},{14,13},{17,18},{18,... | collective-permute-start | bytes 196616 | tf_op jit(solution)/shard_map/ppermute | solution.py:42
  76.8 5.1 %collective-permute-start.30 = (f32[4,16,128]{2,1,0:T(8,128)S(1)}, f32[4,16,128]{2,1,0:T(8,128)S(1)}, u32[]{:S(2)}, u32[]{:S(2)}) collective-permute-start(f32[4,16,128]{2,1,0:T(8,128)S(1)} %divide_subtract_fusion), channel_id=1, source_target_pairs={{0,24},{4,28},{8,16},{12,20},{16,8},{20,12},{24,0},{28,4},{1,25},{... | collective-permute-start | bytes 98312 | tf_op jit(solution)/shard_map/ppermute | solution.py:46
  (13 other events, 44.3 us)

commit v4 on v3

--- a/solution.py
+++ b/solution.py
@@ -35,11 +35,26 @@
 
 
 def swapped(values, axis, odd):
-    count = lax.axis_size(axis)
+    if not odd:
+        return lax.ppermute(values, axis, [(i, i ^ 1) for i in range(lax.axis_size(axis))])
+    rows, cols = lax.axis_size("sy"), lax.axis_size("sx")
     pairs = []
-    for first in range(1 if odd else 0, count - 1, 2):
-        pairs += [(first, first + 1), (first + 1, first)]
-    return lax.ppermute(values, axis, pairs)
+    for row in range(rows):
+        for col in range(cols):
+            to_row, to_col = row, col
+            if axis == "sy":
+                to_row = (row + 1 if row % 2 else row - 1) % rows
+            elif 0 < col < cols - 1:
+                to_col = col + 1 if col % 2 else col - 1
+            else:
+                to_row = row ^ 1
+            pairs.append((row * cols + col, to_row * cols + to_col))
+    return lax.ppermute(values, ("sy", "sx"), pairs)
+
+
+def partnered(received, axis):
+    at = lax.axis_index(axis)
+    return jnp.where((at == 0) | (at == lax.axis_size(axis) - 1), 0.0, received)
 
 
 def flipped(values, axis, bits):
@@ -346,7 +361,7 @@
     near, far = jnp.where(odd_row, upper, lower), jnp.where(odd_row, lower, upper)
     own = jnp.pad((after(offs, near, far) + 1).astype(jnp.float32), ((0, 6), (0, lanes - offs.shape[1])))
     near, far = jnp.concatenate([near, own]), jnp.concatenate([far, own])
-    rows_near, rows_far = swapped(near, "sy", False), swapped(far, "sy", True)
+    rows_near, rows_far = swapped(near, "sy", False), partnered(swapped(far, "sy", True), "sy")
     side = after(tile, near, far)
     left = jnp.concatenate([side[0, :, :halo], side[1, :, :halo]], axis=1)
     right = jnp.concatenate([side[0, :, halo:], side[1, :, halo:]], axis=1)
@@ -364,7 +379,7 @@
         return jnp.concatenate([ends[0], middle, ends[1], reach])
 
     cols_near = swapped(columns_of(left, odd_col), "sx", False)
-    cols_far = swapped(columns_of(right, ~odd_col), "sx", True)
+    cols_far = partnered(swapped(columns_of(right, ~odd_col), "sx", True), "sx")
     return rows_near, rows_far, cols_near, cols_far, reach
 
 
@@ -451,23 +466,24 @@
         scale = light(probe, after(corners, both))
         if not final:
             side_a = given[0] + swapped(given[0], "sx", False)
-            side_b = given[1] + swapped(given[1], "sx", True)
+            side_b = given[1] + partnered(swapped(given[1], "sx", True), "sx")
             near, far = jnp.stack([side_a[0], side_b[0]]), jnp.stack([side_a[1], side_b[1]])
             near = near + swapped(near, "sy", False)
-            far = far + swapped(far, "sy", True)
+            far = far + partnered(swapped(far, "sy", True), "sy")
             total = after(chip_sum(both), near, scale)
             chunk = after(probe_fresh(across(total, 1), chunk), near, far)
         else:
             own_rows, far = given
             far = swapped(far, "sy", True)
             total = after(chip_sum(both), far, scale).reshape(-1, extent)
+            far = partnered(after(far, total), "sy")
             message = f32(total.shape[0] + tile, tile)
             middle, near, far = kernel_call(
                 middle_kernel, (f32(2, tile, tile), message, message), (scal, own_rows, received, far, total), scalars=1
             )
             head = total.shape[0]
             near = flipped(near, "sx", 1)
-            far = swapped(far[head:], "sx", True)
+            far = partnered(swapped(far[head:], "sx", True), "sx")
             parts = across(total, 2)
             parts.insert(1, near[:head])
             chunk = probe_fresh(parts, chunk)

time: 86.5 us -> 78.4 us (0.906)
  starting transfers between devices: 43.6 us -> 37.7 us
  waiting for transfers between devices: 24.2 us -> 22.2 us
    ppermute x18, waiting for transfers between devices: 15.6 us -> 10.6 us  [flipped(): lax.ppermute(values, axis, [(i, i ^ bits) for i in range(lax.axis_size(ax...]
    ppermute x18, starting transfers between devices: 28.1 us -> 23.1 us  [flipped(): lax.ppermute(values, axis, [(i, i ^ bits) for i in range(lax.axis_size(ax...]
    ppermute x14, waiting for transfers between devices: 8.58 us -> 11.6 us  [the longest x8 7.11 us: swapped(): lax.ppermute(values, axis, [(i, i ^ 1) for i in range(lax.axis_size(axis))])]
    ppermute x14, starting transfers between devices: 15.5 us -> 14.6 us  [the longest x6 7.51 us: swapped(): return lax.ppermute(values, ('sy', 'sx'), pairs)]
  transfers between devices with their start and end apart: 32 -> 32, of which waited for: 21 -> 17; matrix products, arithmetic and copies ran while one was open for 1% -> 1% of each run, Pallas kernels for 5% -> 6%
where the time goes in v4:
time: 78.4 us; the launch traced here: 78.3 us
  starting transfers between devices  37.7 us (48%)
  waiting for transfers between devices  22.2 us (28%)
  Pallas kernels  14.1 us (18%)
  other arithmetic  1.98 us (3%)
  local copies, waits for them, and re-layouts  1.17 us (1%)
  between operations  1.1 us (1%)
    ppermute x18, starting transfers between devices, flipped(): lax.ppermute(values, axis, [(i, i ^ bits) for i in range(lax.axis_size(ax...  23.1 us
    pallas_call x7, Pallas kernels, kernel_call(): pl.pallas_call(body, out_shape=outs, in_specs=[SMEM] * scalars + [VMEM] *...  14.1 us
    ppermute x18, waiting for transfers between devices, flipped(): lax.ppermute(values, axis, [(i, i ^ bits) for i in range(lax.axis_size(ax...  10.6 us
    ppermute x6, starting transfers between devices, swapped(): return lax.ppermute(values, ('sy', 'sx'), pairs)  7.51 us
    ppermute x8, waiting for transfers between devices, swapped(): lax.ppermute(values, axis, [(i, i ^ 1) for i in range(lax.axis_size(axis))])  7.11 us
    ppermute x8, starting transfers between devices, swapped(): lax.ppermute(values, axis, [(i, i ^ 1) for i in range(lax.axis_size(axis))])  7.09 us
    ppermute x6, waiting for transfers between devices, swapped(): return lax.ppermute(values, ('sy', 'sx'), pairs)  4.46 us
  transfers between devices with their start and end apart: 32, of which 17 were waited for; matrix products, arithmetic and copies ran while one was open for 1% of the time, Pallas kernels for 6%

profile of v4, /device:TPU:0, one launch (start us, length us, event | category | flops | bytes accessed | tf_op | source)
XLA Modules:
  0.0 78.3 jit_solution(13749003658339615253)
XLA Ops:
  2.3 3.4 %collective-permute-start.1 = (f32[136,128]{1,0:T(8,128)S(1)}, f32[136,128]{1,0:T(8,128)S(1)}, u32[]{:S(2)}, u32[]{:S(2)}) collective-permute-start(f32[136,128]{1,0:T(8,128)S(1)} %get-tuple-element.82), channel_id=1, source_target_pairs={{0,28},{1,29},{2,30},{3,31},{4,8},{5,9},{6,10},{7,11},{8,4},{9,5},... | collective-permute-start | bytes 208904 | tf_op jit(solution)/shard_map/ppermute | solution.py:52
  6.0 1.7 %collective-permute-done.1 = f32[136,128]{1,0:T(8,128)S(1)} collective-permute-done((f32[136,128]{1,0:T(8,128)S(1)}, f32[136,128]{1,0:T(8,128)S(1)}, u32[]{:S(2)}, u32[]{:S(2)}) %collective-permute-start.1) | collective-permute-done | bytes 69664 | tf_op jit(solution)/shard_map/ppermute | solution.py:52
  8.3 4.6 %collective-permute-start.2 = (f32[264,128]{1,0:T(8,128)S(1)}, f32[264,128]{1,0:T(8,128)S(1)}, u32[]{:S(2)}, u32[]{:S(2)}) collective-permute-start(f32[264,128]{1,0:T(8,128)S(1)} %concatenate.45), channel_id=1, source_target_pairs={{0,1},{1,0},{2,3},{3,2},{4,5},{5,4},{6,7},{7,6},{8,9},{9,8},{10,11... | collective-permute-start | bytes 405512 | tf_op jit(solution)/shard_map/ppermute | solution.py:39
  13.0 2.9 %collective-permute-done.2.cols_near = f32[264,128]{1,0:T(8,128)S(1)} collective-permute-done((f32[264,128]{1,0:T(8,128)S(1)}, f32[264,128]{1,0:T(8,128)S(1)}, u32[]{:S(2)}, u32[]{:S(2)}) %collective-permute-start.2) | collective-permute-done | bytes 135200 | tf_op jit(solution)/shard_map/ppermute | solution.py:39
  15.9 4.0 %shard_map.68 = (f32[24,128]{1,0:T(8,128)S(1)}, f32[2,2,128,128]{3,2,1,0:T(8,128)S(1)}, f32[2,2,128,128]{3,2,1,0:T(8,128)S(1)}, f32[4,5,16,128]{3,2,1,0:T(8,128)...) custom-call(s32[7]{0:T(128)S(1)} %stack.75.scal, s32[2,4]{1,0:T(2,128)S(1)} %bitcast.90, ...), custom_call_target="tpu_custom_call" | custom-call | flops 1610612736 | bytes 1048576 | tf_op jit(solution)/shard_map/pallas_call | solution.py:346
  20.2 2.0 %collective-permute-start.5 = (f32[2,2,128,128]{3,2,1,0:T(8,128)S(1)}, f32[2,2,128,128]{3,2,1,0:T(8,128)S(1)}, u32[]{:S(2)}, u32[]{:S(2)}) collective-permute-start(f32[2,2,128,128]{3,2,1,0:T(8,128)S(1)} %get-tuple-element.35), channel_id=1, source_target_pairs={{0,1},{1,0},{2,3},{3,2},{4,5},{5,4},{6,7},{7,6},{8,9},{9,8},{10,11... | collective-permute-start | bytes 786440 | tf_op jit(solution)/shard_map/ppermute | solution.py:39
  22.6 1.9 %collective-permute-start.11 = (f32[5,16,128]{2,1,0:T(8,128)S(1)}, f32[5,16,128]{2,1,0:T(8,128)S(1)}, u32[]{:S(2)}, u32[]{:S(2)}) collective-permute-start(f32[5,16,128]{2,1,0:T(8,128)S(1)} %get-tuple-element.63), channel_id=1, source_target_pairs={{0,24},{4,28},{8,16},{12,20},{16,8},{20,12},{24,0},{28,4},{1,25},{... | collective-permute-start | bytes 122888 | tf_op jit(solution)/shard_map/ppermute | solution.py:61
  26.1 1.5 %shard_map.69.scale_ref = f32[2,256,128]{2,1,0:T(8,128)S(1)} custom-call(s32[7]{0:T(128)S(1)} %stack.75.scal, s32[9,2,4]{2,1,0:T(2,128)S(1)} %compare_select_fusion.corners, f32[2,2,128,128]{3,2,1,0:T(8,128)S(1)} %copy-done.1), custom_call_target="tpu_custom_call" | custom-call | flops 805306368 | bytes 1048576 | tf_op jit(solution)/shard_map/pallas_call | solution.py:346
  27.6 1.5 %collective-permute-done.5 = f32[2,2,128,128]{3,2,1,0:T(8,128)S(1)} collective-permute-done((f32[2,2,128,128]{3,2,1,0:T(8,128)S(1)}, f32[2,2,128,128]{3,2,1,0:T(8,128)S(1)}, u32[]{:S(2)}, u32[]{:S(2)}) %collective-permute-start.5) | collective-permute-done | bytes 262176 | tf_op jit(solution)/shard_map/ppermute | solution.py:39
  29.4 2.0 %collective-permute-start.8 = (f32[2,2,128,128]{3,2,1,0:T(8,128)S(1)}, f32[2,2,128,128]{3,2,1,0:T(8,128)S(1)}, u32[]{:S(2)}, u32[]{:S(2)}) collective-permute-start(f32[2,2,128,128]{3,2,1,0:T(8,128)S(1)} %pad_maximum_fusion.1), channel_id=1, source_target_pairs={{0,28},{1,29},{2,30},{3,31},{4,8},{5,9},{6,10},{7,11},{8,4},{9,5},... | collective-permute-start | bytes 786440 | tf_op jit(solution)/shard_map/ppermute | solution.py:52
  31.5 3.0 %collective-permute-start.14 = (f32[5,16,128]{2,1,0:T(8,128)S(1)}, f32[5,16,128]{2,1,0:T(8,128)S(1)}, u32[]{:S(2)}, u32[]{:S(2)}) collective-permute-start(f32[5,16,128]{2,1,0:T(8,128)S(1)} %fusion.4), channel_id=1, source_target_pairs={{0,3},{1,2},{2,1},{3,0},{4,7},{5,6},{6,5},{7,4},{8,11},{9,10},{10,... | collective-permute-start | bytes 122888 | tf_op jit(solution)/shard_map/ppermute | solution.py:61
  35.9 2.8 %collective-permute-done.8 = f32[2,2,128,128]{3,2,1,0:T(8,128)S(1)} collective-permute-done((f32[2,2,128,128]{3,2,1,0:T(8,128)S(1)}, f32[2,2,128,128]{3,2,1,0:T(8,128)S(1)}, u32[]{:S(2)}, u32[]{:S(2)}) %collective-permute-start.8) | collective-permute-done | bytes 262176 | tf_op jit(solution)/shard_map/ppermute | solution.py:52
  41.8 1.7 %collective-permute-start.15 = (f32[4,16,128]{2,1,0:T(8,128)S(1)}, f32[4,16,128]{2,1,0:T(8,128)S(1)}, u32[]{:S(2)}, u32[]{:S(2)}) collective-permute-start(f32[4,16,128]{2,1,0:T(8,128)S(1)} %fusion.6), channel_id=1, source_target_pairs={{0,8},{4,12},{8,0},{12,4},{16,24},{20,28},{24,16},{28,20},{1,9},{5... | collective-permute-start | bytes 98312 | tf_op jit(solution)/shard_map/ppermute | solution.py:61
  47.1 3.8 %shard_map.70 = (f32[2,2,128,128]{3,2,1,0:T(8,128)S(1)}, f32[256,128]{1,0:T(8,128)S(1)}, f32[4,5,16,128]{3,2,1,0:T(8,128)S(1)}, f32[576,128]{1,0:T(8,128)S(1)}, ...) custom-call(s32[7]{0:T(128)S(1)} %stack.75.scal, s32[2,4]{1,0:T(2,128)S(1)} %bitcast.91, ...), custom_call_target="tpu_custom_call" | custom-call | flops 1610612736 | bytes 1048576 | tf_op jit(solution)/shard_map/pallas_call | solution.py:346
  51.2 1.8 %collective-permute-start.20 = (f32[256,128]{1,0:T(8,128)S(1)}, f32[256,128]{1,0:T(8,128)S(1)}, u32[]{:S(2)}, u32[]{:S(2)}) collective-permute-start(f32[256,128]{1,0:T(8,128)S(1)} %get-tuple-element.45), channel_id=1, source_target_pairs={{0,28},{1,29},{2,30},{3,31},{4,8},{5,9},{6,10},{7,11},{8,4},{9,5},... | collective-permute-start | bytes 393224 | tf_op jit(solution)/shard_map/ppermute | solution.py:52
  53.0 1.5 %collective-permute-start.23 = (f32[5,16,128]{2,1,0:T(8,128)S(1)}, f32[5,16,128]{2,1,0:T(8,128)S(1)}, u32[]{:S(2)}, u32[]{:S(2)}) collective-permute-start(f32[5,16,128]{2,1,0:T(8,128)S(1)} %get-tuple-element.60), channel_id=1, source_target_pairs={{0,24},{4,28},{8,16},{12,20},{16,8},{20,12},{24,0},{28,4},{1,25},{... | collective-permute-start | bytes 122888 | tf_op jit(solution)/shard_map/ppermute | solution.py:61
  56.6 1.5 %shard_map.71.scale_ref = f32[2,256,128]{2,1,0:T(8,128)S(1)} custom-call(s32[7]{0:T(128)S(1)} %stack.75.scal, s32[9,2,4]{2,1,0:T(2,128)S(1)} %compare_select_fusion.corners, f32[2,2,128,128]{3,2,1,0:T(8,128)S(1)} %get-tuple-element.43.probe_ref), custom_call_target="tpu_custom_call" | custom-call | flops 805306368 | bytes 1048576 | tf_op jit(solution)/shard_map/pallas_call | solution.py:346
  60.6 1.4 %collective-permute-start.24 = (f32[208,128]{1,0:T(8,128)S(1)}, f32[208,128]{1,0:T(8,128)S(1)}, u32[]{:S(2)}, u32[]{:S(2)}) collective-permute-start(f32[208,128]{1,0:T(8,128)S(1)} %get-tuple-element.49), channel_id=1, source_target_pairs={{0,1},{1,0},{2,3},{3,2},{4,5},{5,4},{6,7},{7,6},{8,9},{9,8},{10,11... | collective-permute-start | bytes 319496 | tf_op jit(solution)/shard_map/ppermute | solution.py:61
  61.9 1.5 %collective-permute-start.26 = (f32[80,128]{1,0:T(8,128)S(1)}, f32[80,128]{1,0:T(8,128)S(1)}, u32[]{:S(2)}, u32[]{:S(2)}) collective-permute-start(f32[80,128]{1,0:T(8,128)S(1)} %bitcast.86), channel_id=1, source_target_pairs={{0,2},{1,3},{2,0},{3,1},{4,6},{5,7},{6,4},{7,5},{8,10},{9,11},{10,... | collective-permute-start | bytes 122888 | tf_op jit(solution)/shard_map/ppermute | solution.py:61
  63.5 1.6 %collective-permute-start.27 = (f32[80,128]{1,0:T(8,128)S(1)}, f32[80,128]{1,0:T(8,128)S(1)}, u32[]{:S(2)}, u32[]{:S(2)}) collective-permute-start(f32[80,128]{1,0:T(8,128)S(1)} %bitcast.87), channel_id=1, source_target_pairs={{0,3},{1,2},{2,1},{3,0},{4,7},{5,6},{6,5},{7,4},{8,11},{9,10},{10,... | collective-permute-start | bytes 122888 | tf_op jit(solution)/shard_map/ppermute | solution.py:61
  65.1 2.6 %collective-permute-done.26 = f32[80,128]{1,0:T(8,128)S(1)} collective-permute-done((f32[80,128]{1,0:T(8,128)S(1)}, f32[80,128]{1,0:T(8,128)S(1)}, u32[]{:S(2)}, u32[]{:S(2)}) %collective-permute-start.26) | collective-permute-done | bytes 40992 | tf_op jit(solution)/shard_map/ppermute | solution.py:61
  67.6 1.8 %collective-permute-done.27 = f32[80,128]{1,0:T(8,128)S(1)} collective-permute-done((f32[80,128]{1,0:T(8,128)S(1)}, f32[80,128]{1,0:T(8,128)S(1)}, u32[]{:S(2)}, u32[]{:S(2)}) %collective-permute-start.27) | collective-permute-done | bytes 40992 | tf_op jit(solution)/shard_map/ppermute | solution.py:61
  69.5 1.5 %collective-permute-start.30 = (f32[4,16,128]{2,1,0:T(8,128)S(1)}, f32[4,16,128]{2,1,0:T(8,128)S(1)}, u32[]{:S(2)}, u32[]{:S(2)}) collective-permute-start(f32[4,16,128]{2,1,0:T(8,128)S(1)} %divide_subtract_fusion), channel_id=1, source_target_pairs={{0,24},{4,28},{8,16},{12,20},{16,8},{20,12},{24,0},{28,4},{1,25},{... | collective-permute-start | bytes 98312 | tf_op jit(solution)/shard_map/ppermute | solution.py:61
  73.0 1.4 %shard_map.73 = f32[2,128,128]{2,1,0:T(8,128)} custom-call(s32[7]{0:T(128)S(1)} %stack.75.scal, f32[2,2,256,128]{3,2,1,0:T(8,128)S(1)} %get-tuple-element.39.old_ref, f32[2,256,128]{2,1,0:T(8,128)S(1)} %shard_map.71.scale_ref, f32[2,128,128]{2,1,0:T(8,128)S(1)} %get-tuple-element.48.middle_ref, f32[208,128]{1,0:T(8,128)S(1)} %collective-permute-done.24.near_ref, ...), custom_call_target="tpu_custom_call" | custom-call | bytes 1048576 | tf_op jit(solution)/shard_map/pallas_call | solution.py:346
  (119 shorter events, 23.8 us)
Async XLA Ops:
  2.3 5.4 %collective-permute-start.1 = (f32[136,128]{1,0:T(8,128)S(1)}, f32[136,128]{1,0:T(8,128)S(1)}, u32[]{:S(2)}, u32[]{:S(2)}) collective-permute-start(f32[136,128]{1,0:T(8,128)S(1)} %get-tuple-element.82), channel_id=1, source_target_pairs={{0,28},{1,29},{2,30},{3,31},{4,8},{5,9},{6,10},{7,11},{8,4},{9,5},... | collective-permute-start | bytes 208904 | tf_op jit(solution)/shard_map/ppermute | solution.py:52
  8.1 4.9 %collective-permute-start.3 = (f32[264,128]{1,0:T(8,128)S(1)}, f32[264,128]{1,0:T(8,128)S(1)}, u32[]{:S(2)}, u32[]{:S(2)}) collective-permute-start(f32[264,128]{1,0:T(8,128)S(1)} %concatenate.48), channel_id=1, source_target_pairs={{0,4},{1,2},{2,1},{3,7},{4,0},{5,6},{6,5},{7,3},{8,12},{9,10},{10,... | collective-permute-start | bytes 405512 | tf_op jit(solution)/shard_map/ppermute | solution.py:52
  8.3 7.6 %collective-permute-start.2 = (f32[264,128]{1,0:T(8,128)S(1)}, f32[264,128]{1,0:T(8,128)S(1)}, u32[]{:S(2)}, u32[]{:S(2)}) collective-permute-start(f32[264,128]{1,0:T(8,128)S(1)} %concatenate.45), channel_id=1, source_target_pairs={{0,1},{1,0},{2,3},{3,2},{4,5},{5,4},{6,7},{7,6},{8,9},{9,8},{10,11... | collective-permute-start | bytes 405512 | tf_op jit(solution)/shard_map/ppermute | solution.py:39
  20.2 8.9 %collective-permute-start.5 = (f32[2,2,128,128]{3,2,1,0:T(8,128)S(1)}, f32[2,2,128,128]{3,2,1,0:T(8,128)S(1)}, u32[]{:S(2)}, u32[]{:S(2)}) collective-permute-start(f32[2,2,128,128]{3,2,1,0:T(8,128)S(1)} %get-tuple-element.35), channel_id=1, source_target_pairs={{0,1},{1,0},{2,3},{3,2},{4,5},{5,4},{6,7},{7,6},{8,9},{9,8},{10,11... | collective-permute-start | bytes 786440 | tf_op jit(solution)/shard_map/ppermute | solution.py:39
  22.1 7.0 %collective-permute-start.6 = (f32[2,2,128,128]{3,2,1,0:T(8,128)S(1)}, f32[2,2,128,128]{3,2,1,0:T(8,128)S(1)}, u32[]{:S(2)}, u32[]{:S(2)}) collective-permute-start(f32[2,2,128,128]{3,2,1,0:T(8,128)S(1)} %get-tuple-element.36), channel_id=1, source_target_pairs={{0,4},{1,2},{2,1},{3,7},{4,0},{5,6},{6,5},{7,3},{8,12},{9,10},{10,... | collective-permute-start | bytes 786440 | tf_op jit(solution)/shard_map/ppermute | solution.py:52
  22.6 8.8 %collective-permute-start.11 = (f32[5,16,128]{2,1,0:T(8,128)S(1)}, f32[5,16,128]{2,1,0:T(8,128)S(1)}, u32[]{:S(2)}, u32[]{:S(2)}) collective-permute-start(f32[5,16,128]{2,1,0:T(8,128)S(1)} %get-tuple-element.63), channel_id=1, source_target_pairs={{0,24},{4,28},{8,16},{12,20},{16,8},{20,12},{24,0},{28,4},{1,25},{... | collective-permute-start | bytes 122888 | tf_op jit(solution)/shard_map/ppermute | solution.py:61
  24.5 6.9 %collective-permute-start.10 = (f32[5,16,128]{2,1,0:T(8,128)S(1)}, f32[5,16,128]{2,1,0:T(8,128)S(1)}, u32[]{:S(2)}, u32[]{:S(2)}) collective-permute-start(f32[5,16,128]{2,1,0:T(8,128)S(1)} %get-tuple-element.64), channel_id=1, source_target_pairs={{0,16},{4,20},{8,24},{12,28},{16,0},{20,4},{24,8},{28,12},{1,17},{... | collective-permute-start | bytes 122888 | tf_op jit(solution)/shard_map/ppermute | solution.py:61
  25.3 6.1 %collective-permute-start.9 = (f32[5,16,128]{2,1,0:T(8,128)S(1)}, f32[5,16,128]{2,1,0:T(8,128)S(1)}, u32[]{:S(2)}, u32[]{:S(2)}) collective-permute-start(f32[5,16,128]{2,1,0:T(8,128)S(1)} %get-tuple-element.65), channel_id=1, source_target_pairs={{0,8},{4,12},{8,0},{12,4},{16,24},{20,28},{24,16},{28,20},{1,9},{5... | collective-permute-start | bytes 122888 | tf_op jit(solution)/shard_map/ppermute | solution.py:61
  29.4 9.3 %collective-permute-start.8 = (f32[2,2,128,128]{3,2,1,0:T(8,128)S(1)}, f32[2,2,128,128]{3,2,1,0:T(8,128)S(1)}, u32[]{:S(2)}, u32[]{:S(2)}) collective-permute-start(f32[2,2,128,128]{3,2,1,0:T(8,128)S(1)} %pad_maximum_fusion.1), channel_id=1, source_target_pairs={{0,28},{1,29},{2,30},{3,31},{4,8},{5,9},{6,10},{7,11},{8,4},{9,5},... | collective-permute-start | bytes 786440 | tf_op jit(solution)/shard_map/ppermute | solution.py:52
  31.5 7.3 %collective-permute-start.14 = (f32[5,16,128]{2,1,0:T(8,128)S(1)}, f32[5,16,128]{2,1,0:T(8,128)S(1)}, u32[]{:S(2)}, u32[]{:S(2)}) collective-permute-start(f32[5,16,128]{2,1,0:T(8,128)S(1)} %fusion.4), channel_id=1, source_target_pairs={{0,3},{1,2},{2,1},{3,0},{4,7},{5,6},{6,5},{7,4},{8,11},{9,10},{10,... | collective-permute-start | bytes 122888 | tf_op jit(solution)/shard_map/ppermute | solution.py:61
  34.5 5.3 %collective-permute-start.13 = (f32[5,16,128]{2,1,0:T(8,128)S(1)}, f32[5,16,128]{2,1,0:T(8,128)S(1)}, u32[]{:S(2)}, u32[]{:S(2)}) collective-permute-start(f32[5,16,128]{2,1,0:T(8,128)S(1)} %fusion.4), channel_id=1, source_target_pairs={{0,2},{1,3},{2,0},{3,1},{4,6},{5,7},{6,4},{7,5},{8,10},{9,11},{10,... | collective-permute-start | bytes 122888 | tf_op jit(solution)/shard_map/ppermute | solution.py:61
  35.0 4.9 %collective-permute-start.12 = (f32[5,16,128]{2,1,0:T(8,128)S(1)}, f32[5,16,128]{2,1,0:T(8,128)S(1)}, u32[]{:S(2)}, u32[]{:S(2)}) collective-permute-start(f32[5,16,128]{2,1,0:T(8,128)S(1)} %fusion.4), channel_id=1, source_target_pairs={{0,1},{1,0},{2,3},{3,2},{4,5},{5,4},{6,7},{7,6},{8,9},{9,8},{10,11... | collective-permute-start | bytes 122888 | tf_op jit(solution)/shard_map/ppermute | solution.py:61
  39.9 4.9 %collective-permute-start.17 = (f32[4,16,128]{2,1,0:T(8,128)S(1)}, f32[4,16,128]{2,1,0:T(8,128)S(1)}, u32[]{:S(2)}, u32[]{:S(2)}) collective-permute-start(f32[4,16,128]{2,1,0:T(8,128)S(1)} %fusion.6), channel_id=1, source_target_pairs={{0,24},{4,28},{8,16},{12,20},{16,8},{20,12},{24,0},{28,4},{1,25},{... | collective-permute-start | bytes 98312 | tf_op jit(solution)/shard_map/ppermute | solution.py:61
  41.1 4.1 %collective-permute-start.16 = (f32[4,16,128]{2,1,0:T(8,128)S(1)}, f32[4,16,128]{2,1,0:T(8,128)S(1)}, u32[]{:S(2)}, u32[]{:S(2)}) collective-permute-start(f32[4,16,128]{2,1,0:T(8,128)S(1)} %fusion.6), channel_id=1, source_target_pairs={{0,16},{4,20},{8,24},{12,28},{16,0},{20,4},{24,8},{28,12},{1,17},{... | collective-permute-start | bytes 98312 | tf_op jit(solution)/shard_map/ppermute | solution.py:61
  41.8 3.9 %collective-permute-start.15 = (f32[4,16,128]{2,1,0:T(8,128)S(1)}, f32[4,16,128]{2,1,0:T(8,128)S(1)}, u32[]{:S(2)}, u32[]{:S(2)}) collective-permute-start(f32[4,16,128]{2,1,0:T(8,128)S(1)} %fusion.6), channel_id=1, source_target_pairs={{0,8},{4,12},{8,0},{12,4},{16,24},{20,28},{24,16},{28,20},{1,9},{5... | collective-permute-start | bytes 98312 | tf_op jit(solution)/shard_map/ppermute | solution.py:61
  51.2 8.7 %collective-permute-start.20 = (f32[256,128]{1,0:T(8,128)S(1)}, f32[256,128]{1,0:T(8,128)S(1)}, u32[]{:S(2)}, u32[]{:S(2)}) collective-permute-start(f32[256,128]{1,0:T(8,128)S(1)} %get-tuple-element.45), channel_id=1, source_target_pairs={{0,28},{1,29},{2,30},{3,31},{4,8},{5,9},{6,10},{7,11},{8,4},{9,5},... | collective-permute-start | bytes 393224 | tf_op jit(solution)/shard_map/ppermute | solution.py:52
  53.0 6.0 %collective-permute-start.23 = (f32[5,16,128]{2,1,0:T(8,128)S(1)}, f32[5,16,128]{2,1,0:T(8,128)S(1)}, u32[]{:S(2)}, u32[]{:S(2)}) collective-permute-start(f32[5,16,128]{2,1,0:T(8,128)S(1)} %get-tuple-element.60), channel_id=1, source_target_pairs={{0,24},{4,28},{8,16},{12,20},{16,8},{20,12},{24,0},{28,4},{1,25},{... | collective-permute-start | bytes 122888 | tf_op jit(solution)/shard_map/ppermute | solution.py:61
  54.6 4.6 %collective-permute-start.22 = (f32[5,16,128]{2,1,0:T(8,128)S(1)}, f32[5,16,128]{2,1,0:T(8,128)S(1)}, u32[]{:S(2)}, u32[]{:S(2)}) collective-permute-start(f32[5,16,128]{2,1,0:T(8,128)S(1)} %get-tuple-element.61), channel_id=1, source_target_pairs={{0,16},{4,20},{8,24},{12,28},{16,0},{20,4},{24,8},{28,12},{1,17},{... | collective-permute-start | bytes 122888 | tf_op jit(solution)/shard_map/ppermute | solution.py:61
  55.8 4.0 %collective-permute-start.21 = (f32[5,16,128]{2,1,0:T(8,128)S(1)}, f32[5,16,128]{2,1,0:T(8,128)S(1)}, u32[]{:S(2)}, u32[]{:S(2)}) collective-permute-start(f32[5,16,128]{2,1,0:T(8,128)S(1)} %get-tuple-element.62), channel_id=1, source_target_pairs={{0,8},{4,12},{8,0},{12,4},{16,24},{20,28},{24,16},{28,20},{1,9},{5... | collective-permute-start | bytes 122888 | tf_op jit(solution)/shard_map/ppermute | solution.py:61
  60.6 8.8 %collective-permute-start.24 = (f32[208,128]{1,0:T(8,128)S(1)}, f32[208,128]{1,0:T(8,128)S(1)}, u32[]{:S(2)}, u32[]{:S(2)}) collective-permute-start(f32[208,128]{1,0:T(8,128)S(1)} %get-tuple-element.49), channel_id=1, source_target_pairs={{0,1},{1,0},{2,3},{3,2},{4,5},{5,4},{6,7},{7,6},{8,9},{9,8},{10,11... | collective-permute-start | bytes 319496 | tf_op jit(solution)/shard_map/ppermute | solution.py:61
  61.9 5.7 %collective-permute-start.26 = (f32[80,128]{1,0:T(8,128)S(1)}, f32[80,128]{1,0:T(8,128)S(1)}, u32[]{:S(2)}, u32[]{:S(2)}) collective-permute-start(f32[80,128]{1,0:T(8,128)S(1)} %bitcast.86), channel_id=1, source_target_pairs={{0,2},{1,3},{2,0},{3,1},{4,6},{5,7},{6,4},{7,5},{8,10},{9,11},{10,... | collective-permute-start | bytes 122888 | tf_op jit(solution)/shard_map/ppermute | solution.py:61
  63.5 5.9 %collective-permute-start.27 = (f32[80,128]{1,0:T(8,128)S(1)}, f32[80,128]{1,0:T(8,128)S(1)}, u32[]{:S(2)}, u32[]{:S(2)}) collective-permute-start(f32[80,128]{1,0:T(8,128)S(1)} %bitcast.87), channel_id=1, source_target_pairs={{0,3},{1,2},{2,1},{3,0},{4,7},{5,6},{6,5},{7,4},{8,11},{9,10},{10,... | collective-permute-start | bytes 122888 | tf_op jit(solution)/shard_map/ppermute | solution.py:61
  65.0 8.0 %collective-permute-start.25 = (f32[128,128]{1,0:T(8,128)S(1)}, f32[128,128]{1,0:T(8,128)S(1)}, u32[]{:S(2)}, u32[]{:S(2)}) collective-permute-start(f32[128,128]{1,0:T(8,128)S(1)} %slice.186), channel_id=1, source_target_pairs={{0,4},{1,2},{2,1},{3,7},{4,0},{5,6},{6,5},{7,3},{8,12},{9,10},{10,... | collective-permute-start | bytes 196616 | tf_op jit(solution)/shard_map/ppermute | solution.py:52
  69.5 5.0 %collective-permute-start.30 = (f32[4,16,128]{2,1,0:T(8,128)S(1)}, f32[4,16,128]{2,1,0:T(8,128)S(1)}, u32[]{:S(2)}, u32[]{:S(2)}) collective-permute-start(f32[4,16,128]{2,1,0:T(8,128)S(1)} %divide_subtract_fusion), channel_id=1, source_target_pairs={{0,24},{4,28},{8,16},{12,20},{16,8},{20,12},{24,0},{28,4},{1,25},{... | collective-permute-start | bytes 98312 | tf_op jit(solution)/shard_map/ppermute | solution.py:61
  (13 other events, 46.6 us)

commit v5 on v4

--- a/solution.py
+++ b/solution.py
@@ -138,7 +138,7 @@
     w2 = (table_ref[2], table_ref[3])
     grad[...] = jnp.zeros_like(grad)
     lane = lax.broadcasted_iota(jnp.int32, (extent, extent), 1)
-    group = positions // 2
+    group = positions
     for first in range(0, positions, group):
         span = range(first, min(first + group, positions))
         patches = []
@@ -245,11 +245,10 @@
             outs[1][at : at + halo, :] = grad[plane, side, pl.ds(outer[1], halo), :]
 
 
-def middle_kernel(scal, own_ref, near_ref, far_ref, total_ref, middle_ref, near_out, far_out):
+def middle_kernel(scal, own_ref, near_ref, far_ref, middle_ref, near_out, far_out):
     planes, sides, extent, _ = own_ref.shape
     halo = extent // 2
     base = near_ref.shape[0] - planes * sides * halo
-    head = total_ref.shape[0]
     odd_row, odd_col = scal[0] == 1, scal[1] == 1
     lane = lax.broadcasted_iota(jnp.int32, (extent, extent), 1)
     rims = []
@@ -264,9 +263,8 @@
         middle_ref[plane] = jnp.where(lane < halo, turned[0], turned[1])
         rims.append((rows[0], turned[1]) if plane == 0 else (turned[0], rows[1]))
     left, right = (jnp.where(lane < halo, rims[0][side], rims[1][side]) for side in range(sides))
-    for ref, rim in ((near_out, jnp.where(odd_col, left, right)), (far_out, jnp.where(odd_col, right, left))):
-        ref[:head, :] = total_ref[...]
-        ref[head:, :] = rim
+    near_out[...] = jnp.where(odd_col, left, right)
+    far_out[...] = jnp.where(odd_col, right, left)
 
 
 def object_kernel(scal, old_ref, scale_ref, middle_ref, near_ref, far_ref, object_ref):
@@ -280,7 +278,7 @@
 
     scale = tile_of([scale_ref[side, middle] for side in range(2)])
     odd = scal[1] == 1
-    near, far = (ref[ref.shape[0] - extent :, :] for ref in (near_ref, far_ref))
+    near, far = near_ref[...], far_ref[...]
     left = jnp.where(scal[5] > 0, 0.0, jnp.where(odd, near, far))
     right = jnp.where(scal[6] < 2 * extent, 0.0, jnp.where(odd, far, near))
     for part in range(2):
@@ -465,8 +463,8 @@
             corners = corners_of(after(reaches, both), positions, tile)
         scale = light(probe, after(corners, both))
         if not final:
+            side_b = given[1] + partnered(swapped(given[1], "sx", True), "sx")
             side_a = given[0] + swapped(given[0], "sx", False)
-            side_b = given[1] + partnered(swapped(given[1], "sx", True), "sx")
             near, far = jnp.stack([side_a[0], side_b[0]]), jnp.stack([side_a[1], side_b[1]])
             near = near + swapped(near, "sy", False)
             far = far + partnered(swapped(far, "sy", True), "sy")
@@ -475,17 +473,14 @@
         else:
             own_rows, far = given
             far = swapped(far, "sy", True)
-            total = after(chip_sum(both), far, scale).reshape(-1, extent)
+            total = after(chip_sum(both), far, scale)
             far = partnered(after(far, total), "sy")
-            message = f32(total.shape[0] + tile, tile)
             middle, near, far = kernel_call(
-                middle_kernel, (f32(2, tile, tile), message, message), (scal, own_rows, received, far, total), scalars=1
+                middle_kernel, (f32(2, tile, tile),) + (f32(tile, tile),) * 2, (scal, own_rows, received, far), scalars=1
             )
-            head = total.shape[0]
-            near = flipped(near, "sx", 1)
-            far = partnered(swapped(far[head:], "sx", True), "sx")
-            parts = across(total, 2)
-            parts.insert(1, near[:head])
+            near = swapped(near, "sx", False)
+            far = partnered(swapped(far, "sx", True), "sx")
+            parts = across(total, 1)
             chunk = probe_fresh(parts, chunk)
             outcome = kernel_call(object_kernel, f32(2, tile, tile), (scal, canvas, scale, middle, near, far), scalars=1)
         own = probe_spread(chunk, chips)

time: 78.4 us -> 76.5 us (0.976)
  waiting for transfers between devices: 22.2 us -> 20.2 us
    ppermute x18, waiting for transfers between devices: 10.6 us -> 8.58 us  [flipped(): lax.ppermute(values, axis, [(i, i ^ bits) for i in range(lax.axis_size(ax...]
    ppermute x8 -> x9, starting transfers between devices: 7.09 us -> 7.58 us  [swapped(): lax.ppermute(values, axis, [(i, i ^ 1) for i in range(lax.axis_size(axis))])]
    ppermute x8 -> x9, waiting for transfers between devices: 7.11 us -> 7.11 us  [swapped(): lax.ppermute(values, axis, [(i, i ^ 1) for i in range(lax.axis_size(axis))])]
  transfers between devices with their start and end apart: 32 -> 33, of which waited for: 17 -> 17; matrix products, arithmetic and copies ran while one was open for 1% -> 1% of each run, Pallas kernels for 6% -> 7%
where the time goes in v5:
time: 76.5 us
  starting transfers between devices  38.2 us (50%)
  waiting for transfers between devices  20.2 us (26%)
  Pallas kernels  13.9 us (18%)
  other arithmetic  1.97 us (3%)
  local copies, waits for them, and re-layouts  1.17 us (2%)
  between operations  1.1 us (1%)
    ppermute x18, starting transfers between devices, flipped(): lax.ppermute(values, axis, [(i, i ^ bits) for i in range(lax.axis_size(ax...  23.1 us
    pallas_call x7, Pallas kernels, kernel_call(): pl.pallas_call(body, out_shape=outs, in_specs=[SMEM] * scalars + [VMEM] *...  13.9 us
    ppermute x18, waiting for transfers between devices, flipped(): lax.ppermute(values, axis, [(i, i ^ bits) for i in range(lax.axis_size(ax...  8.58 us
    ppermute x9, starting transfers between devices, swapped(): lax.ppermute(values, axis, [(i, i ^ 1) for i in range(lax.axis_size(axis))])  7.58 us
    ppermute x6, starting transfers between devices, swapped(): return lax.ppermute(values, ('sy', 'sx'), pairs)  7.54 us
    ppermute x9, waiting for transfers between devices, swapped(): lax.ppermute(values, axis, [(i, i ^ 1) for i in range(lax.axis_size(axis))])  7.11 us
    ppermute x6, waiting for transfers between devices, swapped(): return lax.ppermute(values, ('sy', 'sx'), pairs)  4.48 us
  transfers between devices with their start and end apart: 33, of which 17 were waited for; matrix products, arithmetic and copies ran while one was open for 1% of the time, Pallas kernels for 7%

profile of v5, /device:TPU:0, one launch (start us, length us, event | category | flops | bytes accessed | tf_op | source)
XLA Modules:
  0.0 76.5 jit_solution(12472455592924446275)
XLA Ops:
  2.3 3.4 %collective-permute-start.1 = (f32[136,128]{1,0:T(8,128)S(1)}, f32[136,128]{1,0:T(8,128)S(1)}, u32[]{:S(2)}, u32[]{:S(2)}) collective-permute-start(f32[136,128]{1,0:T(8,128)S(1)} %get-tuple-element.82), channel_id=1, source_target_pairs={{0,28},{1,29},{2,30},{3,31},{4,8},{5,9},{6,10},{7,11},{8,4},{9,5},... | collective-permute-start | bytes 208904 | tf_op jit(solution)/shard_map/ppermute | solution.py:52
  6.0 1.7 %collective-permute-done.1 = f32[136,128]{1,0:T(8,128)S(1)} collective-permute-done((f32[136,128]{1,0:T(8,128)S(1)}, f32[136,128]{1,0:T(8,128)S(1)}, u32[]{:S(2)}, u32[]{:S(2)}) %collective-permute-start.1) | collective-permute-done | bytes 69664 | tf_op jit(solution)/shard_map/ppermute | solution.py:52
  8.3 4.6 %collective-permute-start.2 = (f32[264,128]{1,0:T(8,128)S(1)}, f32[264,128]{1,0:T(8,128)S(1)}, u32[]{:S(2)}, u32[]{:S(2)}) collective-permute-start(f32[264,128]{1,0:T(8,128)S(1)} %concatenate.45), channel_id=1, source_target_pairs={{0,1},{1,0},{2,3},{3,2},{4,5},{5,4},{6,7},{7,6},{8,9},{9,8},{10,11... | collective-permute-start | bytes 405512 | tf_op jit(solution)/shard_map/ppermute | solution.py:39
  13.0 2.9 %collective-permute-done.2.cols_near = f32[264,128]{1,0:T(8,128)S(1)} collective-permute-done((f32[264,128]{1,0:T(8,128)S(1)}, f32[264,128]{1,0:T(8,128)S(1)}, u32[]{:S(2)}, u32[]{:S(2)}) %collective-permute-start.2) | collective-permute-done | bytes 135200 | tf_op jit(solution)/shard_map/ppermute | solution.py:39
  15.9 3.9 %shard_map.68 = (f32[24,128]{1,0:T(8,128)S(1)}, f32[2,2,128,128]{3,2,1,0:T(8,128)S(1)}, f32[2,2,128,128]{3,2,1,0:T(8,128)S(1)}, f32[4,5,16,128]{3,2,1,0:T(8,128)...) custom-call(s32[7]{0:T(128)S(1)} %stack.75.scal, s32[2,4]{1,0:T(2,128)S(1)} %bitcast.86, ...), custom_call_target="tpu_custom_call" | custom-call | flops 1610612736 | bytes 1048576 | tf_op jit(solution)/shard_map/pallas_call | solution.py:344
  20.0 2.0 %collective-permute-start.5 = (f32[2,2,128,128]{3,2,1,0:T(8,128)S(1)}, f32[2,2,128,128]{3,2,1,0:T(8,128)S(1)}, u32[]{:S(2)}, u32[]{:S(2)}) collective-permute-start(f32[2,2,128,128]{3,2,1,0:T(8,128)S(1)} %get-tuple-element.35), channel_id=1, source_target_pairs={{0,1},{1,0},{2,3},{3,2},{4,5},{5,4},{6,7},{7,6},{8,9},{9,8},{10,11... | collective-permute-start | bytes 786440 | tf_op jit(solution)/shard_map/ppermute | solution.py:39
  22.5 1.9 %collective-permute-start.11 = (f32[5,16,128]{2,1,0:T(8,128)S(1)}, f32[5,16,128]{2,1,0:T(8,128)S(1)}, u32[]{:S(2)}, u32[]{:S(2)}) collective-permute-start(f32[5,16,128]{2,1,0:T(8,128)S(1)} %get-tuple-element.63), channel_id=1, source_target_pairs={{0,24},{4,28},{8,16},{12,20},{16,8},{20,12},{24,0},{28,4},{1,25},{... | collective-permute-start | bytes 122888 | tf_op jit(solution)/shard_map/ppermute | solution.py:61
  26.0 1.5 %shard_map.69.scale_ref = f32[2,256,128]{2,1,0:T(8,128)S(1)} custom-call(s32[7]{0:T(128)S(1)} %stack.75.scal, s32[9,2,4]{2,1,0:T(2,128)S(1)} %compare_select_fusion.corners, f32[2,2,128,128]{3,2,1,0:T(8,128)S(1)} %copy-done.1), custom_call_target="tpu_custom_call" | custom-call | flops 805306368 | bytes 1048576 | tf_op jit(solution)/shard_map/pallas_call | solution.py:344
  27.5 1.5 %collective-permute-done.5 = f32[2,2,128,128]{3,2,1,0:T(8,128)S(1)} collective-permute-done((f32[2,2,128,128]{3,2,1,0:T(8,128)S(1)}, f32[2,2,128,128]{3,2,1,0:T(8,128)S(1)}, u32[]{:S(2)}, u32[]{:S(2)}) %collective-permute-start.5) | collective-permute-done | bytes 262176 | tf_op jit(solution)/shard_map/ppermute | solution.py:39
  29.3 2.0 %collective-permute-start.8 = (f32[2,2,128,128]{3,2,1,0:T(8,128)S(1)}, f32[2,2,128,128]{3,2,1,0:T(8,128)S(1)}, u32[]{:S(2)}, u32[]{:S(2)}) collective-permute-start(f32[2,2,128,128]{3,2,1,0:T(8,128)S(1)} %pad_maximum_fusion.1), channel_id=1, source_target_pairs={{0,28},{1,29},{2,30},{3,31},{4,8},{5,9},{6,10},{7,11},{8,4},{9,5},... | collective-permute-start | bytes 786440 | tf_op jit(solution)/shard_map/ppermute | solution.py:52
  31.4 3.0 %collective-permute-start.14 = (f32[5,16,128]{2,1,0:T(8,128)S(1)}, f32[5,16,128]{2,1,0:T(8,128)S(1)}, u32[]{:S(2)}, u32[]{:S(2)}) collective-permute-start(f32[5,16,128]{2,1,0:T(8,128)S(1)} %fusion.3), channel_id=1, source_target_pairs={{0,3},{1,2},{2,1},{3,0},{4,7},{5,6},{6,5},{7,4},{8,11},{9,10},{10,... | collective-permute-start | bytes 122888 | tf_op jit(solution)/shard_map/ppermute | solution.py:61
  35.8 2.8 %collective-permute-done.8 = f32[2,2,128,128]{3,2,1,0:T(8,128)S(1)} collective-permute-done((f32[2,2,128,128]{3,2,1,0:T(8,128)S(1)}, f32[2,2,128,128]{3,2,1,0:T(8,128)S(1)}, u32[]{:S(2)}, u32[]{:S(2)}) %collective-permute-start.8) | collective-permute-done | bytes 262176 | tf_op jit(solution)/shard_map/ppermute | solution.py:52
  41.7 1.7 %collective-permute-start.15 = (f32[4,16,128]{2,1,0:T(8,128)S(1)}, f32[4,16,128]{2,1,0:T(8,128)S(1)}, u32[]{:S(2)}, u32[]{:S(2)}) collective-permute-start(f32[4,16,128]{2,1,0:T(8,128)S(1)} %fusion.7), channel_id=1, source_target_pairs={{0,8},{4,12},{8,0},{12,4},{16,24},{20,28},{24,16},{28,20},{1,9},{5... | collective-permute-start | bytes 98312 | tf_op jit(solution)/shard_map/ppermute | solution.py:61
  43.3 1.3 %collective-permute-done.17 = f32[4,16,128]{2,1,0:T(8,128)S(1)} collective-permute-done((f32[4,16,128]{2,1,0:T(8,128)S(1)}, f32[4,16,128]{2,1,0:T(8,128)S(1)}, u32[]{:S(2)}, u32[]{:S(2)}) %collective-permute-start.17) | collective-permute-done | bytes 32800 | tf_op jit(solution)/shard_map/ppermute | solution.py:61
  47.0 3.7 %shard_map.70 = (f32[2,2,128,128]{3,2,1,0:T(8,128)S(1)}, f32[256,128]{1,0:T(8,128)S(1)}, f32[4,5,16,128]{3,2,1,0:T(8,128)S(1)}, f32[576,128]{1,0:T(8,128)S(1)}, ...) custom-call(s32[7]{0:T(128)S(1)} %stack.75.scal, s32[2,4]{1,0:T(2,128)S(1)} %bitcast.87, ...), custom_call_target="tpu_custom_call" | custom-call | flops 1610612736 | bytes 1048576 | tf_op jit(solution)/shard_map/pallas_call | solution.py:344
  50.9 1.8 %collective-permute-start.20 = (f32[256,128]{1,0:T(8,128)S(1)}, f32[256,128]{1,0:T(8,128)S(1)}, u32[]{:S(2)}, u32[]{:S(2)}) collective-permute-start(f32[256,128]{1,0:T(8,128)S(1)} %get-tuple-element.45), channel_id=1, source_target_pairs={{0,28},{1,29},{2,30},{3,31},{4,8},{5,9},{6,10},{7,11},{8,4},{9,5},... | collective-permute-start | bytes 393224 | tf_op jit(solution)/shard_map/ppermute | solution.py:52
  52.8 1.5 %collective-permute-start.23 = (f32[5,16,128]{2,1,0:T(8,128)S(1)}, f32[5,16,128]{2,1,0:T(8,128)S(1)}, u32[]{:S(2)}, u32[]{:S(2)}) collective-permute-start(f32[5,16,128]{2,1,0:T(8,128)S(1)} %get-tuple-element.60), channel_id=1, source_target_pairs={{0,24},{4,28},{8,16},{12,20},{16,8},{20,12},{24,0},{28,4},{1,25},{... | collective-permute-start | bytes 122888 | tf_op jit(solution)/shard_map/ppermute | solution.py:61
  56.4 1.5 %shard_map.71.scale_ref = f32[2,256,128]{2,1,0:T(8,128)S(1)} custom-call(s32[7]{0:T(128)S(1)} %stack.75.scal, s32[9,2,4]{2,1,0:T(2,128)S(1)} %compare_select_fusion.corners, f32[2,2,128,128]{3,2,1,0:T(8,128)S(1)} %get-tuple-element.43.probe_ref), custom_call_target="tpu_custom_call" | custom-call | flops 805306368 | bytes 1048576 | tf_op jit(solution)/shard_map/pallas_call | solution.py:344
  59.6 2.3 %collective-permute-start.28 = (f32[5,16,128]{2,1,0:T(8,128)S(1)}, f32[5,16,128]{2,1,0:T(8,128)S(1)}, u32[]{:S(2)}, u32[]{:S(2)}) collective-permute-start(f32[5,16,128]{2,1,0:T(8,128)S(1)} %fusion.1), channel_id=1, source_target_pairs={{0,3},{1,2},{2,1},{3,0},{4,7},{5,6},{6,5},{7,4},{8,11},{9,10},{10,... | collective-permute-start | bytes 122888 | tf_op jit(solution)/shard_map/ppermute | solution.py:61
  62.5 1.6 %collective-permute-start.26 = (f32[5,16,128]{2,1,0:T(8,128)S(1)}, f32[5,16,128]{2,1,0:T(8,128)S(1)}, u32[]{:S(2)}, u32[]{:S(2)}) collective-permute-start(f32[5,16,128]{2,1,0:T(8,128)S(1)} %fusion.1), channel_id=1, source_target_pairs={{0,1},{1,0},{2,3},{3,2},{4,5},{5,4},{6,7},{7,6},{8,9},{9,8},{10,11... | collective-permute-start | bytes 122888 | tf_op jit(solution)/shard_map/ppermute | solution.py:61
  65.5 1.8 %collective-permute-done.27 = f32[5,16,128]{2,1,0:T(8,128)S(1)} collective-permute-done((f32[5,16,128]{2,1,0:T(8,128)S(1)}, f32[5,16,128]{2,1,0:T(8,128)S(1)}, u32[]{:S(2)}, u32[]{:S(2)}) %collective-permute-start.27) | collective-permute-done | bytes 40992 | tf_op jit(solution)/shard_map/ppermute | solution.py:61
  67.4 1.7 %collective-permute-start.31 = (f32[4,16,128]{2,1,0:T(8,128)S(1)}, f32[4,16,128]{2,1,0:T(8,128)S(1)}, u32[]{:S(2)}, u32[]{:S(2)}) collective-permute-start(f32[4,16,128]{2,1,0:T(8,128)S(1)} %fusion.5), channel_id=1, source_target_pairs={{0,24},{4,28},{8,16},{12,20},{16,8},{20,12},{24,0},{28,4},{1,25},{... | collective-permute-start | bytes 98312 | tf_op jit(solution)/shard_map/ppermute | solution.py:61
  71.0 1.4 %shard_map.73 = f32[2,128,128]{2,1,0:T(8,128)} custom-call(s32[7]{0:T(128)S(1)} %stack.75.scal, f32[2,2,256,128]{3,2,1,0:T(8,128)S(1)} %get-tuple-element.39.old_ref, f32[2,256,128]{2,1,0:T(8,128)S(1)} %shard_map.71.scale_ref, f32[2,128,128]{2,1,0:T(8,128)S(1)} %get-tuple-element.48.middle_ref, f32[128,128]{1,0:T(8,128)S(1)} %collective-permute-done.24.near_ref, ...), custom_call_target="tpu_custom_call" | custom-call | bytes 1048576 | tf_op jit(solution)/shard_map/pallas_call | solution.py:344
  73.9 1.3 %collective-permute-done.32.other_ref = f32[4,4,16,128]{3,2,1,0:T(8,128)S(1)} collective-permute-done((f32[4,4,16,128]{3,2,1,0:T(8,128)S(1)}, f32[4,4,16,128]{3,2,1,0:T(8,128)S(1)}, u32[]{:S(2)}, u32[]{:S(2)}) %collective-permute-start.32) | collective-permute-done | bytes 131104 | tf_op jit(solution)/shard_map/ppermute | solution.py:39
  (119 shorter events, 22.4 us)
Async XLA Ops:
  2.3 5.4 %collective-permute-start.1 = (f32[136,128]{1,0:T(8,128)S(1)}, f32[136,128]{1,0:T(8,128)S(1)}, u32[]{:S(2)}, u32[]{:S(2)}) collective-permute-start(f32[136,128]{1,0:T(8,128)S(1)} %get-tuple-element.82), channel_id=1, source_target_pairs={{0,28},{1,29},{2,30},{3,31},{4,8},{5,9},{6,10},{7,11},{8,4},{9,5},... | collective-permute-start | bytes 208904 | tf_op jit(solution)/shard_map/ppermute | solution.py:52
  8.1 4.9 %collective-permute-start.3 = (f32[264,128]{1,0:T(8,128)S(1)}, f32[264,128]{1,0:T(8,128)S(1)}, u32[]{:S(2)}, u32[]{:S(2)}) collective-permute-start(f32[264,128]{1,0:T(8,128)S(1)} %concatenate.48), channel_id=1, source_target_pairs={{0,4},{1,2},{2,1},{3,7},{4,0},{5,6},{6,5},{7,3},{8,12},{9,10},{10,... | collective-permute-start | bytes 405512 | tf_op jit(solution)/shard_map/ppermute | solution.py:52
  8.3 7.6 %collective-permute-start.2 = (f32[264,128]{1,0:T(8,128)S(1)}, f32[264,128]{1,0:T(8,128)S(1)}, u32[]{:S(2)}, u32[]{:S(2)}) collective-permute-start(f32[264,128]{1,0:T(8,128)S(1)} %concatenate.45), channel_id=1, source_target_pairs={{0,1},{1,0},{2,3},{3,2},{4,5},{5,4},{6,7},{7,6},{8,9},{9,8},{10,11... | collective-permute-start | bytes 405512 | tf_op jit(solution)/shard_map/ppermute | solution.py:39
  20.0 9.0 %collective-permute-start.5 = (f32[2,2,128,128]{3,2,1,0:T(8,128)S(1)}, f32[2,2,128,128]{3,2,1,0:T(8,128)S(1)}, u32[]{:S(2)}, u32[]{:S(2)}) collective-permute-start(f32[2,2,128,128]{3,2,1,0:T(8,128)S(1)} %get-tuple-element.35), channel_id=1, source_target_pairs={{0,1},{1,0},{2,3},{3,2},{4,5},{5,4},{6,7},{7,6},{8,9},{9,8},{10,11... | collective-permute-start | bytes 786440 | tf_op jit(solution)/shard_map/ppermute | solution.py:39
  22.0 7.0 %collective-permute-start.6 = (f32[2,2,128,128]{3,2,1,0:T(8,128)S(1)}, f32[2,2,128,128]{3,2,1,0:T(8,128)S(1)}, u32[]{:S(2)}, u32[]{:S(2)}) collective-permute-start(f32[2,2,128,128]{3,2,1,0:T(8,128)S(1)} %get-tuple-element.36), channel_id=1, source_target_pairs={{0,4},{1,2},{2,1},{3,7},{4,0},{5,6},{6,5},{7,3},{8,12},{9,10},{10,... | collective-permute-start | bytes 786440 | tf_op jit(solution)/shard_map/ppermute | solution.py:52
  22.5 8.8 %collective-permute-start.11 = (f32[5,16,128]{2,1,0:T(8,128)S(1)}, f32[5,16,128]{2,1,0:T(8,128)S(1)}, u32[]{:S(2)}, u32[]{:S(2)}) collective-permute-start(f32[5,16,128]{2,1,0:T(8,128)S(1)} %get-tuple-element.63), channel_id=1, source_target_pairs={{0,24},{4,28},{8,16},{12,20},{16,8},{20,12},{24,0},{28,4},{1,25},{... | collective-permute-start | bytes 122888 | tf_op jit(solution)/shard_map/ppermute | solution.py:61
  24.4 6.9 %collective-permute-start.10 = (f32[5,16,128]{2,1,0:T(8,128)S(1)}, f32[5,16,128]{2,1,0:T(8,128)S(1)}, u32[]{:S(2)}, u32[]{:S(2)}) collective-permute-start(f32[5,16,128]{2,1,0:T(8,128)S(1)} %get-tuple-element.64), channel_id=1, source_target_pairs={{0,16},{4,20},{8,24},{12,28},{16,0},{20,4},{24,8},{28,12},{1,17},{... | collective-permute-start | bytes 122888 | tf_op jit(solution)/shard_map/ppermute | solution.py:61
  25.3 6.0 %collective-permute-start.9 = (f32[5,16,128]{2,1,0:T(8,128)S(1)}, f32[5,16,128]{2,1,0:T(8,128)S(1)}, u32[]{:S(2)}, u32[]{:S(2)}) collective-permute-start(f32[5,16,128]{2,1,0:T(8,128)S(1)} %get-tuple-element.65), channel_id=1, source_target_pairs={{0,8},{4,12},{8,0},{12,4},{16,24},{20,28},{24,16},{28,20},{1,9},{5... | collective-permute-start | bytes 122888 | tf_op jit(solution)/shard_map/ppermute | solution.py:61
  29.3 9.4 %collective-permute-start.8 = (f32[2,2,128,128]{3,2,1,0:T(8,128)S(1)}, f32[2,2,128,128]{3,2,1,0:T(8,128)S(1)}, u32[]{:S(2)}, u32[]{:S(2)}) collective-permute-start(f32[2,2,128,128]{3,2,1,0:T(8,128)S(1)} %pad_maximum_fusion.1), channel_id=1, source_target_pairs={{0,28},{1,29},{2,30},{3,31},{4,8},{5,9},{6,10},{7,11},{8,4},{9,5},... | collective-permute-start | bytes 786440 | tf_op jit(solution)/shard_map/ppermute | solution.py:52
  31.4 7.3 %collective-permute-start.14 = (f32[5,16,128]{2,1,0:T(8,128)S(1)}, f32[5,16,128]{2,1,0:T(8,128)S(1)}, u32[]{:S(2)}, u32[]{:S(2)}) collective-permute-start(f32[5,16,128]{2,1,0:T(8,128)S(1)} %fusion.3), channel_id=1, source_target_pairs={{0,3},{1,2},{2,1},{3,0},{4,7},{5,6},{6,5},{7,4},{8,11},{9,10},{10,... | collective-permute-start | bytes 122888 | tf_op jit(solution)/shard_map/ppermute | solution.py:61
  34.4 5.3 %collective-permute-start.13 = (f32[5,16,128]{2,1,0:T(8,128)S(1)}, f32[5,16,128]{2,1,0:T(8,128)S(1)}, u32[]{:S(2)}, u32[]{:S(2)}) collective-permute-start(f32[5,16,128]{2,1,0:T(8,128)S(1)} %fusion.3), channel_id=1, source_target_pairs={{0,2},{1,3},{2,0},{3,1},{4,6},{5,7},{6,4},{7,5},{8,10},{9,11},{10,... | collective-permute-start | bytes 122888 | tf_op jit(solution)/shard_map/ppermute | solution.py:61
  34.9 4.9 %collective-permute-start.12 = (f32[5,16,128]{2,1,0:T(8,128)S(1)}, f32[5,16,128]{2,1,0:T(8,128)S(1)}, u32[]{:S(2)}, u32[]{:S(2)}) collective-permute-start(f32[5,16,128]{2,1,0:T(8,128)S(1)} %fusion.3), channel_id=1, source_target_pairs={{0,1},{1,0},{2,3},{3,2},{4,5},{5,4},{6,7},{7,6},{8,9},{9,8},{10,11... | collective-permute-start | bytes 122888 | tf_op jit(solution)/shard_map/ppermute | solution.py:61
  39.8 4.9 %collective-permute-start.17 = (f32[4,16,128]{2,1,0:T(8,128)S(1)}, f32[4,16,128]{2,1,0:T(8,128)S(1)}, u32[]{:S(2)}, u32[]{:S(2)}) collective-permute-start(f32[4,16,128]{2,1,0:T(8,128)S(1)} %fusion.7), channel_id=1, source_target_pairs={{0,24},{4,28},{8,16},{12,20},{16,8},{20,12},{24,0},{28,4},{1,25},{... | collective-permute-start | bytes 98312 | tf_op jit(solution)/shard_map/ppermute | solution.py:61
  40.9 4.1 %collective-permute-start.16 = (f32[4,16,128]{2,1,0:T(8,128)S(1)}, f32[4,16,128]{2,1,0:T(8,128)S(1)}, u32[]{:S(2)}, u32[]{:S(2)}) collective-permute-start(f32[4,16,128]{2,1,0:T(8,128)S(1)} %fusion.7), channel_id=1, source_target_pairs={{0,16},{4,20},{8,24},{12,28},{16,0},{20,4},{24,8},{28,12},{1,17},{... | collective-permute-start | bytes 98312 | tf_op jit(solution)/shard_map/ppermute | solution.py:61
  50.9 8.7 %collective-permute-start.20 = (f32[256,128]{1,0:T(8,128)S(1)}, f32[256,128]{1,0:T(8,128)S(1)}, u32[]{:S(2)}, u32[]{:S(2)}) collective-permute-start(f32[256,128]{1,0:T(8,128)S(1)} %get-tuple-element.45), channel_id=1, source_target_pairs={{0,28},{1,29},{2,30},{3,31},{4,8},{5,9},{6,10},{7,11},{8,4},{9,5},... | collective-permute-start | bytes 393224 | tf_op jit(solution)/shard_map/ppermute | solution.py:52
  52.8 5.9 %collective-permute-start.23 = (f32[5,16,128]{2,1,0:T(8,128)S(1)}, f32[5,16,128]{2,1,0:T(8,128)S(1)}, u32[]{:S(2)}, u32[]{:S(2)}) collective-permute-start(f32[5,16,128]{2,1,0:T(8,128)S(1)} %get-tuple-element.60), channel_id=1, source_target_pairs={{0,24},{4,28},{8,16},{12,20},{16,8},{20,12},{24,0},{28,4},{1,25},{... | collective-permute-start | bytes 122888 | tf_op jit(solution)/shard_map/ppermute | solution.py:61
  54.3 4.6 %collective-permute-start.22 = (f32[5,16,128]{2,1,0:T(8,128)S(1)}, f32[5,16,128]{2,1,0:T(8,128)S(1)}, u32[]{:S(2)}, u32[]{:S(2)}) collective-permute-start(f32[5,16,128]{2,1,0:T(8,128)S(1)} %get-tuple-element.61), channel_id=1, source_target_pairs={{0,16},{4,20},{8,24},{12,28},{16,0},{20,4},{24,8},{28,12},{1,17},{... | collective-permute-start | bytes 122888 | tf_op jit(solution)/shard_map/ppermute | solution.py:61
  55.6 4.0 %collective-permute-start.21 = (f32[5,16,128]{2,1,0:T(8,128)S(1)}, f32[5,16,128]{2,1,0:T(8,128)S(1)}, u32[]{:S(2)}, u32[]{:S(2)}) collective-permute-start(f32[5,16,128]{2,1,0:T(8,128)S(1)} %get-tuple-element.62), channel_id=1, source_target_pairs={{0,8},{4,12},{8,0},{12,4},{16,24},{20,28},{24,16},{28,20},{1,9},{5... | collective-permute-start | bytes 122888 | tf_op jit(solution)/shard_map/ppermute | solution.py:61
  59.6 5.9 %collective-permute-start.28 = (f32[5,16,128]{2,1,0:T(8,128)S(1)}, f32[5,16,128]{2,1,0:T(8,128)S(1)}, u32[]{:S(2)}, u32[]{:S(2)}) collective-permute-start(f32[5,16,128]{2,1,0:T(8,128)S(1)} %fusion.1), channel_id=1, source_target_pairs={{0,3},{1,2},{2,1},{3,0},{4,7},{5,6},{6,5},{7,4},{8,11},{9,10},{10,... | collective-permute-start | bytes 122888 | tf_op jit(solution)/shard_map/ppermute | solution.py:61
  62.0 5.4 %collective-permute-start.27 = (f32[5,16,128]{2,1,0:T(8,128)S(1)}, f32[5,16,128]{2,1,0:T(8,128)S(1)}, u32[]{:S(2)}, u32[]{:S(2)}) collective-permute-start(f32[5,16,128]{2,1,0:T(8,128)S(1)} %fusion.1), channel_id=1, source_target_pairs={{0,2},{1,3},{2,0},{3,1},{4,6},{5,7},{6,4},{7,5},{8,10},{9,11},{10,... | collective-permute-start | bytes 122888 | tf_op jit(solution)/shard_map/ppermute | solution.py:61
  62.5 4.9 %collective-permute-start.26 = (f32[5,16,128]{2,1,0:T(8,128)S(1)}, f32[5,16,128]{2,1,0:T(8,128)S(1)}, u32[]{:S(2)}, u32[]{:S(2)}) collective-permute-start(f32[5,16,128]{2,1,0:T(8,128)S(1)} %fusion.1), channel_id=1, source_target_pairs={{0,1},{1,0},{2,3},{3,2},{4,5},{5,4},{6,7},{7,6},{8,9},{9,8},{10,11... | collective-permute-start | bytes 122888 | tf_op jit(solution)/shard_map/ppermute | solution.py:61
  64.8 6.2 %collective-permute-start.24 = (f32[128,128]{1,0:T(8,128)S(1)}, f32[128,128]{1,0:T(8,128)S(1)}, u32[]{:S(2)}, u32[]{:S(2)}) collective-permute-start(f32[128,128]{1,0:T(8,128)S(1)} %get-tuple-element.49), channel_id=1, source_target_pairs={{0,1},{1,0},{2,3},{3,2},{4,5},{5,4},{6,7},{7,6},{8,9},{9,8},{10,11... | collective-permute-start | bytes 196616 | tf_op jit(solution)/shard_map/ppermute | solution.py:39
  65.3 5.7 %collective-permute-start.25 = (f32[128,128]{1,0:T(8,128)S(1)}, f32[128,128]{1,0:T(8,128)S(1)}, u32[]{:S(2)}, u32[]{:S(2)}) collective-permute-start(f32[128,128]{1,0:T(8,128)S(1)} %get-tuple-element.50), channel_id=1, source_target_pairs={{0,4},{1,2},{2,1},{3,7},{4,0},{5,6},{6,5},{7,3},{8,12},{9,10},{10,... | collective-permute-start | bytes 196616 | tf_op jit(solution)/shard_map/ppermute | solution.py:52
  67.4 5.0 %collective-permute-start.31 = (f32[4,16,128]{2,1,0:T(8,128)S(1)}, f32[4,16,128]{2,1,0:T(8,128)S(1)}, u32[]{:S(2)}, u32[]{:S(2)}) collective-permute-start(f32[4,16,128]{2,1,0:T(8,128)S(1)} %fusion.5), channel_id=1, source_target_pairs={{0,24},{4,28},{8,16},{12,20},{16,8},{20,12},{24,0},{28,4},{1,25},{... | collective-permute-start | bytes 98312 | tf_op jit(solution)/shard_map/ppermute | solution.py:61
  (14 other events, 50.6 us)

commit v6 on v5

--- a/solution.py
+++ b/solution.py
@@ -43,7 +43,10 @@
         for col in range(cols):
             to_row, to_col = row, col
             if axis == "sy":
-                to_row = (row + 1 if row % 2 else row - 1) % rows
+                if 0 < row < rows - 1:
+                    to_row = row + 1 if row % 2 else row - 1
+                else:
+                    to_col = col ^ 1
             elif 0 < col < cols - 1:
                 to_col = col + 1 if col % 2 else col - 1
             else:

time: 76.5 us -> 76 us (level)
  starting transfers between devices: 38.2 us -> 35.7 us
  waiting for transfers between devices: 20.2 us -> 22.1 us
    ppermute x18, waiting for transfers between devices: 8.58 us -> 12.2 us  [flipped(): lax.ppermute(values, axis, [(i, i ^ bits) for i in range(lax.axis_size(ax...]
    ppermute x6, waiting for transfers between devices: 4.48 us -> 1.96 us  [swapped(): return lax.ppermute(values, ('sy', 'sx'), pairs)]
    ppermute x9, starting transfers between devices: 7.58 us -> 6.2 us  [swapped(): lax.ppermute(values, axis, [(i, i ^ 1) for i in range(lax.axis_size(axis))])]
    ppermute x6, starting transfers between devices: 7.54 us -> 6.26 us  [swapped(): return lax.ppermute(values, ('sy', 'sx'), pairs)]
    ppermute x9, waiting for transfers between devices: 7.11 us -> 7.93 us  [swapped(): lax.ppermute(values, axis, [(i, i ^ 1) for i in range(lax.axis_size(axis))])]
  transfers between devices with their start and end apart: 33 -> 33, of which waited for: 17 -> 16; matrix products, arithmetic and copies ran while one was open for 1% -> 1% of each run, Pallas kernels for 7% -> 7%
where the time goes in v6:
time: 76 us; the launch traced here: 75.9 us
  starting transfers between devices  35.7 us (47%)
  waiting for transfers between devices  22.1 us (29%)
  Pallas kernels  13.9 us (18%)
  other arithmetic  1.97 us (3%)
  local copies, waits for them, and re-layouts  1.17 us (2%)
  between operations  1.11 us (1%)
    ppermute x18, starting transfers between devices, flipped(): lax.ppermute(values, axis, [(i, i ^ bits) for i in range(lax.axis_size(ax...  23.3 us
    pallas_call x7, Pallas kernels, kernel_call(): pl.pallas_call(body, out_shape=outs, in_specs=[SMEM] * scalars + [VMEM] *...  13.9 us
    ppermute x18, waiting for transfers between devices, flipped(): lax.ppermute(values, axis, [(i, i ^ bits) for i in range(lax.axis_size(ax...  12.2 us
    ppermute x9, waiting for transfers between devices, swapped(): lax.ppermute(values, axis, [(i, i ^ 1) for i in range(lax.axis_size(axis))])  7.93 us
    ppermute x6, starting transfers between devices, swapped(): return lax.ppermute(values, ('sy', 'sx'), pairs)  6.26 us
    ppermute x9, starting transfers between devices, swapped(): lax.ppermute(values, axis, [(i, i ^ 1) for i in range(lax.axis_size(axis))])  6.2 us
    ppermute x6, waiting for transfers between devices, swapped(): return lax.ppermute(values, ('sy', 'sx'), pairs)  1.96 us
  transfers between devices with their start and end apart: 33, of which 16 were waited for; matrix products, arithmetic and copies ran while one was open for 1% of the time, Pallas kernels for 7%

profile of v6, /device:TPU:0, one launch (start us, length us, event | category | flops | bytes accessed | tf_op | source)
XLA Modules:
  0.0 75.9 jit_solution(18040880667365149489)
XLA Ops:
  2.3 3.1 %collective-permute-start.1 = (f32[136,128]{1,0:T(8,128)S(1)}, f32[136,128]{1,0:T(8,128)S(1)}, u32[]{:S(2)}, u32[]{:S(2)}) collective-permute-start(f32[136,128]{1,0:T(8,128)S(1)} %get-tuple-element.82), channel_id=1, source_target_pairs={{0,1},{1,0},{2,3},{3,2},{4,8},{5,9},{6,10},{7,11},{8,4},{9,5},{10,... | collective-permute-start | bytes 208904 | tf_op jit(solution)/shard_map/ppermute | solution.py:55
  5.7 1.9 %collective-permute-done.1 = f32[136,128]{1,0:T(8,128)S(1)} collective-permute-done((f32[136,128]{1,0:T(8,128)S(1)}, f32[136,128]{1,0:T(8,128)S(1)}, u32[]{:S(2)}, u32[]{:S(2)}) %collective-permute-start.1) | collective-permute-done | bytes 69664 | tf_op jit(solution)/shard_map/ppermute | solution.py:55
  8.3 3.6 %collective-permute-start.2 = (f32[264,128]{1,0:T(8,128)S(1)}, f32[264,128]{1,0:T(8,128)S(1)}, u32[]{:S(2)}, u32[]{:S(2)}) collective-permute-start(f32[264,128]{1,0:T(8,128)S(1)} %concatenate.45), channel_id=1, source_target_pairs={{0,1},{1,0},{2,3},{3,2},{4,5},{5,4},{6,7},{7,6},{8,9},{9,8},{10,11... | collective-permute-start | bytes 405512 | tf_op jit(solution)/shard_map/ppermute | solution.py:39
  12.0 3.0 %collective-permute-done.2.cols_near = f32[264,128]{1,0:T(8,128)S(1)} collective-permute-done((f32[264,128]{1,0:T(8,128)S(1)}, f32[264,128]{1,0:T(8,128)S(1)}, u32[]{:S(2)}, u32[]{:S(2)}) %collective-permute-start.2) | collective-permute-done | bytes 135200 | tf_op jit(solution)/shard_map/ppermute | solution.py:39
  15.0 3.9 %shard_map.68 = (f32[24,128]{1,0:T(8,128)S(1)}, f32[2,2,128,128]{3,2,1,0:T(8,128)S(1)}, f32[2,2,128,128]{3,2,1,0:T(8,128)S(1)}, f32[4,5,16,128]{3,2,1,0:T(8,128)...) custom-call(s32[7]{0:T(128)S(1)} %stack.75.scal, s32[2,4]{1,0:T(2,128)S(1)} %bitcast.86, ...), custom_call_target="tpu_custom_call" | custom-call | flops 1610612736 | bytes 1048576 | tf_op jit(solution)/shard_map/pallas_call | solution.py:347
  19.1 2.0 %collective-permute-start.5 = (f32[2,2,128,128]{3,2,1,0:T(8,128)S(1)}, f32[2,2,128,128]{3,2,1,0:T(8,128)S(1)}, u32[]{:S(2)}, u32[]{:S(2)}) collective-permute-start(f32[2,2,128,128]{3,2,1,0:T(8,128)S(1)} %get-tuple-element.35), channel_id=1, source_target_pairs={{0,1},{1,0},{2,3},{3,2},{4,5},{5,4},{6,7},{7,6},{8,9},{9,8},{10,11... | collective-permute-start | bytes 786440 | tf_op jit(solution)/shard_map/ppermute | solution.py:39
  21.5 2.6 %collective-permute-start.11 = (f32[5,16,128]{2,1,0:T(8,128)S(1)}, f32[5,16,128]{2,1,0:T(8,128)S(1)}, u32[]{:S(2)}, u32[]{:S(2)}) collective-permute-start(f32[5,16,128]{2,1,0:T(8,128)S(1)} %get-tuple-element.63), channel_id=1, source_target_pairs={{0,24},{4,28},{8,16},{12,20},{16,8},{20,12},{24,0},{28,4},{1,25},{... | collective-permute-start | bytes 122888 | tf_op jit(solution)/shard_map/ppermute | solution.py:64
  25.2 1.5 %shard_map.69.scale_ref = f32[2,256,128]{2,1,0:T(8,128)S(1)} custom-call(s32[7]{0:T(128)S(1)} %stack.75.scal, s32[9,2,4]{2,1,0:T(2,128)S(1)} %compare_select_fusion.corners, f32[2,2,128,128]{3,2,1,0:T(8,128)S(1)} %copy-done.1), custom_call_target="tpu_custom_call" | custom-call | flops 805306368 | bytes 1048576 | tf_op jit(solution)/shard_map/pallas_call | solution.py:347
  26.7 1.4 %collective-permute-done.5 = f32[2,2,128,128]{3,2,1,0:T(8,128)S(1)} collective-permute-done((f32[2,2,128,128]{3,2,1,0:T(8,128)S(1)}, f32[2,2,128,128]{3,2,1,0:T(8,128)S(1)}, u32[]{:S(2)}, u32[]{:S(2)}) %collective-permute-start.5) | collective-permute-done | bytes 262176 | tf_op jit(solution)/shard_map/ppermute | solution.py:39
  28.3 2.3 %collective-permute-start.8 = (f32[2,2,128,128]{3,2,1,0:T(8,128)S(1)}, f32[2,2,128,128]{3,2,1,0:T(8,128)S(1)}, u32[]{:S(2)}, u32[]{:S(2)}) collective-permute-start(f32[2,2,128,128]{3,2,1,0:T(8,128)S(1)} %pad_maximum_fusion.1), channel_id=1, source_target_pairs={{0,1},{1,0},{2,3},{3,2},{4,8},{5,9},{6,10},{7,11},{8,4},{9,5},{10,... | collective-permute-start | bytes 786440 | tf_op jit(solution)/shard_map/ppermute | solution.py:55
  30.7 2.7 %collective-permute-start.14 = (f32[5,16,128]{2,1,0:T(8,128)S(1)}, f32[5,16,128]{2,1,0:T(8,128)S(1)}, u32[]{:S(2)}, u32[]{:S(2)}) collective-permute-start(f32[5,16,128]{2,1,0:T(8,128)S(1)} %fusion.3), channel_id=1, source_target_pairs={{0,3},{1,2},{2,1},{3,0},{4,7},{5,6},{6,5},{7,4},{8,11},{9,10},{10,... | collective-permute-start | bytes 122888 | tf_op jit(solution)/shard_map/ppermute | solution.py:64
  33.6 1.5 %collective-permute-start.12 = (f32[5,16,128]{2,1,0:T(8,128)S(1)}, f32[5,16,128]{2,1,0:T(8,128)S(1)}, u32[]{:S(2)}, u32[]{:S(2)}) collective-permute-start(f32[5,16,128]{2,1,0:T(8,128)S(1)} %fusion.3), channel_id=1, source_target_pairs={{0,1},{1,0},{2,3},{3,2},{4,5},{5,4},{6,7},{7,6},{8,9},{9,8},{10,11... | collective-permute-start | bytes 122888 | tf_op jit(solution)/shard_map/ppermute | solution.py:64
  35.2 4.2 %collective-permute-done.14 = f32[5,16,128]{2,1,0:T(8,128)S(1)} collective-permute-done((f32[5,16,128]{2,1,0:T(8,128)S(1)}, f32[5,16,128]{2,1,0:T(8,128)S(1)}, u32[]{:S(2)}, u32[]{:S(2)}) %collective-permute-start.14) | collective-permute-done | bytes 40992 | tf_op jit(solution)/shard_map/ppermute | solution.py:64
  39.4 2.6 %collective-permute-start.17 = (f32[4,16,128]{2,1,0:T(8,128)S(1)}, f32[4,16,128]{2,1,0:T(8,128)S(1)}, u32[]{:S(2)}, u32[]{:S(2)}) collective-permute-start(f32[4,16,128]{2,1,0:T(8,128)S(1)} %fusion.7), channel_id=1, source_target_pairs={{0,24},{4,28},{8,16},{12,20},{16,8},{20,12},{24,0},{28,4},{1,25},{... | collective-permute-start | bytes 98312 | tf_op jit(solution)/shard_map/ppermute | solution.py:64
  43.0 1.4 %collective-permute-done.17 = f32[4,16,128]{2,1,0:T(8,128)S(1)} collective-permute-done((f32[4,16,128]{2,1,0:T(8,128)S(1)}, f32[4,16,128]{2,1,0:T(8,128)S(1)}, u32[]{:S(2)}, u32[]{:S(2)}) %collective-permute-start.17) | collective-permute-done | bytes 32800 | tf_op jit(solution)/shard_map/ppermute | solution.py:64
  44.4 1.5 %collective-permute-done.16 = f32[4,16,128]{2,1,0:T(8,128)S(1)} collective-permute-done((f32[4,16,128]{2,1,0:T(8,128)S(1)}, f32[4,16,128]{2,1,0:T(8,128)S(1)}, u32[]{:S(2)}, u32[]{:S(2)}) %collective-permute-start.16) | collective-permute-done | bytes 32800 | tf_op jit(solution)/shard_map/ppermute | solution.py:64
  47.3 3.7 %shard_map.70 = (f32[2,2,128,128]{3,2,1,0:T(8,128)S(1)}, f32[256,128]{1,0:T(8,128)S(1)}, f32[4,5,16,128]{3,2,1,0:T(8,128)S(1)}, f32[576,128]{1,0:T(8,128)S(1)}, ...) custom-call(s32[7]{0:T(128)S(1)} %stack.75.scal, s32[2,4]{1,0:T(2,128)S(1)} %bitcast.87, ...), custom_call_target="tpu_custom_call" | custom-call | flops 1610612736 | bytes 1048576 | tf_op jit(solution)/shard_map/pallas_call | solution.py:347
  52.7 2.1 %collective-permute-start.23 = (f32[5,16,128]{2,1,0:T(8,128)S(1)}, f32[5,16,128]{2,1,0:T(8,128)S(1)}, u32[]{:S(2)}, u32[]{:S(2)}) collective-permute-start(f32[5,16,128]{2,1,0:T(8,128)S(1)} %get-tuple-element.60), channel_id=1, source_target_pairs={{0,24},{4,28},{8,16},{12,20},{16,8},{20,12},{24,0},{28,4},{1,25},{... | collective-permute-start | bytes 122888 | tf_op jit(solution)/shard_map/ppermute | solution.py:64
  56.3 1.5 %shard_map.71.scale_ref = f32[2,256,128]{2,1,0:T(8,128)S(1)} custom-call(s32[7]{0:T(128)S(1)} %stack.75.scal, s32[9,2,4]{2,1,0:T(2,128)S(1)} %compare_select_fusion.corners, f32[2,2,128,128]{3,2,1,0:T(8,128)S(1)} %get-tuple-element.43.probe_ref), custom_call_target="tpu_custom_call" | custom-call | flops 805306368 | bytes 1048576 | tf_op jit(solution)/shard_map/pallas_call | solution.py:347
  59.4 2.2 %collective-permute-start.28 = (f32[5,16,128]{2,1,0:T(8,128)S(1)}, f32[5,16,128]{2,1,0:T(8,128)S(1)}, u32[]{:S(2)}, u32[]{:S(2)}) collective-permute-start(f32[5,16,128]{2,1,0:T(8,128)S(1)} %fusion.1), channel_id=1, source_target_pairs={{0,3},{1,2},{2,1},{3,0},{4,7},{5,6},{6,5},{7,4},{8,11},{9,10},{10,... | collective-permute-start | bytes 122888 | tf_op jit(solution)/shard_map/ppermute | solution.py:64
  61.8 2.1 %collective-permute-start.26 = (f32[5,16,128]{2,1,0:T(8,128)S(1)}, f32[5,16,128]{2,1,0:T(8,128)S(1)}, u32[]{:S(2)}, u32[]{:S(2)}) collective-permute-start(f32[5,16,128]{2,1,0:T(8,128)S(1)} %fusion.1), channel_id=1, source_target_pairs={{0,1},{1,0},{2,3},{3,2},{4,5},{5,4},{6,7},{7,6},{8,9},{9,8},{10,11... | collective-permute-start | bytes 122888 | tf_op jit(solution)/shard_map/ppermute | solution.py:64
  66.7 2.6 %collective-permute-start.31 = (f32[4,16,128]{2,1,0:T(8,128)S(1)}, f32[4,16,128]{2,1,0:T(8,128)S(1)}, u32[]{:S(2)}, u32[]{:S(2)}) collective-permute-start(f32[4,16,128]{2,1,0:T(8,128)S(1)} %fusion.5), channel_id=1, source_target_pairs={{0,24},{4,28},{8,16},{12,20},{16,8},{20,12},{24,0},{28,4},{1,25},{... | collective-permute-start | bytes 98312 | tf_op jit(solution)/shard_map/ppermute | solution.py:64
  70.2 1.4 %shard_map.73 = f32[2,128,128]{2,1,0:T(8,128)} custom-call(s32[7]{0:T(128)S(1)} %stack.75.scal, f32[2,2,256,128]{3,2,1,0:T(8,128)S(1)} %get-tuple-element.39.old_ref, f32[2,256,128]{2,1,0:T(8,128)S(1)} %shard_map.71.scale_ref, f32[2,128,128]{2,1,0:T(8,128)S(1)} %get-tuple-element.48.middle_ref, f32[128,128]{1,0:T(8,128)S(1)} %collective-permute-done.24.near_ref, ...), custom_call_target="tpu_custom_call" | custom-call | bytes 1048576 | tf_op jit(solution)/shard_map/pallas_call | solution.py:347
  71.8 1.4 %collective-permute-done.30 = f32[4,16,128]{2,1,0:T(8,128)S(1)} collective-permute-done((f32[4,16,128]{2,1,0:T(8,128)S(1)}, f32[4,16,128]{2,1,0:T(8,128)S(1)}, u32[]{:S(2)}, u32[]{:S(2)}) %collective-permute-start.30) | collective-permute-done | bytes 32800 | tf_op jit(solution)/shard_map/ppermute | solution.py:64
  (119 shorter events, 18.7 us)
Async XLA Ops:
  2.3 5.4 %collective-permute-start.1 = (f32[136,128]{1,0:T(8,128)S(1)}, f32[136,128]{1,0:T(8,128)S(1)}, u32[]{:S(2)}, u32[]{:S(2)}) collective-permute-start(f32[136,128]{1,0:T(8,128)S(1)} %get-tuple-element.82), channel_id=1, source_target_pairs={{0,1},{1,0},{2,3},{3,2},{4,8},{5,9},{6,10},{7,11},{8,4},{9,5},{10,... | collective-permute-start | bytes 208904 | tf_op jit(solution)/shard_map/ppermute | solution.py:55
  8.0 3.9 %collective-permute-start.3 = (f32[264,128]{1,0:T(8,128)S(1)}, f32[264,128]{1,0:T(8,128)S(1)}, u32[]{:S(2)}, u32[]{:S(2)}) collective-permute-start(f32[264,128]{1,0:T(8,128)S(1)} %concatenate.48), channel_id=1, source_target_pairs={{0,4},{1,2},{2,1},{3,7},{4,0},{5,6},{6,5},{7,3},{8,12},{9,10},{10,... | collective-permute-start | bytes 405512 | tf_op jit(solution)/shard_map/ppermute | solution.py:55
  8.3 6.7 %collective-permute-start.2 = (f32[264,128]{1,0:T(8,128)S(1)}, f32[264,128]{1,0:T(8,128)S(1)}, u32[]{:S(2)}, u32[]{:S(2)}) collective-permute-start(f32[264,128]{1,0:T(8,128)S(1)} %concatenate.45), channel_id=1, source_target_pairs={{0,1},{1,0},{2,3},{3,2},{4,5},{5,4},{6,7},{7,6},{8,9},{9,8},{10,11... | collective-permute-start | bytes 405512 | tf_op jit(solution)/shard_map/ppermute | solution.py:39
  19.1 8.9 %collective-permute-start.5 = (f32[2,2,128,128]{3,2,1,0:T(8,128)S(1)}, f32[2,2,128,128]{3,2,1,0:T(8,128)S(1)}, u32[]{:S(2)}, u32[]{:S(2)}) collective-permute-start(f32[2,2,128,128]{3,2,1,0:T(8,128)S(1)} %get-tuple-element.35), channel_id=1, source_target_pairs={{0,1},{1,0},{2,3},{3,2},{4,5},{5,4},{6,7},{7,6},{8,9},{9,8},{10,11... | collective-permute-start | bytes 786440 | tf_op jit(solution)/shard_map/ppermute | solution.py:39
  21.1 7.0 %collective-permute-start.6 = (f32[2,2,128,128]{3,2,1,0:T(8,128)S(1)}, f32[2,2,128,128]{3,2,1,0:T(8,128)S(1)}, u32[]{:S(2)}, u32[]{:S(2)}) collective-permute-start(f32[2,2,128,128]{3,2,1,0:T(8,128)S(1)} %get-tuple-element.36), channel_id=1, source_target_pairs={{0,4},{1,2},{2,1},{3,7},{4,0},{5,6},{6,5},{7,3},{8,12},{9,10},{10,... | collective-permute-start | bytes 786440 | tf_op jit(solution)/shard_map/ppermute | solution.py:55
  21.5 9.1 %collective-permute-start.11 = (f32[5,16,128]{2,1,0:T(8,128)S(1)}, f32[5,16,128]{2,1,0:T(8,128)S(1)}, u32[]{:S(2)}, u32[]{:S(2)}) collective-permute-start(f32[5,16,128]{2,1,0:T(8,128)S(1)} %get-tuple-element.63), channel_id=1, source_target_pairs={{0,24},{4,28},{8,16},{12,20},{16,8},{20,12},{24,0},{28,4},{1,25},{... | collective-permute-start | bytes 122888 | tf_op jit(solution)/shard_map/ppermute | solution.py:64
  24.1 6.5 %collective-permute-start.10 = (f32[5,16,128]{2,1,0:T(8,128)S(1)}, f32[5,16,128]{2,1,0:T(8,128)S(1)}, u32[]{:S(2)}, u32[]{:S(2)}) collective-permute-start(f32[5,16,128]{2,1,0:T(8,128)S(1)} %get-tuple-element.64), channel_id=1, source_target_pairs={{0,16},{4,20},{8,24},{12,28},{16,0},{20,4},{24,8},{28,12},{1,17},{... | collective-permute-start | bytes 122888 | tf_op jit(solution)/shard_map/ppermute | solution.py:64
  25.2 5.4 %collective-permute-start.9 = (f32[5,16,128]{2,1,0:T(8,128)S(1)}, f32[5,16,128]{2,1,0:T(8,128)S(1)}, u32[]{:S(2)}, u32[]{:S(2)}) collective-permute-start(f32[5,16,128]{2,1,0:T(8,128)S(1)} %get-tuple-element.65), channel_id=1, source_target_pairs={{0,8},{4,12},{8,0},{12,4},{16,24},{20,28},{24,16},{28,20},{1,9},{5... | collective-permute-start | bytes 122888 | tf_op jit(solution)/shard_map/ppermute | solution.py:64
  28.3 6.8 %collective-permute-start.8 = (f32[2,2,128,128]{3,2,1,0:T(8,128)S(1)}, f32[2,2,128,128]{3,2,1,0:T(8,128)S(1)}, u32[]{:S(2)}, u32[]{:S(2)}) collective-permute-start(f32[2,2,128,128]{3,2,1,0:T(8,128)S(1)} %pad_maximum_fusion.1), channel_id=1, source_target_pairs={{0,1},{1,0},{2,3},{3,2},{4,8},{5,9},{6,10},{7,11},{8,4},{9,5},{10,... | collective-permute-start | bytes 786440 | tf_op jit(solution)/shard_map/ppermute | solution.py:55
  30.7 8.7 %collective-permute-start.14 = (f32[5,16,128]{2,1,0:T(8,128)S(1)}, f32[5,16,128]{2,1,0:T(8,128)S(1)}, u32[]{:S(2)}, u32[]{:S(2)}) collective-permute-start(f32[5,16,128]{2,1,0:T(8,128)S(1)} %fusion.3), channel_id=1, source_target_pairs={{0,3},{1,2},{2,1},{3,0},{4,7},{5,6},{6,5},{7,4},{8,11},{9,10},{10,... | collective-permute-start | bytes 122888 | tf_op jit(solution)/shard_map/ppermute | solution.py:64
  33.4 6.0 %collective-permute-start.13 = (f32[5,16,128]{2,1,0:T(8,128)S(1)}, f32[5,16,128]{2,1,0:T(8,128)S(1)}, u32[]{:S(2)}, u32[]{:S(2)}) collective-permute-start(f32[5,16,128]{2,1,0:T(8,128)S(1)} %fusion.3), channel_id=1, source_target_pairs={{0,2},{1,3},{2,0},{3,1},{4,6},{5,7},{6,4},{7,5},{8,10},{9,11},{10,... | collective-permute-start | bytes 122888 | tf_op jit(solution)/shard_map/ppermute | solution.py:64
  33.6 5.7 %collective-permute-start.12 = (f32[5,16,128]{2,1,0:T(8,128)S(1)}, f32[5,16,128]{2,1,0:T(8,128)S(1)}, u32[]{:S(2)}, u32[]{:S(2)}) collective-permute-start(f32[5,16,128]{2,1,0:T(8,128)S(1)} %fusion.3), channel_id=1, source_target_pairs={{0,1},{1,0},{2,3},{3,2},{4,5},{5,4},{6,7},{7,6},{8,9},{9,8},{10,11... | collective-permute-start | bytes 122888 | tf_op jit(solution)/shard_map/ppermute | solution.py:64
  39.4 5.0 %collective-permute-start.17 = (f32[4,16,128]{2,1,0:T(8,128)S(1)}, f32[4,16,128]{2,1,0:T(8,128)S(1)}, u32[]{:S(2)}, u32[]{:S(2)}) collective-permute-start(f32[4,16,128]{2,1,0:T(8,128)S(1)} %fusion.7), channel_id=1, source_target_pairs={{0,24},{4,28},{8,16},{12,20},{16,8},{20,12},{24,0},{28,4},{1,25},{... | collective-permute-start | bytes 98312 | tf_op jit(solution)/shard_map/ppermute | solution.py:64
  42.0 3.9 %collective-permute-start.15 = (f32[4,16,128]{2,1,0:T(8,128)S(1)}, f32[4,16,128]{2,1,0:T(8,128)S(1)}, u32[]{:S(2)}, u32[]{:S(2)}) collective-permute-start(f32[4,16,128]{2,1,0:T(8,128)S(1)} %fusion.7), channel_id=1, source_target_pairs={{0,8},{4,12},{8,0},{12,4},{16,24},{20,28},{24,16},{28,20},{1,9},{5... | collective-permute-start | bytes 98312 | tf_op jit(solution)/shard_map/ppermute | solution.py:64
  51.2 8.1 %collective-permute-start.20 = (f32[256,128]{1,0:T(8,128)S(1)}, f32[256,128]{1,0:T(8,128)S(1)}, u32[]{:S(2)}, u32[]{:S(2)}) collective-permute-start(f32[256,128]{1,0:T(8,128)S(1)} %get-tuple-element.45), channel_id=1, source_target_pairs={{0,1},{1,0},{2,3},{3,2},{4,8},{5,9},{6,10},{7,11},{8,4},{9,5},{10,... | collective-permute-start | bytes 393224 | tf_op jit(solution)/shard_map/ppermute | solution.py:55
  52.7 6.1 %collective-permute-start.23 = (f32[5,16,128]{2,1,0:T(8,128)S(1)}, f32[5,16,128]{2,1,0:T(8,128)S(1)}, u32[]{:S(2)}, u32[]{:S(2)}) collective-permute-start(f32[5,16,128]{2,1,0:T(8,128)S(1)} %get-tuple-element.60), channel_id=1, source_target_pairs={{0,24},{4,28},{8,16},{12,20},{16,8},{20,12},{24,0},{28,4},{1,25},{... | collective-permute-start | bytes 122888 | tf_op jit(solution)/shard_map/ppermute | solution.py:64
  54.8 4.2 %collective-permute-start.22 = (f32[5,16,128]{2,1,0:T(8,128)S(1)}, f32[5,16,128]{2,1,0:T(8,128)S(1)}, u32[]{:S(2)}, u32[]{:S(2)}) collective-permute-start(f32[5,16,128]{2,1,0:T(8,128)S(1)} %get-tuple-element.61), channel_id=1, source_target_pairs={{0,16},{4,20},{8,24},{12,28},{16,0},{20,4},{24,8},{28,12},{1,17},{... | collective-permute-start | bytes 122888 | tf_op jit(solution)/shard_map/ppermute | solution.py:64
  55.2 4.1 %collective-permute-start.21 = (f32[5,16,128]{2,1,0:T(8,128)S(1)}, f32[5,16,128]{2,1,0:T(8,128)S(1)}, u32[]{:S(2)}, u32[]{:S(2)}) collective-permute-start(f32[5,16,128]{2,1,0:T(8,128)S(1)} %get-tuple-element.62), channel_id=1, source_target_pairs={{0,8},{4,12},{8,0},{12,4},{16,24},{20,28},{24,16},{28,20},{1,9},{5... | collective-permute-start | bytes 122888 | tf_op jit(solution)/shard_map/ppermute | solution.py:64
  59.4 5.9 %collective-permute-start.28 = (f32[5,16,128]{2,1,0:T(8,128)S(1)}, f32[5,16,128]{2,1,0:T(8,128)S(1)}, u32[]{:S(2)}, u32[]{:S(2)}) collective-permute-start(f32[5,16,128]{2,1,0:T(8,128)S(1)} %fusion.1), channel_id=1, source_target_pairs={{0,3},{1,2},{2,1},{3,0},{4,7},{5,6},{6,5},{7,4},{8,11},{9,10},{10,... | collective-permute-start | bytes 122888 | tf_op jit(solution)/shard_map/ppermute | solution.py:64
  61.6 5.1 %collective-permute-start.27 = (f32[5,16,128]{2,1,0:T(8,128)S(1)}, f32[5,16,128]{2,1,0:T(8,128)S(1)}, u32[]{:S(2)}, u32[]{:S(2)}) collective-permute-start(f32[5,16,128]{2,1,0:T(8,128)S(1)} %fusion.1), channel_id=1, source_target_pairs={{0,2},{1,3},{2,0},{3,1},{4,6},{5,7},{6,4},{7,5},{8,10},{9,11},{10,... | collective-permute-start | bytes 122888 | tf_op jit(solution)/shard_map/ppermute | solution.py:64
  61.8 4.9 %collective-permute-start.26 = (f32[5,16,128]{2,1,0:T(8,128)S(1)}, f32[5,16,128]{2,1,0:T(8,128)S(1)}, u32[]{:S(2)}, u32[]{:S(2)}) collective-permute-start(f32[5,16,128]{2,1,0:T(8,128)S(1)} %fusion.1), channel_id=1, source_target_pairs={{0,1},{1,0},{2,3},{3,2},{4,5},{5,4},{6,7},{7,6},{8,9},{9,8},{10,11... | collective-permute-start | bytes 122888 | tf_op jit(solution)/shard_map/ppermute | solution.py:64
  64.5 5.7 %collective-permute-start.24 = (f32[128,128]{1,0:T(8,128)S(1)}, f32[128,128]{1,0:T(8,128)S(1)}, u32[]{:S(2)}, u32[]{:S(2)}) collective-permute-start(f32[128,128]{1,0:T(8,128)S(1)} %get-tuple-element.49), channel_id=1, source_target_pairs={{0,1},{1,0},{2,3},{3,2},{4,5},{5,4},{6,7},{7,6},{8,9},{9,8},{10,11... | collective-permute-start | bytes 196616 | tf_op jit(solution)/shard_map/ppermute | solution.py:39
  64.6 5.6 %collective-permute-start.25 = (f32[128,128]{1,0:T(8,128)S(1)}, f32[128,128]{1,0:T(8,128)S(1)}, u32[]{:S(2)}, u32[]{:S(2)}) collective-permute-start(f32[128,128]{1,0:T(8,128)S(1)} %get-tuple-element.50), channel_id=1, source_target_pairs={{0,4},{1,2},{2,1},{3,7},{4,0},{5,6},{6,5},{7,3},{8,12},{9,10},{10,... | collective-permute-start | bytes 196616 | tf_op jit(solution)/shard_map/ppermute | solution.py:55
  66.7 5.2 %collective-permute-start.31 = (f32[4,16,128]{2,1,0:T(8,128)S(1)}, f32[4,16,128]{2,1,0:T(8,128)S(1)}, u32[]{:S(2)}, u32[]{:S(2)}) collective-permute-start(f32[4,16,128]{2,1,0:T(8,128)S(1)} %fusion.5), channel_id=1, source_target_pairs={{0,24},{4,28},{8,16},{12,20},{16,8},{20,12},{24,0},{28,4},{1,25},{... | collective-permute-start | bytes 98312 | tf_op jit(solution)/shard_map/ppermute | solution.py:64
  (14 other events, 47.7 us)

commit v7 on v6

--- a/solution.py
+++ b/solution.py
@@ -413,8 +413,10 @@
     return [total] + [flipped(total, "sx", t) for t in range(start, lax.axis_size("sx"))]
 
 
-def probe_spread(fresh, chips):
-    return jnp.stack([fresh] + [flipped(fresh, "sy", 2 * t) for t in range(1, chips)])
+def probe_spread(fresh, chips, *others):
+    first = flipped(fresh, "sy", 2 * (chips - 1))
+    sent = after(fresh, *others) if others else fresh
+    return jnp.stack([fresh] + [flipped(sent, "sy", 2 * t) for t in range(1, chips - 1)] + [first])
 
 
 def per_device(object_tile, probe_modes, scan_offsets, intensities):
@@ -472,7 +474,7 @@
             near = near + swapped(near, "sy", False)
             far = far + partnered(swapped(far, "sy", True), "sy")
             total = after(chip_sum(both), near, scale)
-            chunk = after(probe_fresh(across(total, 1), chunk), near, far)
+            chunk = probe_fresh(across(total, 1), chunk)
         else:
             own_rows, far = given
             far = swapped(far, "sy", True)
@@ -486,7 +488,7 @@
             parts = across(total, 1)
             chunk = probe_fresh(parts, chunk)
             outcome = kernel_call(object_kernel, f32(2, tile, tile), (scal, canvas, scale, middle, near, far), scalars=1)
-        own = probe_spread(chunk, chips)
+        own = probe_spread(chunk, chips) if final else probe_spread(chunk, chips, near, far)
         other = swapped(after(own, outcome) if final else own, "sy", False)
     return outcome, kernel_call(last_kernel, f32(*probe.shape), (scal, own, other), scalars=1)
 

time: 76 us -> 76 us (level)
  no operation moved by 1% of the time
where the time goes in v7:
time: 76 us; the launch traced here: 75.9 us
  starting transfers between devices  35.7 us (47%)
  waiting for transfers between devices  22 us (29%)
  Pallas kernels  13.9 us (18%)
  other arithmetic  1.97 us (3%)
  local copies, waits for them, and re-layouts  1.17 us (2%)
  between operations  1.11 us (1%)
    ppermute x18, starting transfers between devices, flipped(): lax.ppermute(values, axis, [(i, i ^ bits) for i in range(lax.axis_size(ax...  23.3 us
    pallas_call x7, Pallas kernels, kernel_call(): pl.pallas_call(body, out_shape=outs, in_specs=[SMEM] * scalars + [VMEM] *...  13.9 us
    ppermute x18, waiting for transfers between devices, flipped(): lax.ppermute(values, axis, [(i, i ^ bits) for i in range(lax.axis_size(ax...  12.2 us
    ppermute x9, waiting for transfers between devices, swapped(): lax.ppermute(values, axis, [(i, i ^ 1) for i in range(lax.axis_size(axis))])  7.88 us
    ppermute x6, starting transfers between devices, swapped(): return lax.ppermute(values, ('sy', 'sx'), pairs)  6.26 us
    ppermute x9, starting transfers between devices, swapped(): lax.ppermute(values, axis, [(i, i ^ 1) for i in range(lax.axis_size(axis))])  6.18 us
    ppermute x6, waiting for transfers between devices, swapped(): return lax.ppermute(values, ('sy', 'sx'), pairs)  1.96 us
  transfers between devices with their start and end apart: 33, of which 16 were waited for; matrix products, arithmetic and copies ran while one was open for 1% of the time, Pallas kernels for 7%

profile of v7, /device:TPU:0, one launch (start us, length us, event | category | flops | bytes accessed | tf_op | source)
XLA Modules:
  0.0 75.9 jit_solution(18040880667365149489)
XLA Ops:
  2.3 3.1 %collective-permute-start.1 = (f32[136,128]{1,0:T(8,128)S(1)}, f32[136,128]{1,0:T(8,128)S(1)}, u32[]{:S(2)}, u32[]{:S(2)}) collective-permute-start(f32[136,128]{1,0:T(8,128)S(1)} %get-tuple-element.82), channel_id=1, source_target_pairs={{0,1},{1,0},{2,3},{3,2},{4,8},{5,9},{6,10},{7,11},{8,4},{9,5},{10,... | collective-permute-start | bytes 208904 | tf_op jit(solution)/shard_map/ppermute | solution.py:55
  5.7 1.9 %collective-permute-done.1 = f32[136,128]{1,0:T(8,128)S(1)} collective-permute-done((f32[136,128]{1,0:T(8,128)S(1)}, f32[136,128]{1,0:T(8,128)S(1)}, u32[]{:S(2)}, u32[]{:S(2)}) %collective-permute-start.1) | collective-permute-done | bytes 69664 | tf_op jit(solution)/shard_map/ppermute | solution.py:55
  8.3 3.6 %collective-permute-start.2 = (f32[264,128]{1,0:T(8,128)S(1)}, f32[264,128]{1,0:T(8,128)S(1)}, u32[]{:S(2)}, u32[]{:S(2)}) collective-permute-start(f32[264,128]{1,0:T(8,128)S(1)} %concatenate.45), channel_id=1, source_target_pairs={{0,1},{1,0},{2,3},{3,2},{4,5},{5,4},{6,7},{7,6},{8,9},{9,8},{10,11... | collective-permute-start | bytes 405512 | tf_op jit(solution)/shard_map/ppermute | solution.py:39
  12.0 3.0 %collective-permute-done.2.cols_near = f32[264,128]{1,0:T(8,128)S(1)} collective-permute-done((f32[264,128]{1,0:T(8,128)S(1)}, f32[264,128]{1,0:T(8,128)S(1)}, u32[]{:S(2)}, u32[]{:S(2)}) %collective-permute-start.2) | collective-permute-done | bytes 135200 | tf_op jit(solution)/shard_map/ppermute | solution.py:39
  15.0 3.9 %shard_map.68 = (f32[24,128]{1,0:T(8,128)S(1)}, f32[2,2,128,128]{3,2,1,0:T(8,128)S(1)}, f32[2,2,128,128]{3,2,1,0:T(8,128)S(1)}, f32[4,5,16,128]{3,2,1,0:T(8,128)...) custom-call(s32[7]{0:T(128)S(1)} %stack.75.scal, s32[2,4]{1,0:T(2,128)S(1)} %bitcast.86, ...), custom_call_target="tpu_custom_call" | custom-call | flops 1610612736 | bytes 1048576 | tf_op jit(solution)/shard_map/pallas_call | solution.py:347
  19.1 2.0 %collective-permute-start.5 = (f32[2,2,128,128]{3,2,1,0:T(8,128)S(1)}, f32[2,2,128,128]{3,2,1,0:T(8,128)S(1)}, u32[]{:S(2)}, u32[]{:S(2)}) collective-permute-start(f32[2,2,128,128]{3,2,1,0:T(8,128)S(1)} %get-tuple-element.35), channel_id=1, source_target_pairs={{0,1},{1,0},{2,3},{3,2},{4,5},{5,4},{6,7},{7,6},{8,9},{9,8},{10,11... | collective-permute-start | bytes 786440 | tf_op jit(solution)/shard_map/ppermute | solution.py:39
  21.5 2.6 %collective-permute-start.11 = (f32[5,16,128]{2,1,0:T(8,128)S(1)}, f32[5,16,128]{2,1,0:T(8,128)S(1)}, u32[]{:S(2)}, u32[]{:S(2)}) collective-permute-start(f32[5,16,128]{2,1,0:T(8,128)S(1)} %get-tuple-element.63), channel_id=1, source_target_pairs={{0,24},{4,28},{8,16},{12,20},{16,8},{20,12},{24,0},{28,4},{1,25},{... | collective-permute-start | bytes 122888 | tf_op jit(solution)/shard_map/ppermute | solution.py:64
  25.3 1.5 %shard_map.69.scale_ref = f32[2,256,128]{2,1,0:T(8,128)S(1)} custom-call(s32[7]{0:T(128)S(1)} %stack.75.scal, s32[9,2,4]{2,1,0:T(2,128)S(1)} %compare_select_fusion.corners, f32[2,2,128,128]{3,2,1,0:T(8,128)S(1)} %copy-done.1), custom_call_target="tpu_custom_call" | custom-call | flops 805306368 | bytes 1048576 | tf_op jit(solution)/shard_map/pallas_call | solution.py:347
  28.3 2.3 %collective-permute-start.8 = (f32[2,2,128,128]{3,2,1,0:T(8,128)S(1)}, f32[2,2,128,128]{3,2,1,0:T(8,128)S(1)}, u32[]{:S(2)}, u32[]{:S(2)}) collective-permute-start(f32[2,2,128,128]{3,2,1,0:T(8,128)S(1)} %pad_maximum_fusion.1), channel_id=1, source_target_pairs={{0,1},{1,0},{2,3},{3,2},{4,8},{5,9},{6,10},{7,11},{8,4},{9,5},{10,... | collective-permute-start | bytes 786440 | tf_op jit(solution)/shard_map/ppermute | solution.py:55
  30.7 2.7 %collective-permute-start.14 = (f32[5,16,128]{2,1,0:T(8,128)S(1)}, f32[5,16,128]{2,1,0:T(8,128)S(1)}, u32[]{:S(2)}, u32[]{:S(2)}) collective-permute-start(f32[5,16,128]{2,1,0:T(8,128)S(1)} %fusion.3), channel_id=1, source_target_pairs={{0,3},{1,2},{2,1},{3,0},{4,7},{5,6},{6,5},{7,4},{8,11},{9,10},{10,... | collective-permute-start | bytes 122888 | tf_op jit(solution)/shard_map/ppermute | solution.py:64
  33.6 1.5 %collective-permute-start.12 = (f32[5,16,128]{2,1,0:T(8,128)S(1)}, f32[5,16,128]{2,1,0:T(8,128)S(1)}, u32[]{:S(2)}, u32[]{:S(2)}) collective-permute-start(f32[5,16,128]{2,1,0:T(8,128)S(1)} %fusion.3), channel_id=1, source_target_pairs={{0,1},{1,0},{2,3},{3,2},{4,5},{5,4},{6,7},{7,6},{8,9},{9,8},{10,11... | collective-permute-start | bytes 122888 | tf_op jit(solution)/shard_map/ppermute | solution.py:64
  35.2 4.2 %collective-permute-done.14 = f32[5,16,128]{2,1,0:T(8,128)S(1)} collective-permute-done((f32[5,16,128]{2,1,0:T(8,128)S(1)}, f32[5,16,128]{2,1,0:T(8,128)S(1)}, u32[]{:S(2)}, u32[]{:S(2)}) %collective-permute-start.14) | collective-permute-done | bytes 40992 | tf_op jit(solution)/shard_map/ppermute | solution.py:64
  39.4 2.6 %collective-permute-start.17 = (f32[4,16,128]{2,1,0:T(8,128)S(1)}, f32[4,16,128]{2,1,0:T(8,128)S(1)}, u32[]{:S(2)}, u32[]{:S(2)}) collective-permute-start(f32[4,16,128]{2,1,0:T(8,128)S(1)} %fusion.7), channel_id=1, source_target_pairs={{0,24},{4,28},{8,16},{12,20},{16,8},{20,12},{24,0},{28,4},{1,25},{... | collective-permute-start | bytes 98312 | tf_op jit(solution)/shard_map/ppermute | solution.py:64
  42.9 1.4 %collective-permute-done.17 = f32[4,16,128]{2,1,0:T(8,128)S(1)} collective-permute-done((f32[4,16,128]{2,1,0:T(8,128)S(1)}, f32[4,16,128]{2,1,0:T(8,128)S(1)}, u32[]{:S(2)}, u32[]{:S(2)}) %collective-permute-start.17) | collective-permute-done | bytes 32800 | tf_op jit(solution)/shard_map/ppermute | solution.py:64
  44.3 1.6 %collective-permute-done.16 = f32[4,16,128]{2,1,0:T(8,128)S(1)} collective-permute-done((f32[4,16,128]{2,1,0:T(8,128)S(1)}, f32[4,16,128]{2,1,0:T(8,128)S(1)}, u32[]{:S(2)}, u32[]{:S(2)}) %collective-permute-start.16) | collective-permute-done | bytes 32800 | tf_op jit(solution)/shard_map/ppermute | solution.py:64
  47.3 3.7 %shard_map.70 = (f32[2,2,128,128]{3,2,1,0:T(8,128)S(1)}, f32[256,128]{1,0:T(8,128)S(1)}, f32[4,5,16,128]{3,2,1,0:T(8,128)S(1)}, f32[576,128]{1,0:T(8,128)S(1)}, ...) custom-call(s32[7]{0:T(128)S(1)} %stack.75.scal, s32[2,4]{1,0:T(2,128)S(1)} %bitcast.87, ...), custom_call_target="tpu_custom_call" | custom-call | flops 1610612736 | bytes 1048576 | tf_op jit(solution)/shard_map/pallas_call | solution.py:347
  52.7 2.1 %collective-permute-start.23 = (f32[5,16,128]{2,1,0:T(8,128)S(1)}, f32[5,16,128]{2,1,0:T(8,128)S(1)}, u32[]{:S(2)}, u32[]{:S(2)}) collective-permute-start(f32[5,16,128]{2,1,0:T(8,128)S(1)} %get-tuple-element.60), channel_id=1, source_target_pairs={{0,24},{4,28},{8,16},{12,20},{16,8},{20,12},{24,0},{28,4},{1,25},{... | collective-permute-start | bytes 122888 | tf_op jit(solution)/shard_map/ppermute | solution.py:64
  56.3 1.5 %shard_map.71.scale_ref = f32[2,256,128]{2,1,0:T(8,128)S(1)} custom-call(s32[7]{0:T(128)S(1)} %stack.75.scal, s32[9,2,4]{2,1,0:T(2,128)S(1)} %compare_select_fusion.corners, f32[2,2,128,128]{3,2,1,0:T(8,128)S(1)} %get-tuple-element.43.probe_ref), custom_call_target="tpu_custom_call" | custom-call | flops 805306368 | bytes 1048576 | tf_op jit(solution)/shard_map/pallas_call | solution.py:347
  59.4 2.2 %collective-permute-start.28 = (f32[5,16,128]{2,1,0:T(8,128)S(1)}, f32[5,16,128]{2,1,0:T(8,128)S(1)}, u32[]{:S(2)}, u32[]{:S(2)}) collective-permute-start(f32[5,16,128]{2,1,0:T(8,128)S(1)} %fusion.1), channel_id=1, source_target_pairs={{0,3},{1,2},{2,1},{3,0},{4,7},{5,6},{6,5},{7,4},{8,11},{9,10},{10,... | collective-permute-start | bytes 122888 | tf_op jit(solution)/shard_map/ppermute | solution.py:64
  61.8 2.1 %collective-permute-start.26 = (f32[5,16,128]{2,1,0:T(8,128)S(1)}, f32[5,16,128]{2,1,0:T(8,128)S(1)}, u32[]{:S(2)}, u32[]{:S(2)}) collective-permute-start(f32[5,16,128]{2,1,0:T(8,128)S(1)} %fusion.1), channel_id=1, source_target_pairs={{0,1},{1,0},{2,3},{3,2},{4,5},{5,4},{6,7},{7,6},{8,9},{9,8},{10,11... | collective-permute-start | bytes 122888 | tf_op jit(solution)/shard_map/ppermute | solution.py:64
  65.2 1.4 %collective-permute-done.27 = f32[5,16,128]{2,1,0:T(8,128)S(1)} collective-permute-done((f32[5,16,128]{2,1,0:T(8,128)S(1)}, f32[5,16,128]{2,1,0:T(8,128)S(1)}, u32[]{:S(2)}, u32[]{:S(2)}) %collective-permute-start.27) | collective-permute-done | bytes 40992 | tf_op jit(solution)/shard_map/ppermute | solution.py:64
  66.6 2.6 %collective-permute-start.31 = (f32[4,16,128]{2,1,0:T(8,128)S(1)}, f32[4,16,128]{2,1,0:T(8,128)S(1)}, u32[]{:S(2)}, u32[]{:S(2)}) collective-permute-start(f32[4,16,128]{2,1,0:T(8,128)S(1)} %fusion.5), channel_id=1, source_target_pairs={{0,24},{4,28},{8,16},{12,20},{16,8},{20,12},{24,0},{28,4},{1,25},{... | collective-permute-start | bytes 98312 | tf_op jit(solution)/shard_map/ppermute | solution.py:64
  70.2 1.4 %shard_map.73 = f32[2,128,128]{2,1,0:T(8,128)} custom-call(s32[7]{0:T(128)S(1)} %stack.75.scal, f32[2,2,256,128]{3,2,1,0:T(8,128)S(1)} %get-tuple-element.39.old_ref, f32[2,256,128]{2,1,0:T(8,128)S(1)} %shard_map.71.scale_ref, f32[2,128,128]{2,1,0:T(8,128)S(1)} %get-tuple-element.48.middle_ref, f32[128,128]{1,0:T(8,128)S(1)} %collective-permute-done.24.near_ref, ...), custom_call_target="tpu_custom_call" | custom-call | bytes 1048576 | tf_op jit(solution)/shard_map/pallas_call | solution.py:347
  71.8 1.4 %collective-permute-done.30 = f32[4,16,128]{2,1,0:T(8,128)S(1)} collective-permute-done((f32[4,16,128]{2,1,0:T(8,128)S(1)}, f32[4,16,128]{2,1,0:T(8,128)S(1)}, u32[]{:S(2)}, u32[]{:S(2)}) %collective-permute-start.30) | collective-permute-done | bytes 32800 | tf_op jit(solution)/shard_map/ppermute | solution.py:64
  (119 shorter events, 18.7 us)
Async XLA Ops:
  2.3 5.4 %collective-permute-start.1 = (f32[136,128]{1,0:T(8,128)S(1)}, f32[136,128]{1,0:T(8,128)S(1)}, u32[]{:S(2)}, u32[]{:S(2)}) collective-permute-start(f32[136,128]{1,0:T(8,128)S(1)} %get-tuple-element.82), channel_id=1, source_target_pairs={{0,1},{1,0},{2,3},{3,2},{4,8},{5,9},{6,10},{7,11},{8,4},{9,5},{10,... | collective-permute-start | bytes 208904 | tf_op jit(solution)/shard_map/ppermute | solution.py:55
  8.0 3.9 %collective-permute-start.3 = (f32[264,128]{1,0:T(8,128)S(1)}, f32[264,128]{1,0:T(8,128)S(1)}, u32[]{:S(2)}, u32[]{:S(2)}) collective-permute-start(f32[264,128]{1,0:T(8,128)S(1)} %concatenate.48), channel_id=1, source_target_pairs={{0,4},{1,2},{2,1},{3,7},{4,0},{5,6},{6,5},{7,3},{8,12},{9,10},{10,... | collective-permute-start | bytes 405512 | tf_op jit(solution)/shard_map/ppermute | solution.py:55
  8.3 6.7 %collective-permute-start.2 = (f32[264,128]{1,0:T(8,128)S(1)}, f32[264,128]{1,0:T(8,128)S(1)}, u32[]{:S(2)}, u32[]{:S(2)}) collective-permute-start(f32[264,128]{1,0:T(8,128)S(1)} %concatenate.45), channel_id=1, source_target_pairs={{0,1},{1,0},{2,3},{3,2},{4,5},{5,4},{6,7},{7,6},{8,9},{9,8},{10,11... | collective-permute-start | bytes 405512 | tf_op jit(solution)/shard_map/ppermute | solution.py:39
  19.1 8.9 %collective-permute-start.5 = (f32[2,2,128,128]{3,2,1,0:T(8,128)S(1)}, f32[2,2,128,128]{3,2,1,0:T(8,128)S(1)}, u32[]{:S(2)}, u32[]{:S(2)}) collective-permute-start(f32[2,2,128,128]{3,2,1,0:T(8,128)S(1)} %get-tuple-element.35), channel_id=1, source_target_pairs={{0,1},{1,0},{2,3},{3,2},{4,5},{5,4},{6,7},{7,6},{8,9},{9,8},{10,11... | collective-permute-start | bytes 786440 | tf_op jit(solution)/shard_map/ppermute | solution.py:39
  21.1 7.0 %collective-permute-start.6 = (f32[2,2,128,128]{3,2,1,0:T(8,128)S(1)}, f32[2,2,128,128]{3,2,1,0:T(8,128)S(1)}, u32[]{:S(2)}, u32[]{:S(2)}) collective-permute-start(f32[2,2,128,128]{3,2,1,0:T(8,128)S(1)} %get-tuple-element.36), channel_id=1, source_target_pairs={{0,4},{1,2},{2,1},{3,7},{4,0},{5,6},{6,5},{7,3},{8,12},{9,10},{10,... | collective-permute-start | bytes 786440 | tf_op jit(solution)/shard_map/ppermute | solution.py:55
  21.5 9.1 %collective-permute-start.11 = (f32[5,16,128]{2,1,0:T(8,128)S(1)}, f32[5,16,128]{2,1,0:T(8,128)S(1)}, u32[]{:S(2)}, u32[]{:S(2)}) collective-permute-start(f32[5,16,128]{2,1,0:T(8,128)S(1)} %get-tuple-element.63), channel_id=1, source_target_pairs={{0,24},{4,28},{8,16},{12,20},{16,8},{20,12},{24,0},{28,4},{1,25},{... | collective-permute-start | bytes 122888 | tf_op jit(solution)/shard_map/ppermute | solution.py:64
  24.2 6.4 %collective-permute-start.10 = (f32[5,16,128]{2,1,0:T(8,128)S(1)}, f32[5,16,128]{2,1,0:T(8,128)S(1)}, u32[]{:S(2)}, u32[]{:S(2)}) collective-permute-start(f32[5,16,128]{2,1,0:T(8,128)S(1)} %get-tuple-element.64), channel_id=1, source_target_pairs={{0,16},{4,20},{8,24},{12,28},{16,0},{20,4},{24,8},{28,12},{1,17},{... | collective-permute-start | bytes 122888 | tf_op jit(solution)/shard_map/ppermute | solution.py:64
  25.2 5.4 %collective-permute-start.9 = (f32[5,16,128]{2,1,0:T(8,128)S(1)}, f32[5,16,128]{2,1,0:T(8,128)S(1)}, u32[]{:S(2)}, u32[]{:S(2)}) collective-permute-start(f32[5,16,128]{2,1,0:T(8,128)S(1)} %get-tuple-element.65), channel_id=1, source_target_pairs={{0,8},{4,12},{8,0},{12,4},{16,24},{20,28},{24,16},{28,20},{1,9},{5... | collective-permute-start | bytes 122888 | tf_op jit(solution)/shard_map/ppermute | solution.py:64
  28.3 6.8 %collective-permute-start.8 = (f32[2,2,128,128]{3,2,1,0:T(8,128)S(1)}, f32[2,2,128,128]{3,2,1,0:T(8,128)S(1)}, u32[]{:S(2)}, u32[]{:S(2)}) collective-permute-start(f32[2,2,128,128]{3,2,1,0:T(8,128)S(1)} %pad_maximum_fusion.1), channel_id=1, source_target_pairs={{0,1},{1,0},{2,3},{3,2},{4,8},{5,9},{6,10},{7,11},{8,4},{9,5},{10,... | collective-permute-start | bytes 786440 | tf_op jit(solution)/shard_map/ppermute | solution.py:55
  30.7 8.7 %collective-permute-start.14 = (f32[5,16,128]{2,1,0:T(8,128)S(1)}, f32[5,16,128]{2,1,0:T(8,128)S(1)}, u32[]{:S(2)}, u32[]{:S(2)}) collective-permute-start(f32[5,16,128]{2,1,0:T(8,128)S(1)} %fusion.3), channel_id=1, source_target_pairs={{0,3},{1,2},{2,1},{3,0},{4,7},{5,6},{6,5},{7,4},{8,11},{9,10},{10,... | collective-permute-start | bytes 122888 | tf_op jit(solution)/shard_map/ppermute | solution.py:64
  33.4 6.0 %collective-permute-start.13 = (f32[5,16,128]{2,1,0:T(8,128)S(1)}, f32[5,16,128]{2,1,0:T(8,128)S(1)}, u32[]{:S(2)}, u32[]{:S(2)}) collective-permute-start(f32[5,16,128]{2,1,0:T(8,128)S(1)} %fusion.3), channel_id=1, source_target_pairs={{0,2},{1,3},{2,0},{3,1},{4,6},{5,7},{6,4},{7,5},{8,10},{9,11},{10,... | collective-permute-start | bytes 122888 | tf_op jit(solution)/shard_map/ppermute | solution.py:64
  33.6 5.7 %collective-permute-start.12 = (f32[5,16,128]{2,1,0:T(8,128)S(1)}, f32[5,16,128]{2,1,0:T(8,128)S(1)}, u32[]{:S(2)}, u32[]{:S(2)}) collective-permute-start(f32[5,16,128]{2,1,0:T(8,128)S(1)} %fusion.3), channel_id=1, source_target_pairs={{0,1},{1,0},{2,3},{3,2},{4,5},{5,4},{6,7},{7,6},{8,9},{9,8},{10,11... | collective-permute-start | bytes 122888 | tf_op jit(solution)/shard_map/ppermute | solution.py:64
  39.4 5.0 %collective-permute-start.17 = (f32[4,16,128]{2,1,0:T(8,128)S(1)}, f32[4,16,128]{2,1,0:T(8,128)S(1)}, u32[]{:S(2)}, u32[]{:S(2)}) collective-permute-start(f32[4,16,128]{2,1,0:T(8,128)S(1)} %fusion.7), channel_id=1, source_target_pairs={{0,24},{4,28},{8,16},{12,20},{16,8},{20,12},{24,0},{28,4},{1,25},{... | collective-permute-start | bytes 98312 | tf_op jit(solution)/shard_map/ppermute | solution.py:64
  42.0 3.9 %collective-permute-start.16 = (f32[4,16,128]{2,1,0:T(8,128)S(1)}, f32[4,16,128]{2,1,0:T(8,128)S(1)}, u32[]{:S(2)}, u32[]{:S(2)}) collective-permute-start(f32[4,16,128]{2,1,0:T(8,128)S(1)} %fusion.7), channel_id=1, source_target_pairs={{0,16},{4,20},{8,24},{12,28},{16,0},{20,4},{24,8},{28,12},{1,17},{... | collective-permute-start | bytes 98312 | tf_op jit(solution)/shard_map/ppermute | solution.py:64
  51.2 8.1 %collective-permute-start.20 = (f32[256,128]{1,0:T(8,128)S(1)}, f32[256,128]{1,0:T(8,128)S(1)}, u32[]{:S(2)}, u32[]{:S(2)}) collective-permute-start(f32[256,128]{1,0:T(8,128)S(1)} %get-tuple-element.45), channel_id=1, source_target_pairs={{0,1},{1,0},{2,3},{3,2},{4,8},{5,9},{6,10},{7,11},{8,4},{9,5},{10,... | collective-permute-start | bytes 393224 | tf_op jit(solution)/shard_map/ppermute | solution.py:55
  52.7 6.0 %collective-permute-start.23 = (f32[5,16,128]{2,1,0:T(8,128)S(1)}, f32[5,16,128]{2,1,0:T(8,128)S(1)}, u32[]{:S(2)}, u32[]{:S(2)}) collective-permute-start(f32[5,16,128]{2,1,0:T(8,128)S(1)} %get-tuple-element.60), channel_id=1, source_target_pairs={{0,24},{4,28},{8,16},{12,20},{16,8},{20,12},{24,0},{28,4},{1,25},{... | collective-permute-start | bytes 122888 | tf_op jit(solution)/shard_map/ppermute | solution.py:64
  54.8 4.2 %collective-permute-start.22 = (f32[5,16,128]{2,1,0:T(8,128)S(1)}, f32[5,16,128]{2,1,0:T(8,128)S(1)}, u32[]{:S(2)}, u32[]{:S(2)}) collective-permute-start(f32[5,16,128]{2,1,0:T(8,128)S(1)} %get-tuple-element.61), channel_id=1, source_target_pairs={{0,16},{4,20},{8,24},{12,28},{16,0},{20,4},{24,8},{28,12},{1,17},{... | collective-permute-start | bytes 122888 | tf_op jit(solution)/shard_map/ppermute | solution.py:64
  55.2 4.1 %collective-permute-start.21 = (f32[5,16,128]{2,1,0:T(8,128)S(1)}, f32[5,16,128]{2,1,0:T(8,128)S(1)}, u32[]{:S(2)}, u32[]{:S(2)}) collective-permute-start(f32[5,16,128]{2,1,0:T(8,128)S(1)} %get-tuple-element.62), channel_id=1, source_target_pairs={{0,8},{4,12},{8,0},{12,4},{16,24},{20,28},{24,16},{28,20},{1,9},{5... | collective-permute-start | bytes 122888 | tf_op jit(solution)/shard_map/ppermute | solution.py:64
  59.4 5.9 %collective-permute-start.28 = (f32[5,16,128]{2,1,0:T(8,128)S(1)}, f32[5,16,128]{2,1,0:T(8,128)S(1)}, u32[]{:S(2)}, u32[]{:S(2)}) collective-permute-start(f32[5,16,128]{2,1,0:T(8,128)S(1)} %fusion.1), channel_id=1, source_target_pairs={{0,3},{1,2},{2,1},{3,0},{4,7},{5,6},{6,5},{7,4},{8,11},{9,10},{10,... | collective-permute-start | bytes 122888 | tf_op jit(solution)/shard_map/ppermute | solution.py:64
  61.5 5.1 %collective-permute-start.27 = (f32[5,16,128]{2,1,0:T(8,128)S(1)}, f32[5,16,128]{2,1,0:T(8,128)S(1)}, u32[]{:S(2)}, u32[]{:S(2)}) collective-permute-start(f32[5,16,128]{2,1,0:T(8,128)S(1)} %fusion.1), channel_id=1, source_target_pairs={{0,2},{1,3},{2,0},{3,1},{4,6},{5,7},{6,4},{7,5},{8,10},{9,11},{10,... | collective-permute-start | bytes 122888 | tf_op jit(solution)/shard_map/ppermute | solution.py:64
  61.8 4.8 %collective-permute-start.26 = (f32[5,16,128]{2,1,0:T(8,128)S(1)}, f32[5,16,128]{2,1,0:T(8,128)S(1)}, u32[]{:S(2)}, u32[]{:S(2)}) collective-permute-start(f32[5,16,128]{2,1,0:T(8,128)S(1)} %fusion.1), channel_id=1, source_target_pairs={{0,1},{1,0},{2,3},{3,2},{4,5},{5,4},{6,7},{7,6},{8,9},{9,8},{10,11... | collective-permute-start | bytes 122888 | tf_op jit(solution)/shard_map/ppermute | solution.py:64
  64.5 5.7 %collective-permute-start.24 = (f32[128,128]{1,0:T(8,128)S(1)}, f32[128,128]{1,0:T(8,128)S(1)}, u32[]{:S(2)}, u32[]{:S(2)}) collective-permute-start(f32[128,128]{1,0:T(8,128)S(1)} %get-tuple-element.49), channel_id=1, source_target_pairs={{0,1},{1,0},{2,3},{3,2},{4,5},{5,4},{6,7},{7,6},{8,9},{9,8},{10,11... | collective-permute-start | bytes 196616 | tf_op jit(solution)/shard_map/ppermute | solution.py:39
  64.6 5.6 %collective-permute-start.25 = (f32[128,128]{1,0:T(8,128)S(1)}, f32[128,128]{1,0:T(8,128)S(1)}, u32[]{:S(2)}, u32[]{:S(2)}) collective-permute-start(f32[128,128]{1,0:T(8,128)S(1)} %get-tuple-element.50), channel_id=1, source_target_pairs={{0,4},{1,2},{2,1},{3,7},{4,0},{5,6},{6,5},{7,3},{8,12},{9,10},{10,... | collective-permute-start | bytes 196616 | tf_op jit(solution)/shard_map/ppermute | solution.py:55
  66.6 5.2 %collective-permute-start.31 = (f32[4,16,128]{2,1,0:T(8,128)S(1)}, f32[4,16,128]{2,1,0:T(8,128)S(1)}, u32[]{:S(2)}, u32[]{:S(2)}) collective-permute-start(f32[4,16,128]{2,1,0:T(8,128)S(1)} %fusion.5), channel_id=1, source_target_pairs={{0,24},{4,28},{8,16},{12,20},{16,8},{20,12},{24,0},{28,4},{1,25},{... | collective-permute-start | bytes 98312 | tf_op jit(solution)/shard_map/ppermute | solution.py:64
  (14 other events, 47.7 us)
